TPU v7x, 256 devices: a whole 4x4x8 slice. The times are simulated.
256 devices in a mesh: rep: 8 (over x, y_hi), fsdp: 32 (over y_lo, z, core).
Axes of the slice: x: 4, y: 4 (y_hi: 2, y_lo: 2; y = y_hi * 2 + y_lo), z: 8, core: 2. Of those that a mesh axis runs over, the one named last changes fastest.
Arguments:
- global_w: float32 [10240, 768], P('fsdp'), may hold values from -6 to 6
- momentum: float32 [10240, 768], P('fsdp'), may hold values from -3 to 3
- local_w: bfloat16 [8, 10240, 768], P('rep', 'fsdp'), may hold values from -6 to 6
- tokens: bfloat16 [8, 8192, 10240], P('rep', 'fsdp'), may hold values from -6 to 6
Outputs:
- new_global: float32 [10240, 768], P('fsdp')
- new_moment: float32 [10240, 768], P('fsdp')
- new_local: bfloat16 [8, 10240, 768], P('rep', 'fsdp')
- projected: bfloat16 [8, 8192, 768], P('rep', 'fsdp')
All inputs are finite; a program needn't handle non-finite values.
Results may differ from a plain program's by a relative error of at most 0.0049.
Values may be sent and summed in bfloat16 or wider, within the bound.
No kernel may reach another device: no remote copies, remote signals or barrier semaphores. Data moves between devices by JAX's collectives and lax.ppermute only.
A program may use at most 128 MiB of HBM per device.

v0:
```python
import math

import jax
import jax.numpy as jnp
from jax import lax
from jax.sharding import PartitionSpec as P

D = 10240


OUTER_RATE = 0.7
MOMENT_DECAY = 0.9
KEEP_LOCAL = 0.5


def outer_update(global_part, moment_part, local_part, summed, replicas):
    gradient = summed / replicas
    new_moment = MOMENT_DECAY * moment_part + gradient
    new_global = global_part - OUTER_RATE * (gradient + MOMENT_DECAY * new_moment)
    blended = (
        KEEP_LOCAL * local_part.astype(jnp.float32) + (1.0 - KEEP_LOCAL) * new_global
    ).astype(jnp.bfloat16)
    return (new_global, new_moment, blended)


def pseudo_terms(global_part, local_part):
    return global_part - local_part.astype(jnp.float32)


def on_device(global_w, momentum, local_w, tokens):
    replicas = lax.axis_size("rep")
    rows_in = tokens[0]
    local_rows = local_w[0]
    scaling = 1.0 / math.sqrt(D)
    summed = lax.psum(pseudo_terms(global_w, local_rows), "rep")
    new_global, new_moment, blended = outer_update(global_w, momentum, local_rows, summed, replicas)
    running = jnp.dot(
        rows_in,
        lax.all_gather(blended, "fsdp", axis=0, tiled=True),
        preferred_element_type=jnp.float32,
    )
    projected = (running * scaling).astype(jnp.bfloat16)
    return (new_global, new_moment, blended[None], projected[None])


def solution(mesh):
    return jax.shard_map(
        on_device,
        mesh=mesh,
        in_specs=(P("fsdp", None), P("fsdp", None), P("rep", "fsdp", None), P("rep", "fsdp", None)),
        out_specs=(
            P("fsdp", None),
            P("fsdp", None),
            P("rep", "fsdp", None),
            P("rep", "fsdp", None),
        ),
        check_vma=False,
    )
```

profile of v0, /device:TPU:1, one launch (start us, length us, event | category | flops | bytes accessed | tf_op | source)
XLA Modules:
  0.0 224.0 jit_solution(12787539859876234751)
XLA Ops:
  7.2 0.0 all-reduce.2.cloned.1.call-start
  7.2 2.4 %convert_subtract_fusion = f32[320,768]{1,0:T(8,128)} fusion(f32[320,768]{1,0:T(8,128)} %param.4, bf16[1,320,768]{2,1,0:T(8,128)(2,1)} %param.6), kind=kLoop, calls=%fused_computation.5 | loop fusion | flops 491520 | bytes 2457600 | tf_op jit(solution)/shard_map/sub | solution.py:27
  9.6 0.0 all-reduce.2.cloned.1.call-update
  9.6 0.0 all-gather.2.cloned.1.call-start
  9.6 94.0 %all-reduce.2.cloned.1.call-done = f32[320,768]{1,0:T(8,128)} async-done(((f32[320,768]{1,0:T(8,128)}), f32[320,768]{1,0:T(8,128)}) %all-reduce.2.cloned.1.call-update) | async-done | bytes 983056 | tf_op jit(solution)/shard_map/psum | solution.py:35
  103.6 3.6 %fusion.12 = (bf16[320,768]{1,0:T(8,128)(2,1)}, f32[320,768]{1,0:T(8,128)}, f32[320,768]{1,0:T(8,128)}) fusion(bf16[1,320,768]{2,1,0:T(8,128)(2,1)} %param.6, f32[320,768]{1,0:T(8,128)} %param.4, f32[320,768]{1,0:T(8,128)} %all-reduce.2.cloned.1.call-done, f32[320,768]{1,0:T(8,128)} %param.5), kind=kLoop, calls=%fused_computation.8 | loop fusion | flops 2703360 | bytes 5898240 | tf_op jit(solution)/shard_map/convert_element_type | solution.py:22
  107.3 0.0 all-gather.2.cloned.1.call-update
  107.3 97.8 %all-gather.2.cloned.1.call-done = bf16[10240,768]{1,0:T(8,128)(2,1)} async-done(((bf16[320,768]{1,0:T(8,128)(2,1)}), bf16[10240,768]{1,0:T(8,128)(2,1)}) %all-gather.2.cloned.1.call-update) | async-done | bytes 15728656 | tf_op jit(solution)/shard_map/all_gather | solution.py:39
  205.0 11.2 %fusion.8 = bf16[1,256,768]{1,2,0:T(8,128)(2,1)S(1)} fusion(bf16[10240,768]{1,0:T(8,128)(2,1)} %all-gather.2.cloned.1.call-done, bf16[1,256,10240]{2,1,0:T(8,128)(2,1)} %param.7), kind=kOutput, calls=%fused_computation.6 | convolution fusion | flops 4026925056 | bytes 21364736 | tf_op jit(solution)/shard_map/dot_general | solution.py:37
  216.3 0.9 copy.8
Async XLA Ops:
  7.2 96.4 %all-reduce.2.cloned.1.call-start = ((), (), s32[]{:S(2)}) async-start(), calls=%async_computation | async-start | bytes 1966080 | tf_op jit(solution)/shard_map/psum | solution.py:35
  9.6 195.4 %all-gather.2.cloned.1.call-start = ((), (), s32[]{:S(2)}) async-start(), calls=%async_computation.1 | async-start | bytes 16220160 | tf_op jit(solution)/shard_map/all_gather | solution.py:39
Sparse Core Ops, SparseCore 0:
  11.2 92.3 all-reduce.1
  107.4 97.5 all-gather.1
where the time goes:
time: 224 us
  waiting for transfers between devices  192 us (86%)
  between operations  14 us (6%)
  matrix products  11.2 us (5%)
  other arithmetic  6 us (3%)
    all_gather x1, waiting for transfers between devices, on_device(): lax.all_gather(blended, 'fsdp', axis=0, tiled=True)  97.8 us
    psum x1, waiting for transfers between devices, on_device(): summed = lax.psum(pseudo_terms(global_w, local_rows), 'rep')  94 us
    dot_general x1, matrix products, on_device(): jnp.dot(rows_in, lax.all_gather(blended, 'fsdp', axis=0, tiled=True), pre...  11.2 us
  transfers between devices with their start and end apart: 2, of which 2 were waited for; matrix products, arithmetic and copies ran while one was open for 0% of the time, Pallas kernels for 0%

commit v1 on v0

v1 whole, which is shorter than its diff:
```python
import functools
import math

import jax
import jax.numpy as jnp
from jax import lax
from jax.experimental import pallas as pl
from jax.experimental.pallas import tpu as pltpu
from jax.sharding import PartitionSpec as P

D = 10240
COLS = 768
HALF = COLS // 2
REPS = 8
OUTER_RATE = 0.7
MOMENT_DECAY = 0.9
KEEP_LOCAL = 0.5

NX, NYH, NYL, NZ, NC = 4, 2, 2, 8, 2
ROWS = D // (NYL * NZ * NC)
CHIP = ROWS * NC
A = 384
B = CHIP - A
STEP = 4 * CHIP
SLICE = ROWS // NX


def rep_perm(dx, dy):
    return [
        (x * NYH + y, ((x + dx) % NX) * NYH + (y ^ dy)) for x in range(NX) for y in range(NYH)
    ]


def fsdp_perm(dy, dz, dc):
    return [
        ((y * NZ + z) * NC + c, ((y ^ dy) * NZ + (z + dz) % NZ) * NC + (c ^ dc))
        for y in range(NYL)
        for z in range(NZ)
        for c in range(NC)
    ]


def send_rep(v, dx, dy):
    return lax.ppermute(v, "rep", rep_perm(dx, dy))


def send(v, dy, dz, dc):
    return lax.ppermute(v, "fsdp", fsdp_perm(dy, dz, dc))


def pieces_of(d):
    return [(0, d), (1, d)]


ORDER = (
    pieces_of(0) + pieces_of(4)
    + pieces_of(-1) + pieces_of(1)
    + pieces_of(-2) + pieces_of(2)
    + pieces_of(-3) + pieces_of(3)
)


def reorder_kernel(tok_ref, out_ref, sems):
    me = lax.axis_index("fsdp")
    yl = me // (NZ * NC)
    z = (me // NC) % NZ
    copies = []
    for place, (flip, dz) in enumerate(ORDER):
        y = (1 - yl) if flip else yl
        shard = y * NZ + (z + dz + NZ) % NZ
        spans = ((0, 0, CHIP),) if not flip else ((A, 0, B), (0, B, A))
        for source, target, width in spans:
            copy = pltpu.make_async_copy(
                tok_ref.at[:, pl.ds(pl.multiple_of(shard * CHIP + source, 128), width)],
                out_ref.at[:, pl.ds(place * CHIP + target, width)],
                sems.at[len(copies)],
            )
            copy.start()
            copies.append(copy)
    for copy in copies:
        copy.wait()


def reorder(tokens):
    return pl.pallas_call(
        reorder_kernel,
        out_shape=jax.ShapeDtypeStruct(tokens.shape, tokens.dtype),
        in_specs=[pl.BlockSpec(memory_space=pl.ANY)],
        out_specs=pl.BlockSpec(memory_space=pl.ANY),
        scratch_shapes=[pltpu.SemaphoreType.DMA((len(ORDER) * 3 // 2,))],
        cost_estimate=pl.CostEstimate(
            flops=0, bytes_accessed=2 * tokens.size * 2, transcendentals=0
        ),
    )(tokens)


def step_kernel(spans, first, last, scale, *refs):
    arrays = len({array for array, _, _ in spans})
    toks, weights, refs = refs[:2], refs[2 : 2 + arrays], refs[2 + arrays :]
    before, outs = ((), refs) if first else (refs[:2], refs[2:])
    for which, (tok, out) in enumerate(zip(toks, outs)):
        total = None if first else before[which][...]
        at = 0
        for array, start, rows in spans:
            product = jnp.dot(
                tok[:, at : at + rows],
                weights[array][start : start + rows, :],
                preferred_element_type=jnp.float32,
            )
            total = product if total is None else total + product
            at += rows
        out[...] = (total * scale).astype(out.dtype) if last else total


def step(mine, other, weights, spans, totals, block, last):
    rows, width = mine.shape[0], sum(span[2] for span in spans)
    first = totals is None
    kind = jnp.bfloat16 if last else jnp.float32
    tok_spec = pl.BlockSpec((rows, width), lambda i: (0, block))
    whole = pl.BlockSpec(memory_space=pltpu.VMEM)
    operands = (mine, other) + tuple(weights) + (() if first else tuple(totals))
    return pl.pallas_call(
        functools.partial(step_kernel, spans, first, last, 1.0 / math.sqrt(D)),
        out_shape=[jax.ShapeDtypeStruct((rows, HALF), kind)] * 2,
        grid=(1,),
        in_specs=[tok_spec, tok_spec] + [whole] * (len(operands) - 2),
        out_specs=[whole, whole],
        compiler_params=pltpu.CompilerParams(vmem_limit_bytes=32 * 1024 * 1024),
        cost_estimate=pl.CostEstimate(
            flops=2 * 2 * rows * width * HALF,
            bytes_accessed=2 * (2 * rows * width + width * HALF) + 16 * rows * HALF,
            transcendentals=0,
        ),
    )(*operands)


def after(value, *earlier):
    return lax.optimization_barrier((value, earlier))[0]


def in_order(slices, x):
    rows = []
    for place in range(NX):
        value = slices[0]
        for k in range(1, NX):
            value = jnp.where((x - k) % NX == place, slices[k], value)
        rows.append(value)
    return jnp.concatenate(rows, axis=0)


def on_device(global_w, momentum, local_w, tokens):
    local = local_w[0]
    x = lax.axis_index("rep") // NYH
    core = lax.axis_index("fsdp") % NC

    def quarter(v, place):
        return lax.dynamic_slice(v, (place * SLICE, 0), (SLICE, COLS))

    raw = [quarter(local, x)] + [
        send_rep(quarter(local, (x + k) % NX), k, 0) for k in range(1, NX)
    ]
    global_part = quarter(global_w, x)
    four = sum(global_part - r.astype(jnp.float32) for r in raw)
    mine = reorder(after(tokens[0], four))
    other = send(mine, 0, 0, 1)
    gradient = (four + send_rep(four, 0, 1)) / REPS
    moment_part = MOMENT_DECAY * quarter(momentum, x) + gradient
    new_part = global_part - OUTER_RATE * (gradient + MOMENT_DECAY * moment_part)

    def blend(r):
        return (
            KEEP_LOCAL * r.astype(jnp.float32) + (1.0 - KEEP_LOCAL) * new_part
        ).astype(jnp.bfloat16)

    back = [blend(raw[0])] + [send_rep(blend(raw[k]), -k, 0) for k in range(1, NX)]
    back = [back[0], back[3], back[2], back[1]]
    new_local = in_order(back, x)

    left, right = new_local[:, :HALF], new_local[:, HALF:]
    keep = jnp.where(core == 0, left, right)
    got = send(jnp.where(core == 0, right, left), 0, 0, 1)
    shard = jnp.concatenate(
        [jnp.where(core == 0, keep, got), jnp.where(core == 0, got, keep)], axis=0
    )
    own_a, own_b = shard[:A], shard[A:]
    part_b = send(own_b, 1, 0, 0)
    part_a = send(after(own_a, part_b), 1, 0, 0)
    both = jnp.concatenate([own_b, part_b], axis=0)

    spans = ((0, 0, A), (1, 0, 2 * B), (2, 0, A), (3, 0, A), (4, 0, 2 * B), (2, A, A))
    totals = None
    up_a, down_a, up_b, down_b, side = own_a, own_a, both, both, part_a
    for d in range(1, 4):
        up_a, down_a = send(up_a, 0, 1, 0), send(down_a, 0, -1, 0)
        if d > 1:
            totals = step(mine, other, held, spans, totals, d - 1, False)
            up_b, down_b = after((up_b, down_b), *totals)
        up_b, down_b = send(up_b, 0, 1, 0), send(down_b, 0, -1, 0)
        side = send(after(jnp.concatenate([up_a, down_a], axis=0), side), 1, 0, 0)
        held = [up_a, up_b, side, down_a, down_b]
        if d == 2:
            gradient = after(gradient, *totals)
            sums = [gradient] + [send_rep(gradient, k, 0) for k in range(1, NX)]
    far_a = [send(up_a[: A // 2], 0, 1, 0), send(down_a[A // 2 :], 0, -1, 0)]
    far_b = [send(up_b[:B], 0, 1, 0), send(down_b[B:], 0, -1, 0)]
    far_a = jnp.concatenate(far_a, axis=0)
    far_side = send(after(far_a, side), 1, 0, 0)
    totals = step(mine, other, held, spans, totals, 3, False)

    full = in_order(sums, x)
    new_moment = MOMENT_DECAY * momentum + full
    new_global = global_w - OUTER_RATE * (full + MOMENT_DECAY * new_moment)

    weights = [own_a, both, part_a, far_a] + far_b + [far_side]
    spans = ((0, 0, A), (1, 0, 2 * B), (2, 0, A), (3, 0, A), (4, 0, B), (5, 0, B), (6, 0, A))
    own, theirs = step(mine, other, weights, spans, totals, 0, True)

    came = send(theirs, 0, 0, 1)
    projected = jnp.concatenate(
        [jnp.where(core == 0, own, came), jnp.where(core == 0, came, own)], axis=1
    )
    return (new_global, new_moment, new_local[None], projected[None])


def solution(mesh):
    return jax.shard_map(
        on_device,
        mesh=mesh,
        in_specs=(P("fsdp", None), P("fsdp", None), P("rep", "fsdp", None), P("rep", "fsdp", None)),
        out_specs=(
            P("fsdp", None),
            P("fsdp", None),
            P("rep", "fsdp", None),
            P("rep", "fsdp", None),
        ),
        check_vma=False,
    )
```

time: 224 us -> 289 us (1.29)
  Pallas kernels: 0 us -> 172 us
  waiting for transfers between devices: 192 us -> 57.8 us
  starting transfers between devices: 0.08 us -> 50 us
  between operations: 14 us -> 0.97 us
  matrix products: 11.2 us -> 0 us
    pallas_call x0 -> x5, Pallas kernels: none -> 172 us  [the longest x1 160 us: reorder(): pl.pallas_call(reorder_kernel, out_shape=jax.ShapeDtypeStruct(tokens.shap...]
    all_gather x1 -> x0, waiting for transfers between devices: 97.8 us -> none  [on_device(): lax.all_gather(blended, 'fsdp', axis=0, tiled=True)]
    psum x1 -> x0, waiting for transfers between devices: 94 us -> none  [on_device(): summed = lax.psum(pseudo_terms(global_w, local_rows), 'rep')]
    ppermute x0 -> x35, waiting for transfers between devices: none -> 57.8 us  [the longest x25 33.6 us: send(): return lax.ppermute(v, 'fsdp', fsdp_perm(dy, dz, dc))]
    ppermute x0 -> x35, starting transfers between devices: none -> 50 us  [the longest x25 37.1 us: send(): return lax.ppermute(v, 'fsdp', fsdp_perm(dy, dz, dc))]
    dot_general x1 -> x0, matrix products: 11.2 us -> none  [on_device(): jnp.dot(rows_in, lax.all_gather(blended, 'fsdp', axis=0, tiled=True), pre...]
    convert_element_type x1 -> x2, other arithmetic: 3.65 us -> 0.17 us  [blend(): return (KEEP_LOCAL * r.astype(jnp.float32) + (1.0 - KEEP_LOCAL) * new_par...]
  transfers between devices with their start and end apart: 2 -> 35, of which waited for: 2 -> 18; matrix products, arithmetic and copies ran while one was open for 0% -> 1% of each run, Pallas kernels for 0% -> 3%
where the time goes in v1:
time: 289 us; the launch traced here: 288 us
  Pallas kernels  172 us (60%)
  waiting for transfers between devices  57.8 us (20%)
  starting transfers between devices  50 us (17%)
  other arithmetic  5.96 us (2%)
    pallas_call x1, Pallas kernels, reorder(): pl.pallas_call(reorder_kernel, out_shape=jax.ShapeDtypeStruct(tokens.shap...  160 us
    ppermute x25, starting transfers between devices, send(): return lax.ppermute(v, 'fsdp', fsdp_perm(dy, dz, dc))  37.1 us
    ppermute x25, waiting for transfers between devices, send(): return lax.ppermute(v, 'fsdp', fsdp_perm(dy, dz, dc))  33.6 us
    ppermute x10, waiting for transfers between devices, send_rep(): return lax.ppermute(v, 'rep', rep_perm(dx, dy))  24.2 us
    ppermute x10, starting transfers between devices, send_rep(): return lax.ppermute(v, 'rep', rep_perm(dx, dy))  12.9 us
    pallas_call x4, Pallas kernels, step(): pl.pallas_call(functools.partial(step_kernel, spans, first, last, 1.0 / m...  12.2 us
  transfers between devices with their start and end apart: 35, of which 18 were waited for; matrix products, arithmetic and copies ran while one was open for 1% of the time, Pallas kernels for 3%

profile of v1, /device:TPU:1, one launch (start us, length us, event | category | flops | bytes accessed | tf_op | source)
XLA Modules:
  0.0 288.3 jit_solution(18119555676657215856)
XLA Ops:
  0.7 1.1 dynamic-slice_bitcast_fusion.1
  1.8 2.1 collective-permute-start
  3.9 2.5 collective-permute-start.1
  6.3 1.2 collective-permute-start.2
  7.5 4.2 %collective-permute-done.1 = bf16[80,768]{1,0:T(8,128)(2,1)S(1)} collective-permute-done((bf16[80,768]{1,0:T(8,128)(2,1)S(1)}, bf16[80,768]{1,0:T(8,128)(2,1)S(1)}, u32[]{:S(2)}, u32[]{:S(2)}) %collective-permute-start.1) | collective-permute-done | bytes 122912 | tf_op jit(solution)/shard_map/ppermute | solution.py:44
  11.7 1.1 fusion.2
  12.8 160.2 %shard_map.75.refs_0_ = bf16[256,10240]{1,0:T(8,128)(2,1)} custom-call(bf16[256,10240]{1,0:T(8,128)(2,1)} %bitcast.16), custom_call_target="tpu_custom_call" | custom-call | bytes 10485760 | tf_op jit(solution)/shard_map/pallas_call | solution.py:85
  173.0 2.0 collective-permute-start.4
  175.0 2.6 collective-permute-start.3
  177.6 6.5 %collective-permute-done.3 = f32[80,768]{1,0:T(8,128)S(1)} collective-permute-done((f32[80,768]{1,0:T(8,128)S(1)}, f32[80,768]{1,0:T(8,128)S(1)}, u32[]{:S(2)}, u32[]{:S(2)}) %collective-permute-start.3) | collective-permute-done | bytes 245792 | tf_op jit(solution)/shard_map/ppermute | solution.py:44
  184.2 2.2 collective-permute-start.5
  187.2 2.3 collective-permute-done.5
  189.5 2.3 collective-permute-done.6
  191.8 3.5 %collective-permute-done.7 = bf16[80,768]{1,0:T(8,128)(2,1)S(1)} collective-permute-done((bf16[80,768]{1,0:T(8,128)(2,1)S(1)}, bf16[80,768]{1,0:T(8,128)(2,1)S(1)}, u32[]{:S(2)}, u32[]{:S(2)}) %collective-permute-start.7) | collective-permute-done | bytes 122912 | tf_op jit(solution)/shard_map/ppermute | solution.py:44
  195.3 1.0 select_select_fusion.7
  196.4 0.8 fusion.11
  197.3 1.1 collective-permute-start.8
  198.4 1.1 collective-permute-done.8
  199.6 0.9 collective-permute-start.10
  200.6 1.7 collective-permute-start.9
  202.3 4.0 %collective-permute-start.12 = (bf16[384,384]{1,0:T(8,128)(2,1)S(1)}, bf16[384,384]{1,0:T(8,128)(2,1)S(1)}, u32[]{:S(2)}, u32[]{:S(2)}) collective-permute-start(bf16[384,384]{1,0:T(8,128)(2,1)S(1)} %pad_maximum_fusion.6.refs_2_), channel_id=1, source_target_pairs={{0,14},{1,15},{2,0},{3,1},{4,2},{5,3},{6,4},{7,5},{8,6},{9,7},{10,... | collective-permute-start | bytes 884744 | tf_op jit(solution)/shard_map/ppermute | solution.py:48
  206.6 6.3 %collective-permute-done.9.refs_2_ = bf16[384,384]{1,0:T(8,128)(2,1)S(1)} collective-permute-done((bf16[384,384]{1,0:T(8,128)(2,1)S(1)}, bf16[384,384]{1,0:T(8,128)(2,1)S(1)}, u32[]{:S(2)}, u32[]{:S(2)}) %collective-permute-start.9) | collective-permute-done | bytes 294944 | tf_op jit(solution)/shard_map/ppermute | solution.py:48
  213.0 0.8 collective-permute-done.13.refs_4_
  213.9 1.6 collective-permute-start.19
  215.6 3.9 %collective-permute-start.22 = (bf16[384,384]{1,0:T(8,128)(2,1)S(1)}, bf16[384,384]{1,0:T(8,128)(2,1)S(1)}, u32[]{:S(2)}, u32[]{:S(2)}) collective-permute-start(bf16[384,384]{1,0:T(8,128)(2,1)S(1)} %collective-permute-done.12.refs_5_), channel_id=1, source_target_pairs={{0,14},{1,15},{2,0},{3,1},{4,2},{5,3},{6,4},{7,5},{8,6},{9,7},{10,... | collective-permute-start | bytes 884744 | tf_op jit(solution)/shard_map/ppermute | solution.py:48
  219.8 4.6 %collective-permute-done.19.refs_2_ = bf16[384,384]{1,0:T(8,128)(2,1)S(1)} collective-permute-done((bf16[384,384]{1,0:T(8,128)(2,1)S(1)}, bf16[384,384]{1,0:T(8,128)(2,1)S(1)}, u32[]{:S(2)}, u32[]{:S(2)}) %collective-permute-start.19) | collective-permute-done | bytes 294944 | tf_op jit(solution)/shard_map/ppermute | solution.py:48
  224.4 1.2 collective-permute-start.15
  225.7 1.2 collective-permute-done.14.refs_4_
  226.9 1.4 collective-permute-start.20
  228.3 4.6 %collective-permute-done.11.refs_3_ = bf16[512,384]{1,0:T(8,128)(2,1)S(1)} collective-permute-done((bf16[512,384]{1,0:T(8,128)(2,1)S(1)}, bf16[512,384]{1,0:T(8,128)(2,1)S(1)}, u32[]{:S(2)}, u32[]{:S(2)}) %collective-permute-start.11) | collective-permute-done | bytes 393248 | tf_op jit(solution)/shard_map/ppermute | solution.py:48
  232.9 1.2 collective-permute-start.23
  234.1 3.1 %shard_map.76 = (f32[256,384]{1,0:T(8,128)S(1)}, f32[256,384]{1,0:T(8,128)S(1)}) custom-call(bf16[256,10240]{1,0:T(8,128)(2,1)S(1)} %copy-done, bf16[256,10240]{1,0:T(8,128)(2,1)} %collective-permute-done.4.refs_1_, bf16[384,384]{1,0:T(8,128)(2,1)S(1)} %collective-permute-done.9.refs_2_, bf16[512,384]{1,0:T(8,128)(2,1)S(1)} %collective-permute-done.11.refs_3_, ...), custom_call_target="tpu_custom_call" | custom-call | flops 1006632960 | bytes 6160384 | tf_op jit(solution)/shard_map/pallas_call | solution.py:122
  237.5 2.4 collective-permute-start.26
  239.9 0.8 collective-permute-done.23.refs_5_
  241.0 4.8 %collective-permute-done.25.refs_3_ = bf16[512,384]{1,0:T(8,128)(2,1)S(1)} collective-permute-done((bf16[512,384]{1,0:T(8,128)(2,1)S(1)}, bf16[512,384]{1,0:T(8,128)(2,1)S(1)}, u32[]{:S(2)}, u32[]{:S(2)}) %collective-permute-start.25) | collective-permute-done | bytes 393248 | tf_op jit(solution)/shard_map/ppermute | solution.py:48
  245.7 2.9 collective-permute-done.26.refs_6_
  248.6 3.0 %shard_map.77 = (f32[256,384]{1,0:T(8,128)S(1)}, f32[256,384]{1,0:T(8,128)S(1)}) custom-call(bf16[256,10240]{1,0:T(8,128)(2,1)S(1)} %copy-done, bf16[256,10240]{1,0:T(8,128)(2,1)} %collective-permute-done.4.refs_1_, bf16[384,384]{1,0:T(8,128)(2,1)S(1)} %collective-permute-done.19.refs_2_, bf16[512,384]{1,0:T(8,128)(2,1)S(1)} %collective-permute-done.25.refs_3_, ...), custom_call_target="tpu_custom_call" | custom-call | flops 1006632960 | bytes 6160384 | tf_op jit(solution)/shard_map/pallas_call | solution.py:122
  251.9 2.7 collective-permute-start.30
  254.6 1.5 collective-permute-start.24
  256.1 6.5 %collective-permute-done.21 = bf16[192,384]{1,0:T(8,128)(2,1)S(1)} collective-permute-done((bf16[192,384]{1,0:T(8,128)(2,1)S(1)}, bf16[192,384]{1,0:T(8,128)(2,1)S(1)}, u32[]{:S(2)}, u32[]{:S(2)}) %collective-permute-start.21) | collective-permute-done | bytes 147488 | tf_op jit(solution)/shard_map/ppermute | solution.py:48
  264.6 1.0 collective-permute-start.29
  265.6 2.3 collective-permute-done.16
  268.0 1.1 collective-permute-start.31
  269.6 2.5 collective-permute-done.18
  272.2 3.1 %shard_map.78 = (f32[256,384]{1,0:T(8,128)S(1)}, f32[256,384]{1,0:T(8,128)S(1)}) custom-call(bf16[256,10240]{1,0:T(8,128)(2,1)S(1)} %copy-done, bf16[256,10240]{1,0:T(8,128)(2,1)} %collective-permute-done.4.refs_1_, bf16[384,384]{1,0:T(8,128)(2,1)S(1)} %collective-permute-done.20.refs_2_, bf16[512,384]{1,0:T(8,128)(2,1)S(1)} %collective-permute-done.28.refs_3_, ...), custom_call_target="tpu_custom_call" | custom-call | flops 1006632960 | bytes 6160384 | tf_op jit(solution)/shard_map/pallas_call | solution.py:122
  275.3 3.1 %shard_map.79 = (bf16[256,384]{1,0:T(8,128)(2,1)S(1)}, bf16[256,384]{1,0:T(8,128)(2,1)S(1)}) custom-call(bf16[256,10240]{1,0:T(8,128)(2,1)S(1)} %copy-done, bf16[256,10240]{1,0:T(8,128)(2,1)} %collective-permute-done.4.refs_1_, bf16[384,384]{1,0:T(8,128)(2,1)S(1)} %pad_maximum_fusion.6.refs_2_, bf16[512,384]{1,0:T(8,128)(2,1)S(1)} %pad_maximum_fusion.5.refs_3_, ...), custom_call_target="tpu_custom_call" | custom-call | flops 1006632960 | bytes 6160384 | tf_op jit(solution)/shard_map/pallas_call | solution.py:122
  278.4 7.6 %collective-permute-start.34 = (bf16[256,384]{1,0:T(8,128)(2,1)S(1)}, bf16[256,384]{1,0:T(8,128)(2,1)S(1)}, u32[]{:S(2)}, u32[]{:S(2)}) collective-permute-start(bf16[256,384]{1,0:T(8,128)(2,1)S(1)} %get-tuple-element.41), channel_id=1, source_target_pairs={{0,1},{1,0},{2,3},{3,2},{4,5},{5,4},{6,7},{7,6},{8,9},{9,8},{10,11... | collective-permute-start | bytes 589832 | tf_op jit(solution)/shard_map/ppermute | solution.py:48
  286.0 1.5 multiply_subtract_fusion
  (58 shorter events, 6.3 us)
Async XLA Ops:
  1.8 5.7 %collective-permute-start = (bf16[80,768]{1,0:T(8,128)(2,1)S(1)}, bf16[80,768]{1,0:T(8,128)(2,1)S(1)}, u32[]{:S(2)}, u32[]{:S(2)}) collective-permute-start(bf16[80,768]{1,0:T(8,128)(2,1)S(1)} %get-tuple-element.61), channel_id=1, source_target_pairs={{0,64},{32,96},{64,128},{96,160},{128,192},{160,224},{192,0},{224,... | collective-permute-start | bytes 368648 | tf_op jit(solution)/shard_map/ppermute | solution.py:44
  3.9 7.8 %collective-permute-start.1 = (bf16[80,768]{1,0:T(8,128)(2,1)S(1)}, bf16[80,768]{1,0:T(8,128)(2,1)S(1)}, u32[]{:S(2)}, u32[]{:S(2)}) collective-permute-start(bf16[80,768]{1,0:T(8,128)(2,1)S(1)} %get-tuple-element.60), channel_id=1, source_target_pairs={{0,128},{32,160},{64,192},{96,224},{128,0},{160,32},{192,64},{224,... | collective-permute-start | bytes 368648 | tf_op jit(solution)/shard_map/ppermute | solution.py:44
  6.3 5.4 %collective-permute-start.2 = (bf16[80,768]{1,0:T(8,128)(2,1)S(1)}, bf16[80,768]{1,0:T(8,128)(2,1)S(1)}, u32[]{:S(2)}, u32[]{:S(2)}) collective-permute-start(bf16[80,768]{1,0:T(8,128)(2,1)S(1)} %get-tuple-element.62), channel_id=1, source_target_pairs={{0,192},{32,224},{64,0},{96,32},{128,64},{160,96},{192,128},{224,1... | collective-permute-start | bytes 368648 | tf_op jit(solution)/shard_map/ppermute | solution.py:44
  12.8 171.2 %copy-start.1 = (f32[320,768]{1,0:T(8,128)S(1)}, f32[320,768]{1,0:T(8,128)}, u32[]{:S(2)}) copy-start(f32[320,768]{1,0:T(8,128)} %param.4) | copy-start | bytes 2949124
  12.8 171.2 %copy-start.2 = (f32[320,768]{1,0:T(8,128)S(1)}, f32[320,768]{1,0:T(8,128)}, u32[]{:S(2)}) copy-start(f32[320,768]{1,0:T(8,128)} %param.5) | copy-start | bytes 2949124
  173.0 61.0 %collective-permute-start.4 = (bf16[256,10240]{1,0:T(8,128)(2,1)}, bf16[256,10240]{1,0:T(8,128)(2,1)}, u32[]{:S(2)}, u32[]{:S(2)}) collective-permute-start(bf16[256,10240]{1,0:T(8,128)(2,1)} %shard_map.75.refs_0_), channel_id=1, source_target_pairs={{0,1},{1,0},{2,3},{3,2},{4,5},{5,4},{6,7},{7,6},{8,9},{9,8},{10,11... | collective-permute-start | bytes 15728648 | tf_op jit(solution)/shard_map/ppermute | solution.py:48
  175.0 9.0 %collective-permute-start.3 = (f32[80,768]{1,0:T(8,128)S(1)}, f32[80,768]{1,0:T(8,128)S(1)}, u32[]{:S(2)}, u32[]{:S(2)}) collective-permute-start(f32[80,768]{1,0:T(8,128)S(1)} %fusion.2), channel_id=1, source_target_pairs={{0,32},{32,0},{64,96},{96,64},{128,160},{160,128},{192,224},{224,1... | collective-permute-start | bytes 737288 | tf_op jit(solution)/shard_map/ppermute | solution.py:44
  184.2 5.3 %collective-permute-start.5 = (bf16[80,768]{1,0:T(8,128)(2,1)S(1)}, bf16[80,768]{1,0:T(8,128)(2,1)S(1)}, u32[]{:S(2)}, u32[]{:S(2)}) collective-permute-start(bf16[80,768]{1,0:T(8,128)(2,1)S(1)} %get-tuple-element.66), channel_id=1, source_target_pairs={{0,192},{32,224},{64,0},{96,32},{128,64},{160,96},{192,128},{224,1... | collective-permute-start | bytes 368648 | tf_op jit(solution)/shard_map/ppermute | solution.py:44
  186.5 5.3 %collective-permute-start.6 = (bf16[80,768]{1,0:T(8,128)(2,1)S(1)}, bf16[80,768]{1,0:T(8,128)(2,1)S(1)}, u32[]{:S(2)}, u32[]{:S(2)}) collective-permute-start(bf16[80,768]{1,0:T(8,128)(2,1)S(1)} %get-tuple-element.65), channel_id=1, source_target_pairs={{0,128},{32,160},{64,192},{96,224},{128,0},{160,32},{192,64},{224,... | collective-permute-start | bytes 368648 | tf_op jit(solution)/shard_map/ppermute | solution.py:44
  186.9 8.4 %collective-permute-start.7 = (bf16[80,768]{1,0:T(8,128)(2,1)S(1)}, bf16[80,768]{1,0:T(8,128)(2,1)S(1)}, u32[]{:S(2)}, u32[]{:S(2)}) collective-permute-start(bf16[80,768]{1,0:T(8,128)(2,1)S(1)} %get-tuple-element.46), channel_id=1, source_target_pairs={{0,64},{32,96},{64,128},{96,160},{128,192},{160,224},{192,0},{224,... | collective-permute-start | bytes 368648 | tf_op jit(solution)/shard_map/ppermute | solution.py:44
  197.3 2.2 collective-permute-start.8
  199.5 34.6 %copy-start = (bf16[256,10240]{1,0:T(8,128)(2,1)S(1)}, bf16[256,10240]{1,0:T(8,128)(2,1)}, u32[]{:S(2)}) copy-start(bf16[256,10240]{1,0:T(8,128)(2,1)} %shard_map.75.refs_0_) | copy-start | bytes 15728644
  199.6 6.7 %collective-permute-start.10 = (bf16[256,384]{1,0:T(8,128)(2,1)S(1)}, bf16[256,384]{1,0:T(8,128)(2,1)S(1)}, u32[]{:S(2)}, u32[]{:S(2)}) collective-permute-start(bf16[256,384]{1,0:T(8,128)(2,1)S(1)} %slice.34), channel_id=1, source_target_pairs={{0,16},{1,17},{2,18},{3,19},{4,20},{5,21},{6,22},{7,23},{8,24},{9,... | collective-permute-start | bytes 589832 | tf_op jit(solution)/shard_map/ppermute | solution.py:48
  200.6 12.4 %collective-permute-start.9 = (bf16[384,384]{1,0:T(8,128)(2,1)S(1)}, bf16[384,384]{1,0:T(8,128)(2,1)S(1)}, u32[]{:S(2)}, u32[]{:S(2)}) collective-permute-start(bf16[384,384]{1,0:T(8,128)(2,1)S(1)} %pad_maximum_fusion.6.refs_2_), channel_id=1, source_target_pairs={{0,2},{1,3},{2,4},{3,5},{4,6},{5,7},{6,8},{7,9},{8,10},{9,11},{10,... | collective-permute-start | bytes 884744 | tf_op jit(solution)/shard_map/ppermute | solution.py:48
  202.3 10.7 %collective-permute-start.12 = (bf16[384,384]{1,0:T(8,128)(2,1)S(1)}, bf16[384,384]{1,0:T(8,128)(2,1)S(1)}, u32[]{:S(2)}, u32[]{:S(2)}) collective-permute-start(bf16[384,384]{1,0:T(8,128)(2,1)S(1)} %pad_maximum_fusion.6.refs_2_), channel_id=1, source_target_pairs={{0,14},{1,15},{2,0},{3,1},{4,2},{5,3},{6,4},{7,5},{8,6},{9,7},{10,... | collective-permute-start | bytes 884744 | tf_op jit(solution)/shard_map/ppermute | solution.py:48
  206.3 7.6 %collective-permute-start.13 = (bf16[384,384]{1,0:T(8,128)(2,1)S(1)}, bf16[384,384]{1,0:T(8,128)(2,1)S(1)}, u32[]{:S(2)}, u32[]{:S(2)}) collective-permute-start(bf16[384,384]{1,0:T(8,128)(2,1)S(1)} %pad_maximum_fusion.6.refs_2_), channel_id=1, source_target_pairs={{0,16},{1,17},{2,18},{3,19},{4,20},{5,21},{6,22},{7,23},{8,24},{9,... | collective-permute-start | bytes 884744 | tf_op jit(solution)/shard_map/ppermute | solution.py:48
  213.9 13.0 %collective-permute-start.14 = (bf16[768,384]{1,0:T(8,128)(2,1)S(1)}, bf16[768,384]{1,0:T(8,128)(2,1)S(1)}, u32[]{:S(2)}, u32[]{:S(2)}) collective-permute-start(bf16[768,384]{1,0:T(8,128)(2,1)S(1)} %pad_maximum_fusion.1), channel_id=1, source_target_pairs={{0,16},{1,17},{2,18},{3,19},{4,20},{5,21},{6,22},{7,23},{8,24},{9,... | collective-permute-start | bytes 1769480 | tf_op jit(solution)/shard_map/ppermute | solution.py:48
  213.9 10.5 %collective-permute-start.19 = (bf16[384,384]{1,0:T(8,128)(2,1)S(1)}, bf16[384,384]{1,0:T(8,128)(2,1)S(1)}, u32[]{:S(2)}, u32[]{:S(2)}) collective-permute-start(bf16[384,384]{1,0:T(8,128)(2,1)S(1)} %collective-permute-done.9.refs_2_), channel_id=1, source_target_pairs={{0,2},{1,3},{2,4},{3,5},{4,6},{5,7},{6,8},{7,9},{8,10},{9,11},{10,... | collective-permute-start | bytes 884744 | tf_op jit(solution)/shard_map/ppermute | solution.py:48
  215.6 10.0 %collective-permute-start.22 = (bf16[384,384]{1,0:T(8,128)(2,1)S(1)}, bf16[384,384]{1,0:T(8,128)(2,1)S(1)}, u32[]{:S(2)}, u32[]{:S(2)}) collective-permute-start(bf16[384,384]{1,0:T(8,128)(2,1)S(1)} %collective-permute-done.12.refs_5_), channel_id=1, source_target_pairs={{0,14},{1,15},{2,0},{3,1},{4,2},{5,3},{6,4},{7,5},{8,6},{9,7},{10,... | collective-permute-start | bytes 884744 | tf_op jit(solution)/shard_map/ppermute | solution.py:48
  219.6 13.3 %collective-permute-start.11 = (bf16[512,384]{1,0:T(8,128)(2,1)S(1)}, bf16[512,384]{1,0:T(8,128)(2,1)S(1)}, u32[]{:S(2)}, u32[]{:S(2)}) collective-permute-start(bf16[512,384]{1,0:T(8,128)(2,1)S(1)} %pad_maximum_fusion.5.refs_3_), channel_id=1, source_target_pairs={{0,2},{1,3},{2,4},{3,5},{4,6},{5,7},{6,8},{7,9},{8,10},{9,11},{10,... | collective-permute-start | bytes 1179656 | tf_op jit(solution)/shard_map/ppermute | solution.py:48
  224.4 9.6 %collective-permute-start.15 = (bf16[512,384]{1,0:T(8,128)(2,1)S(1)}, bf16[512,384]{1,0:T(8,128)(2,1)S(1)}, u32[]{:S(2)}, u32[]{:S(2)}) collective-permute-start(bf16[512,384]{1,0:T(8,128)(2,1)S(1)} %pad_maximum_fusion.5.refs_3_), channel_id=1, source_target_pairs={{0,14},{1,15},{2,0},{3,1},{4,2},{5,3},{6,4},{7,5},{8,6},{9,7},{10,... | collective-permute-start | bytes 1179656 | tf_op jit(solution)/shard_map/ppermute | solution.py:48
  226.9 13.9 %collective-permute-start.27 = (bf16[768,384]{1,0:T(8,128)(2,1)S(1)}, bf16[768,384]{1,0:T(8,128)(2,1)S(1)}, u32[]{:S(2)}, u32[]{:S(2)}) collective-permute-start(bf16[768,384]{1,0:T(8,128)(2,1)S(1)} %pad_maximum_fusion.2), channel_id=1, source_target_pairs={{0,16},{1,17},{2,18},{3,19},{4,20},{5,21},{6,22},{7,23},{8,24},{9,... | collective-permute-start | bytes 1769480 | tf_op jit(solution)/shard_map/ppermute | solution.py:48
  226.9 13.0 %collective-permute-start.20 = (bf16[384,384]{1,0:T(8,128)(2,1)S(1)}, bf16[384,384]{1,0:T(8,128)(2,1)S(1)}, u32[]{:S(2)}, u32[]{:S(2)}) collective-permute-start(bf16[384,384]{1,0:T(8,128)(2,1)S(1)} %collective-permute-done.19.refs_2_), channel_id=1, source_target_pairs={{0,2},{1,3},{2,4},{3,5},{4,6},{5,7},{6,8},{7,9},{8,10},{9,11},{10,... | collective-permute-start | bytes 884744 | tf_op jit(solution)/shard_map/ppermute | solution.py:48
  232.9 7.8 %collective-permute-start.23 = (bf16[384,384]{1,0:T(8,128)(2,1)S(1)}, bf16[384,384]{1,0:T(8,128)(2,1)S(1)}, u32[]{:S(2)}, u32[]{:S(2)}) collective-permute-start(bf16[384,384]{1,0:T(8,128)(2,1)S(1)} %collective-permute-done.22.refs_5_), channel_id=1, source_target_pairs={{0,14},{1,15},{2,0},{3,1},{4,2},{5,3},{6,4},{7,5},{8,6},{9,7},{10,... | collective-permute-start | bytes 884744 | tf_op jit(solution)/shard_map/ppermute | solution.py:48
  237.1 8.6 %collective-permute-start.25 = (bf16[512,384]{1,0:T(8,128)(2,1)S(1)}, bf16[512,384]{1,0:T(8,128)(2,1)S(1)}, u32[]{:S(2)}, u32[]{:S(2)}) collective-permute-start(bf16[512,384]{1,0:T(8,128)(2,1)S(1)} %collective-permute-done.11.refs_3_), channel_id=1, source_target_pairs={{0,2},{1,3},{2,4},{3,5},{4,6},{5,7},{6,8},{7,9},{8,10},{9,11},{10,... | collective-permute-start | bytes 1179656 | tf_op jit(solution)/shard_map/ppermute | solution.py:48
  237.5 11.1 %collective-permute-start.26 = (bf16[512,384]{1,0:T(8,128)(2,1)S(1)}, bf16[512,384]{1,0:T(8,128)(2,1)S(1)}, u32[]{:S(2)}, u32[]{:S(2)}) collective-permute-start(bf16[512,384]{1,0:T(8,128)(2,1)S(1)} %collective-permute-done.15.refs_6_), channel_id=1, source_target_pairs={{0,14},{1,15},{2,0},{3,1},{4,2},{5,3},{6,4},{7,5},{8,6},{9,7},{10,... | collective-permute-start | bytes 1179656 | tf_op jit(solution)/shard_map/ppermute | solution.py:48
  240.7 22.9 %collective-permute-start.32 = (bf16[768,384]{1,0:T(8,128)(2,1)S(1)}, bf16[768,384]{1,0:T(8,128)(2,1)S(1)}, u32[]{:S(2)}, u32[]{:S(2)}) collective-permute-start(bf16[768,384]{1,0:T(8,128)(2,1)S(1)} %pad_maximum_fusion.3), channel_id=1, source_target_pairs={{0,16},{1,17},{2,18},{3,19},{4,20},{5,21},{6,22},{7,23},{8,24},{9,... | collective-permute-start | bytes 1769480 | tf_op jit(solution)/shard_map/ppermute | solution.py:48
  251.7 12.6 %collective-permute-start.28 = (bf16[512,384]{1,0:T(8,128)(2,1)S(1)}, bf16[512,384]{1,0:T(8,128)(2,1)S(1)}, u32[]{:S(2)}, u32[]{:S(2)}) collective-permute-start(bf16[512,384]{1,0:T(8,128)(2,1)S(1)} %collective-permute-done.25.refs_3_), channel_id=1, source_target_pairs={{0,2},{1,3},{2,4},{3,5},{4,6},{5,7},{6,8},{7,9},{8,10},{9,11},{10,... | collective-permute-start | bytes 1179656 | tf_op jit(solution)/shard_map/ppermute | solution.py:48
  251.8 10.8 %collective-permute-start.21 = (bf16[192,384]{1,0:T(8,128)(2,1)S(1)}, bf16[192,384]{1,0:T(8,128)(2,1)S(1)}, u32[]{:S(2)}, u32[]{:S(2)}) collective-permute-start(bf16[192,384]{1,0:T(8,128)(2,1)S(1)} %slice.35), channel_id=1, source_target_pairs={{0,2},{1,3},{2,4},{3,5},{4,6},{5,7},{6,8},{7,9},{8,10},{9,11},{10,... | collective-permute-start | bytes 442376 | tf_op jit(solution)/shard_map/ppermute | solution.py:48
  251.9 12.7 %collective-permute-start.30 = (bf16[512,384]{1,0:T(8,128)(2,1)S(1)}, bf16[512,384]{1,0:T(8,128)(2,1)S(1)}, u32[]{:S(2)}, u32[]{:S(2)}) collective-permute-start(bf16[512,384]{1,0:T(8,128)(2,1)S(1)} %collective-permute-done.26.refs_6_), channel_id=1, source_target_pairs={{0,14},{1,15},{2,0},{3,1},{4,2},{5,3},{6,4},{7,5},{8,6},{9,7},{10,... | collective-permute-start | bytes 1179656 | tf_op jit(solution)/shard_map/ppermute | solution.py:48
  254.6 8.3 %collective-permute-start.24 = (bf16[192,384]{1,0:T(8,128)(2,1)S(1)}, bf16[192,384]{1,0:T(8,128)(2,1)S(1)}, u32[]{:S(2)}, u32[]{:S(2)}) collective-permute-start(bf16[192,384]{1,0:T(8,128)(2,1)S(1)} %slice.36), channel_id=1, source_target_pairs={{0,14},{1,15},{2,0},{3,1},{4,2},{5,3},{6,4},{7,5},{8,6},{9,7},{10,... | collective-permute-start | bytes 442376 | tf_op jit(solution)/shard_map/ppermute | solution.py:48
  262.6 5.3 %collective-permute-start.16 = (f32[80,768]{1,0:T(8,128)S(1)}, f32[80,768]{1,0:T(8,128)S(1)}, u32[]{:S(2)}, u32[]{:S(2)}) collective-permute-start(f32[80,768]{1,0:T(8,128)S(1)} %get-tuple-element.28), channel_id=1, source_target_pairs={{0,192},{32,224},{64,0},{96,32},{128,64},{160,96},{192,128},{224,1... | collective-permute-start | bytes 737288 | tf_op jit(solution)/shard_map/ppermute | solution.py:44
  262.9 6.7 %collective-permute-start.17 = (f32[80,768]{1,0:T(8,128)S(1)}, f32[80,768]{1,0:T(8,128)S(1)}, u32[]{:S(2)}, u32[]{:S(2)}) collective-permute-start(f32[80,768]{1,0:T(8,128)S(1)} %get-tuple-element.28), channel_id=1, source_target_pairs={{0,128},{32,160},{64,192},{96,224},{128,0},{160,32},{192,64},{224,... | collective-permute-start | bytes 737288 | tf_op jit(solution)/shard_map/ppermute | solution.py:44
  263.7 8.4 %collective-permute-start.18 = (f32[80,768]{1,0:T(8,128)S(1)}, f32[80,768]{1,0:T(8,128)S(1)}, u32[]{:S(2)}, u32[]{:S(2)}) collective-permute-start(f32[80,768]{1,0:T(8,128)S(1)} %get-tuple-element.28), channel_id=1, source_target_pairs={{0,64},{32,96},{64,128},{96,160},{128,192},{160,224},{192,0},{224,... | collective-permute-start | bytes 737288 | tf_op jit(solution)/shard_map/ppermute | solution.py:44
  264.3 11.0 %collective-permute-start.33 = (bf16[384,384]{1,0:T(8,128)(2,1)S(1)}, bf16[384,384]{1,0:T(8,128)(2,1)S(1)}, u32[]{:S(2)}, u32[]{:S(2)}) collective-permute-start(bf16[384,384]{1,0:T(8,128)(2,1)S(1)} %constant_dynamic-update-slice_fusion.refs_5_), channel_id=1, source_target_pairs={{0,16},{1,17},{2,18},{3,19},{4,20},{5,21},{6,22},{7,23},{8,24},{9,... | collective-permute-start | bytes 884744 | tf_op jit(solution)/shard_map/ppermute | solution.py:48
  264.6 10.7 %collective-permute-start.29 = (bf16[256,384]{1,0:T(8,128)(2,1)S(1)}, bf16[256,384]{1,0:T(8,128)(2,1)S(1)}, u32[]{:S(2)}, u32[]{:S(2)}) collective-permute-start(bf16[256,384]{1,0:T(8,128)(2,1)S(1)} %slice.37), channel_id=1, source_target_pairs={{0,2},{1,3},{2,4},{3,5},{4,6},{5,7},{6,8},{7,9},{8,10},{9,11},{10,... | collective-permute-start | bytes 589832 | tf_op jit(solution)/shard_map/ppermute | solution.py:48
  268.0 7.3 %collective-permute-start.31 = (bf16[256,384]{1,0:T(8,128)(2,1)S(1)}, bf16[256,384]{1,0:T(8,128)(2,1)S(1)}, u32[]{:S(2)}, u32[]{:S(2)}) collective-permute-start(bf16[256,384]{1,0:T(8,128)(2,1)S(1)} %slice.38), channel_id=1, source_target_pairs={{0,14},{1,15},{2,0},{3,1},{4,2},{5,3},{6,4},{7,5},{8,6},{9,7},{10,... | collective-permute-start | bytes 589832 | tf_op jit(solution)/shard_map/ppermute | solution.py:48
  278.4 9.1 %collective-permute-start.34 = (bf16[256,384]{1,0:T(8,128)(2,1)S(1)}, bf16[256,384]{1,0:T(8,128)(2,1)S(1)}, u32[]{:S(2)}, u32[]{:S(2)}) collective-permute-start(bf16[256,384]{1,0:T(8,128)(2,1)S(1)} %get-tuple-element.41), channel_id=1, source_target_pairs={{0,1},{1,0},{2,3},{3,2},{4,5},{5,4},{6,7},{7,6},{8,9},{9,8},{10,11... | collective-permute-start | bytes 589832 | tf_op jit(solution)/shard_map/ppermute | solution.py:48

commit v2 on v0

v2 whole, which is shorter than its diff:
```python
import functools
import math

import jax
import jax.numpy as jnp
from jax import lax
from jax.experimental import pallas as pl
from jax.experimental.pallas import tpu as pltpu
from jax.sharding import PartitionSpec as P

D = 10240
COLS = 768
REPS = 8
OUTER_RATE = 0.7
MOMENT_DECAY = 0.9
KEEP_LOCAL = 0.5
SCALE = 1.0 / math.sqrt(D)

NX, NYH, NYL, NZ, NC = 4, 2, 2, 8, 2
ROWS = D // (NYL * NZ * NC)
CHIP = ROWS * NC
SLICE = ROWS // NX
FAR = ROWS // 2
BIG = 60 * 1024 * 1024
LONG = 30_000_000_000
CHUNKS = 3
WIDTH = COLS // CHUNKS


def rep_perm(dx, dy):
    return [
        (x * NYH + y, ((x + dx) % NX) * NYH + (y ^ dy)) for x in range(NX) for y in range(NYH)
    ]


def send_rep(v, dx, dy, name):
    with jax.named_scope(name):
        return lax.ppermute(v, "rep", rep_perm(dx, dy))


def send(v, to, name, cores=(0, 1)):
    perm = []
    for y in range(NYL):
        for z in range(NZ):
            for c in cores:
                ty, tz, tc = to(y, z, c)
                perm.append(((y * NZ + z) * NC + c, (ty * NZ + tz % NZ) * NC + tc))
    with jax.named_scope(name):
        return lax.ppermute(v, "fsdp", perm)


def to_core(y, z, c):
    return y, z, 1 - c


def to_side(y, z, c):
    return 1 - y, z, c


def to_cross(y, z, c):
    return 1 - y, z, 1 - c


def to_ring(y, z, c):
    return y, (z - 1 if c else z + 1), c


def fence_kernel(*refs):
    del refs


def fence(values, *earlier):
    anywhere = pl.BlockSpec(memory_space=pl.ANY)
    operands = tuple(values) + earlier
    return pl.pallas_call(
        fence_kernel,
        out_shape=[jax.ShapeDtypeStruct(v.shape, v.dtype) for v in values],
        in_specs=[anywhere] * len(operands),
        out_specs=[anywhere] * len(values),
        input_output_aliases={i: i for i in range(len(values))},
        compiler_params=pltpu.CompilerParams(vmem_limit_bytes=1024 * 1024),
        cost_estimate=pl.CostEstimate(flops=LONG, bytes_accessed=4096, transcendentals=0),
    )(*operands)


def in_order(slices, x):
    rows = []
    for place in range(NX):
        value = slices[0]
        for k in range(1, NX):
            value = jnp.where((x - k) % NX == place, slices[k], value)
        rows.append(value)
    return jnp.concatenate(rows, axis=0)


def dot(a, b):
    return jnp.dot(a, b, preferred_element_type=jnp.float32)


def either(core, first, second):
    return jnp.where(core == 0, first, second)


def stack(*rows):
    return jnp.concatenate(rows, axis=0)


HERE = pl.BlockSpec(memory_space=pl.ANY)
WHOLE = pl.BlockSpec(memory_space=pltpu.VMEM)
SCALARS = pl.BlockSpec(memory_space=pltpu.SMEM)

A_ROWS, B_ROWS = (0, ROWS), (ROWS, 0)
A_NEAR, A_REST = (0, ROWS + FAR), (FAR, ROWS)
B_NEAR, B_REST = (ROWS, FAR), (ROWS + FAR, 0)


def product_kernel(slots, parts, near, empty, totals, counts, where_ref, *refs):
    core = where_ref[0]
    split = [0]
    for count in counts:
        split.append(split[-1] + count)
    tokens, arrays, before, outs = (refs[i:j] for i, j in zip(split, split[1:]))
    tok, weight, total, sems = refs[split[-1] :]
    rows = tokens[0].shape[0]
    started = []

    def start(source, target):
        copy = pltpu.make_async_copy(source, target, sems.at[len(started)])
        copy.start()
        started.append(copy)

    def spot(slot, place, size):
        at = slot * CHIP + either(core, place[0], place[1])
        return pl.ds(pl.multiple_of(at, 16), size)

    def extra(own, n):
        last, cols = (len(slots) - 1) * CHIP, pl.ds(n * WIDTH, WIDTH)
        pair = (arrays[-4], arrays[-3]) if own else (arrays[-2], arrays[-1])
        return [
            pltpu.make_async_copy(
                array.at[:, cols],
                weight.at[n, pl.ds(last + i * ROWS, ROWS)],
                sems.at[sems.shape[0] - 1 - 2 * n - i],
            )
            for i, array in enumerate(pair)
        ]

    for s, slot in enumerate(slots):
        span = pl.ds(pl.multiple_of(where_ref[slot] * CHIP, 128), CHIP)
        for i, ref in enumerate(tokens):
            start(ref.at[:, span], tok.at[pl.ds(i * rows, rows), pl.ds(s * CHIP, CHIP)])
    ends = []
    for n in range(CHUNKS):
        cols = pl.ds(n * WIDTH, WIDTH)
        for array, first, size, slot, place in parts:
            start(
                arrays[array].at[pl.ds(first, size), cols],
                weight.at[n, spot(slot, place, size)],
            )
        for i, ref in enumerate(before):
            start(ref.at[:, cols], total.at[n, pl.ds(i * rows, rows)])
        if near:

            @pl.when(core == 0)
            def _(n=n):
                for copy in extra(True, n):
                    copy.start()

            @pl.when(core == 1)
            def _(n=n):
                for copy in extra(False, n):
                    copy.start()

        ends.append(len(started))
    for n in range(CHUNKS):
        for slot, place in empty:
            weight[n, spot(slot, place, FAR), :] = jnp.zeros((FAR, WIDTH), jnp.bfloat16)
    done = 0
    for n in range(CHUNKS):
        for copy in started[done : ends[n]]:
            copy.wait()
        done = ends[n]
        if near:
            for copy in extra(True, n):
                copy.wait()
        value = jnp.dot(tok[...], weight[n], preferred_element_type=jnp.float32)
        if totals:
            value = value + total[n]
        for i, out in enumerate(outs):
            out[:, n * WIDTH : (n + 1) * WIDTH] = value[i * rows : (i + 1) * rows].astype(out.dtype)


def product_step(where, slots, tokens, arrays, parts, near, empty, totals, final=False):
    rows, outs, depth = tokens[0].shape[0], len(tokens), len(slots) * CHIP
    kinds = (jnp.float32, jnp.bfloat16 if final else jnp.float32)
    operands = tuple(tokens) + tuple(arrays) + tuple(near) + tuple(totals)
    counts = (outs, len(arrays) + len(near), len(totals), outs)
    copies = len(slots) * outs + CHUNKS * (len(parts) + len(totals) + 2)
    return pl.pallas_call(
        functools.partial(product_kernel, slots, parts, bool(near), empty, bool(totals), counts),
        out_shape=[jax.ShapeDtypeStruct((rows, COLS), k) for k in kinds],
        in_specs=[SCALARS] + [HERE] * len(operands),
        out_specs=[WHOLE] * outs,
        scratch_shapes=[
            pltpu.VMEM((outs * rows, depth), jnp.bfloat16),
            pltpu.VMEM((CHUNKS, depth, WIDTH), jnp.bfloat16),
            pltpu.VMEM((CHUNKS, outs * rows, WIDTH), jnp.float32),
            pltpu.SemaphoreType.DMA((copies,)),
        ],
        compiler_params=pltpu.CompilerParams(vmem_limit_bytes=BIG),
        cost_estimate=pl.CostEstimate(
            flops=LONG,
            bytes_accessed=depth * (2 * outs * rows + 2 * COLS) + 8 * rows * COLS,
            transcendentals=0,
        ),
    )(where, *operands)


def on_device(global_w, momentum, local_w, tokens):
    local = local_w[0]
    x = lax.axis_index("rep") // NYH
    me = lax.axis_index("fsdp")
    core, z, y = me % NC, (me // NC) % NZ, me // (NC * NZ)

    def own_at(d):
        return y * NZ + either(core, z - d, z + d) % NZ

    def part_at(d):
        return (1 - y) * NZ + either(core, z - d, z + d) % NZ

    near_at = either(core, y, 1 - y) * NZ + z

    where = [core, near_at] + [at(d) for d in range(1, 5) for at in (own_at, part_at)]
    where = jnp.stack(where).astype(jnp.int32)

    def quarter(v, place):
        return lax.dynamic_slice(v, (place * SLICE, 0), (SLICE, COLS))

    raw = [quarter(local, x)] + [
        send_rep(quarter(local, (x + k) % NX), k, 0, "quarters") for k in range(1, NX)
    ]
    global_part, moment_part = quarter(global_w, x), quarter(momentum, x)
    four = sum(global_part - r.astype(jnp.float32) for r in raw)
    gradient = (four + send_rep(four, 0, 1, "four")) / REPS
    mine = tokens[0]
    other = send(mine, to_core, "other")

    def update(global_rows, moment_rows, gradient):
        new_moment = MOMENT_DECAY * moment_rows + gradient
        return global_rows - OUTER_RATE * (gradient + MOMENT_DECAY * new_moment), new_moment

    def blend(local_rows, new_rows):
        return (
            KEEP_LOCAL * local_rows.astype(jnp.float32) + (1.0 - KEEP_LOCAL) * new_rows
        ).astype(jnp.bfloat16)

    new_part, _ = update(global_part, moment_part, gradient)
    home = [blend(r, new_part) for r in raw]
    back = [home[0]] + [send_rep(home[NX - k], k, 0, "home") for k in range(1, NX)]
    shard = in_order(back, x)

    def near_half(v):
        return either(core, v[:FAR], v[FAR:])

    tokens = (mine, other)
    a = shard
    b = send(shard, to_core, "b")
    a1 = send(a, to_ring, "a1")
    part_b = send(shard, to_cross, "part_b")
    (b,) = fence((b,))
    b1 = send(b, to_ring, "b1")
    (a1,) = fence((a1,), b)
    a2 = send(a1, to_ring, "a2")
    side1 = send(a1, to_side, "side1")
    (part_b,) = fence((part_b,), a1)
    part_b1 = send(part_b, to_ring, "part_b1")
    side = send(shard, to_side, "side", (1,))
    (b1,) = fence((b1,), part_b)
    b2 = send(b1, to_ring, "b2")
    (a2,) = fence((a2,), b1)
    a3 = send(a2, to_ring, "a3")
    side2 = send(a2, to_side, "side2")
    (part_b1,) = fence((part_b1,), a2)
    part_b2 = send(part_b1, to_ring, "part_b2")
    totals = product_step(
        where, (2, 1), tokens, (a1, b1),
        ((0, 0, ROWS, 0, A_ROWS), (1, 0, ROWS, 0, B_ROWS)),
        (a, b, part_b, side), (), (),
    )
    b2, *totals = fence((b2, *totals), part_b1)
    b3 = send(b2, to_ring, "b3")
    (a3,) = fence((a3,), b2)
    a4 = send(near_half(a3), to_ring, "a4")
    side3 = send(a3, to_side, "side3")
    (gradient,) = fence((gradient,), a3)
    sums = [send_rep(gradient, k, 0, "gradient") for k in range(1, NX)]
    (part_b2,) = fence((part_b2,), a3)
    part_b3 = send(part_b2, to_ring, "part_b3")
    totals = product_step(
        where, (4, 5, 3), tokens,
        (a2, b2, side2, part_b2, side1, part_b1),
        (
            (0, 0, ROWS, 0, A_ROWS), (1, 0, ROWS, 0, B_ROWS),
            (2, 0, ROWS, 1, A_ROWS), (3, 0, ROWS, 1, B_ROWS),
            (4, 0, ROWS, 2, A_ROWS), (5, 0, ROWS, 2, B_ROWS),
        ),
        (), (), totals,
    )
    b3, *totals = fence((b3, *totals), part_b2)
    b4 = send(near_half(b3), to_ring, "b4")
    (a4,) = fence((a4,), b3)
    far_side = send(a4, to_side, "far_side")
    sums = [gradient] + list(fence(sums, a4))

    full = in_order(sums, x)
    new_global, new_moment = update(global_w, momentum, full)
    new_local = blend(local, new_global)

    (part_b3,) = fence((part_b3,), new_local)
    part_b4 = send(near_half(part_b3), to_ring, "part_b4")
    totals = product_step(
        where, (6, 7), tokens, (a3, b3, side3, part_b3),
        (
            (0, 0, ROWS, 0, A_ROWS), (1, 0, ROWS, 0, B_ROWS),
            (2, 0, ROWS, 1, A_ROWS), (3, 0, ROWS, 1, B_ROWS),
        ),
        (), (), totals,
    )
    total, late = product_step(
        where, (8, 9), tokens, (a4, b4, far_side, part_b4),
        (
            (0, 0, FAR, 0, A_NEAR), (1, 0, FAR, 0, B_NEAR),
            (2, 0, FAR, 1, A_NEAR), (3, 0, FAR, 1, B_NEAR),
        ),
        (), ((0, A_REST), (0, B_REST), (1, A_REST), (1, B_REST)), totals, True,
    )
    late = send(late, to_core, "late")
    projected = ((total + late.astype(jnp.float32)) * SCALE).astype(jnp.bfloat16)
    return (new_global, new_moment, new_local[None], projected[None])


def solution(mesh):
    return jax.shard_map(
        on_device,
        mesh=mesh,
        in_specs=(P("fsdp", None), P("fsdp", None), P("rep", "fsdp", None), P("rep", "fsdp", None)),
        out_specs=(
            P("fsdp", None),
            P("fsdp", None),
            P("rep", "fsdp", None),
            P("rep", "fsdp", None),
        ),
        check_vma=False,
    )
```

time: 224 us -> 131 us (0.58)
  waiting for transfers between devices: 192 us -> 31.4 us
  starting transfers between devices: 0.08 us -> 51.7 us
  Pallas kernels: 0 us -> 24.1 us
  between operations: 14 us -> 0.97 us
  local copies, waits for them, and re-layouts: 0.92 us -> 13.9 us
  matrix products: 11.2 us -> 0 us
    all_gather x1 -> x0, waiting for transfers between devices: 97.8 us -> none  [on_device(): lax.all_gather(blended, 'fsdp', axis=0, tiled=True)]
    psum x1 -> x0, waiting for transfers between devices: 94 us -> none  [on_device(): summed = lax.psum(pseudo_terms(global_w, local_rows), 'rep')]
    ppermute x0 -> x31, starting transfers between devices: none -> 51.7 us  [the longest x21 38.5 us: send(): return lax.ppermute(v, 'fsdp', perm)]
    ppermute x0 -> x31, waiting for transfers between devices: none -> 31.4 us  [the longest x21 17.2 us: send(): return lax.ppermute(v, 'fsdp', perm)]
    pallas_call x0 -> x18, Pallas kernels: none -> 24.1 us  [the longest x4 24.1 us: product_step(): pl.pallas_call(functools.partial(product_kernel, slots, parts, bool(near)...]
    unnamed x1 -> x52, local copies, waits for them, and re-layouts: 0.92 us -> 12.2 us
    dot_general x1 -> x0, matrix products: 11.2 us -> none  [on_device(): jnp.dot(rows_in, lax.all_gather(blended, 'fsdp', axis=0, tiled=True), pre...]
    sub x1 -> x0, other arithmetic: 2.35 us -> none  [pseudo_terms(): return global_part - local_part.astype(jnp.float32)]
  transfers between devices with their start and end apart: 2 -> 31, of which waited for: 2 -> 13; matrix products, arithmetic and copies ran while one was open for 0% -> 2% of each run, Pallas kernels for 0% -> 14%
where the time goes in v2:
time: 131 us; the launch traced here: 130 us
  starting transfers between devices  51.7 us (39%)
  waiting for transfers between devices  31.4 us (24%)
  Pallas kernels  24.1 us (18%)
  local copies, waits for them, and re-layouts  13.9 us (11%)
  other arithmetic  7.96 us (6%)
    ppermute x21, starting transfers between devices, send(): return lax.ppermute(v, 'fsdp', perm)  38.5 us
    pallas_call x4, Pallas kernels, product_step(): pl.pallas_call(functools.partial(product_kernel, slots, parts, bool(near)...  24.1 us
    ppermute x21, waiting for transfers between devices, send(): return lax.ppermute(v, 'fsdp', perm)  17.2 us
    ppermute x10, waiting for transfers between devices, send_rep(): return lax.ppermute(v, 'rep', rep_perm(dx, dy))  14.2 us
    ppermute x10, starting transfers between devices, send_rep(): return lax.ppermute(v, 'rep', rep_perm(dx, dy))  13.2 us
    unnamed x52, local copies, waits for them, and re-layouts  12.2 us
    convert_element_type x3, other arithmetic, blend(): return (KEEP_LOCAL * local_rows.astype(jnp.float32) + (1.0 - KEEP_LOCAL)...  2.82 us
  transfers between devices with their start and end apart: 31, of which 13 were waited for; matrix products, arithmetic and copies ran while one was open for 2% of the time, Pallas kernels for 14%

profile of v2, /device:TPU:1, one launch (start us, length us, event | category | flops | bytes accessed | tf_op | source)
XLA Modules:
  0.0 130.0 jit_solution(10424262122506996675)
XLA Ops:
  0.7 1.1 dynamic-slice_bitcast_fusion.1
  1.8 2.1 %collective-permute-start = (bf16[80,768]{1,0:T(8,128)(2,1)S(1)}, bf16[80,768]{1,0:T(8,128)(2,1)S(1)}, u32[]{:S(2)}, u32[]{:S(2)}) collective-permute-start(bf16[80,768]{1,0:T(8,128)(2,1)S(1)} %get-tuple-element.54), channel_id=1, source_target_pairs={{0,64},{32,96},{64,128},{96,160},{128,192},{160,224},{192,0},{224,... | collective-permute-start | bytes 368648 | tf_op jit(solution)/shard_map/quarters/ppermute | solution.py:38
  3.9 2.5 %collective-permute-start.1 = (bf16[80,768]{1,0:T(8,128)(2,1)S(1)}, bf16[80,768]{1,0:T(8,128)(2,1)S(1)}, u32[]{:S(2)}, u32[]{:S(2)}) collective-permute-start(bf16[80,768]{1,0:T(8,128)(2,1)S(1)} %get-tuple-element.53), channel_id=1, source_target_pairs={{0,128},{32,160},{64,192},{96,224},{128,0},{160,32},{192,64},{224,... | collective-permute-start | bytes 368648 | tf_op jit(solution)/shard_map/quarters/ppermute | solution.py:38
  6.3 1.2 collective-permute-start.2
  7.5 4.2 %collective-permute-done.1 = bf16[80,768]{1,0:T(8,128)(2,1)S(1)} collective-permute-done((bf16[80,768]{1,0:T(8,128)(2,1)S(1)}, bf16[80,768]{1,0:T(8,128)(2,1)S(1)}, u32[]{:S(2)}, u32[]{:S(2)}) %collective-permute-start.1) | collective-permute-done | bytes 122912 | tf_op jit(solution)/shard_map/quarters/ppermute | solution.py:38
  11.7 1.1 fusion.5
  12.8 3.0 %collective-permute-start.3 = (f32[80,768]{1,0:T(8,128)S(1)}, f32[80,768]{1,0:T(8,128)S(1)}, u32[]{:S(2)}, u32[]{:S(2)}) collective-permute-start(f32[80,768]{1,0:T(8,128)S(1)} %fusion.5), channel_id=1, source_target_pairs={{0,32},{32,0},{64,96},{96,64},{128,160},{160,128},{192,224},{224,1... | collective-permute-start | bytes 737288 | tf_op jit(solution)/shard_map/four/ppermute | solution.py:38
  15.8 4.1 %collective-permute-done.3 = f32[80,768]{1,0:T(8,128)S(1)} collective-permute-done((f32[80,768]{1,0:T(8,128)S(1)}, f32[80,768]{1,0:T(8,128)S(1)}, u32[]{:S(2)}, u32[]{:S(2)}) %collective-permute-start.3) | collective-permute-done | bytes 245792 | tf_op jit(solution)/shard_map/four/ppermute | solution.py:38
  19.9 1.2 fusion.11
  21.2 2.4 %collective-permute-start.4 = (bf16[80,768]{1,0:T(8,128)(2,1)S(1)}, bf16[80,768]{1,0:T(8,128)(2,1)S(1)}, u32[]{:S(2)}, u32[]{:S(2)}) collective-permute-start(bf16[80,768]{1,0:T(8,128)(2,1)S(1)} %get-tuple-element.57), channel_id=1, source_target_pairs={{0,192},{32,224},{64,0},{96,32},{128,64},{160,96},{192,128},{224,1... | collective-permute-start | bytes 368648 | tf_op jit(solution)/shard_map/home/ppermute | solution.py:38
  24.3 2.5 %collective-permute-done.4 = bf16[80,768]{1,0:T(8,128)(2,1)S(1)} collective-permute-done((bf16[80,768]{1,0:T(8,128)(2,1)S(1)}, bf16[80,768]{1,0:T(8,128)(2,1)S(1)}, u32[]{:S(2)}, u32[]{:S(2)}) %collective-permute-start.4) | collective-permute-done | bytes 122912 | tf_op jit(solution)/shard_map/home/ppermute | solution.py:38
  26.7 2.2 %collective-permute-done.5 = bf16[80,768]{1,0:T(8,128)(2,1)S(1)} collective-permute-done((bf16[80,768]{1,0:T(8,128)(2,1)S(1)}, bf16[80,768]{1,0:T(8,128)(2,1)S(1)}, u32[]{:S(2)}, u32[]{:S(2)}) %collective-permute-start.5) | collective-permute-done | bytes 122912 | tf_op jit(solution)/shard_map/home/ppermute | solution.py:38
  28.9 1.2 collective-permute-done.6
  30.1 1.0 select_select_fusion.7
  31.2 0.8 pad_maximum_fusion.1.refs_4_
  32.0 4.2 %collective-permute-start.8 = (bf16[320,768]{1,0:T(8,128)(2,1)}, bf16[320,768]{1,0:T(8,128)(2,1)S(1)}, u32[]{:S(2)}, u32[]{:S(2)}) collective-permute-start(bf16[320,768]{1,0:T(8,128)(2,1)} %pad_maximum_fusion.1.refs_4_), channel_id=1, source_target_pairs={{0,1},{1,0},{2,3},{3,2},{4,5},{5,4},{6,7},{7,6},{8,9},{9,8},{10,11... | collective-permute-start | bytes 1474568 | tf_op jit(solution)/shard_map/b/ppermute | solution.py:49
  36.8 5.6 %collective-permute-start.7 = (bf16[320,768]{1,0:T(8,128)(2,1)}, bf16[320,768]{1,0:T(8,128)(2,1)}, u32[]{:S(2)}, u32[]{:S(2)}) collective-permute-start(bf16[320,768]{1,0:T(8,128)(2,1)} %pad_maximum_fusion.1.refs_4_), channel_id=1, source_target_pairs={{0,2},{1,15},{2,4},{3,1},{4,6},{5,3},{6,8},{7,5},{8,10},{9,7},{10,... | collective-permute-start | bytes 1474568 | tf_op jit(solution)/shard_map/a1/ppermute | solution.py:49
  42.5 3.2 %collective-permute-start.15 = (bf16[320,768]{1,0:T(8,128)(2,1)}, bf16[320,768]{1,0:T(8,128)(2,1)}, u32[]{:S(2)}, u32[]{:S(2)}) collective-permute-start(bf16[320,768]{1,0:T(8,128)(2,1)} %pad_maximum_fusion.1.refs_4_), channel_id=1, source_target_pairs={{1,17},{3,19},{5,21},{7,23},{9,25},{11,27},{13,29},{15,31},{17,1},... | collective-permute-start | bytes 1474568 | tf_op jit(solution)/shard_map/side/ppermute | solution.py:49
  46.5 2.0 %collective-permute-done.7.refs_0_ = bf16[320,768]{1,0:T(8,128)(2,1)} collective-permute-done((bf16[320,768]{1,0:T(8,128)(2,1)}, bf16[320,768]{1,0:T(8,128)(2,1)}, u32[]{:S(2)}, u32[]{:S(2)}) %collective-permute-start.7) | collective-permute-done | bytes 491552 | tf_op jit(solution)/shard_map/a1/ppermute | solution.py:49
  48.5 3.1 %collective-permute-start.9 = (bf16[320,768]{1,0:T(8,128)(2,1)}, bf16[320,768]{1,0:T(8,128)(2,1)}, u32[]{:S(2)}, u32[]{:S(2)}) collective-permute-start(bf16[320,768]{1,0:T(8,128)(2,1)} %shard_map.76.refs_1_.refs_2_), channel_id=1, source_target_pairs={{0,2},{1,15},{2,4},{3,1},{4,6},{5,3},{6,8},{7,5},{8,10},{9,7},{10,... | collective-permute-start | bytes 1474568 | tf_op jit(solution)/shard_map/a2/ppermute | solution.py:49
  51.7 4.9 %collective-permute-done.11.refs_0_ = bf16[320,768]{1,0:T(8,128)(2,1)S(1)} collective-permute-done((bf16[320,768]{1,0:T(8,128)(2,1)}, bf16[320,768]{1,0:T(8,128)(2,1)S(1)}, u32[]{:S(2)}, u32[]{:S(2)}) %collective-permute-start.11) | collective-permute-done | bytes 491552 | tf_op jit(solution)/shard_map/part_b/ppermute | solution.py:49
  56.5 1.4 %collective-permute-start.24 = (bf16[320,768]{1,0:T(8,128)(2,1)}, bf16[320,768]{1,0:T(8,128)(2,1)}, u32[]{:S(2)}, u32[]{:S(2)}) collective-permute-start(bf16[320,768]{1,0:T(8,128)(2,1)} %shard_map.76.refs_1_.refs_2_), channel_id=1, source_target_pairs={{0,16},{1,17},{2,18},{3,19},{4,20},{5,21},{6,22},{7,23},{8,24},{9,... | collective-permute-start | bytes 1474568 | tf_op jit(solution)/shard_map/side1/ppermute | solution.py:49
  59.1 3.1 %collective-permute-start.13 = (bf16[320,768]{1,0:T(8,128)(2,1)S(1)}, bf16[320,768]{1,0:T(8,128)(2,1)S(1)}, u32[]{:S(2)}, u32[]{:S(2)}) collective-permute-start(bf16[320,768]{1,0:T(8,128)(2,1)S(1)} %shard_map.78.refs_1_.refs_3_), channel_id=1, source_target_pairs={{0,2},{1,15},{2,4},{3,1},{4,6},{5,3},{6,8},{7,5},{8,10},{9,7},{10,... | collective-permute-start | bytes 1474568 | tf_op jit(solution)/shard_map/b2/ppermute | solution.py:49
  62.2 3.8 %collective-permute-done.16.refs_0_ = bf16[320,768]{1,0:T(8,128)(2,1)S(1)} collective-permute-done((bf16[320,768]{1,0:T(8,128)(2,1)S(1)}, bf16[320,768]{1,0:T(8,128)(2,1)S(1)}, u32[]{:S(2)}, u32[]{:S(2)}) %collective-permute-start.16) | collective-permute-done | bytes 491552 | tf_op jit(solution)/shard_map/part_b1/ppermute | solution.py:49
  66.0 1.5 %collective-permute-start.12 = (bf16[320,768]{1,0:T(8,128)(2,1)}, bf16[320,768]{1,0:T(8,128)(2,1)S(1)}, u32[]{:S(2)}, u32[]{:S(2)}) collective-permute-start(bf16[320,768]{1,0:T(8,128)(2,1)} %shard_map.79.refs_1_.refs_2_), channel_id=1, source_target_pairs={{0,2},{1,15},{2,4},{3,1},{4,6},{5,3},{6,8},{7,5},{8,10},{9,7},{10,... | collective-permute-start | bytes 1474568 | tf_op jit(solution)/shard_map/a3/ppermute | solution.py:49
  67.5 1.2 collective-permute-start.22
  68.8 5.5 %shard_map.80 = (f32[256,768]{1,0:T(8,128)}, f32[256,768]{1,0:T(8,128)}) custom-call(s32[10]{0:T(128)} %stack.43.where_ref, bf16[256,10240]{1,0:T(8,128)(2,1)} %bitcast.30, bf16[256,10240]{1,0:T(8,128)(2,1)} %collective-permute-done.14.refs_1_, bf16[320,768]{1,0:T(8,128)(2,1)} %shard_map.76.refs_1_.refs_2_, bf16[320,768]{1,0:T(8,128)(2,1)} %copy-done.9, ...), custom_call_target="tpu_custom_call" | custom-call | flops 30000001024 | bytes 4849664 | tf_op jit(solution)/shard_map/pallas_call | solution.py:199
  74.3 1.1 copy-done.16
  75.4 1.1 copy-done.18
  76.6 0.9 copy-done.17
  77.5 0.9 copy-done.19
  79.1 2.6 %collective-permute-done.23.refs_0_ = bf16[320,768]{1,0:T(8,128)(2,1)S(1)} collective-permute-done((bf16[320,768]{1,0:T(8,128)(2,1)S(1)}, bf16[320,768]{1,0:T(8,128)(2,1)S(1)}, u32[]{:S(2)}, u32[]{:S(2)}) %collective-permute-start.23) | collective-permute-done | bytes 491552 | tf_op jit(solution)/shard_map/part_b2/ppermute | solution.py:49
  82.2 0.9 collective-permute-start.19
  83.1 1.6 %collective-permute-start.27 = (bf16[320,768]{1,0:T(8,128)(2,1)S(1)}, bf16[320,768]{1,0:T(8,128)(2,1)S(1)}, u32[]{:S(2)}, u32[]{:S(2)}) collective-permute-start(bf16[320,768]{1,0:T(8,128)(2,1)S(1)} %shard_map.85.refs_5_.refs_3_), channel_id=1, source_target_pairs={{0,2},{1,15},{2,4},{3,1},{4,6},{5,3},{6,8},{7,5},{8,10},{9,7},{10,... | collective-permute-start | bytes 1474568 | tf_op jit(solution)/shard_map/part_b3/ppermute | solution.py:49
  84.7 7.2 %shard_map.86 = (f32[256,768]{1,0:T(8,128)}, f32[256,768]{1,0:T(8,128)}) custom-call(s32[10]{0:T(128)} %stack.43.where_ref, bf16[256,10240]{1,0:T(8,128)(2,1)} %bitcast.31, bf16[256,10240]{1,0:T(8,128)(2,1)} %collective-permute-done.14.refs_1_, bf16[320,768]{1,0:T(8,128)(2,1)} %shard_map.79.refs_1_.refs_2_, bf16[320,768]{1,0:T(8,128)(2,1)} %copy-done.7, ...), custom_call_target="tpu_custom_call" | custom-call | flops 30000001024 | bytes 6488064 | tf_op jit(solution)/shard_map/pallas_call | solution.py:199
  92.1 1.0 copy-done.6
  93.1 1.1 copy-done.12
  94.2 1.1 copy-done.14
  95.4 1.0 copy-done.13
  97.1 1.2 collective-permute-start.29
  100.0 1.6 %fusion.1 = (bf16[320,768]{1,0:T(8,128)(2,1)S(1)}, f32[320,768]{1,0:T(8,128)}, f32[320,768]{1,0:T(8,128)}) fusion(bf16[1,320,768]{2,1,0:T(8,128)(2,1)S(1)} %copy-done.20, f32[320,768]{1,0:T(8,128)S(1)} %copy-done.21, f32[80,768]{1,0:T(8,128)S(1)} %get-tuple-element.47, f32[80,768]{1,0:T(8,128)S(1)} %get-tuple-element.48, f32[80,768]{1,0:T(8,128)S(1)} %get-tuple-element.49, ...), kind=kLoop, calls=%fused_computation.3 | loop fusion | flops 3194880 | bytes 5898240 | tf_op jit(solution)/shard_map/convert_element_type | solution.py:255
  102.4 1.3 collective-permute-start.28
  104.0 1.1 collective-permute-done.29.refs_4_
  105.9 5.8 %shard_map.91 = (f32[256,768]{1,0:T(8,128)}, f32[256,768]{1,0:T(8,128)}) custom-call(s32[10]{0:T(128)} %stack.43.where_ref, bf16[256,10240]{1,0:T(8,128)(2,1)} %bitcast.32, bf16[256,10240]{1,0:T(8,128)(2,1)} %collective-permute-done.14.refs_1_, bf16[320,768]{1,0:T(8,128)(2,1)} %copy-done.2, bf16[320,768]{1,0:T(8,128)(2,1)} %copy-done.1, ...), custom_call_target="tpu_custom_call" | custom-call | flops 30000001024 | bytes 4849664 | tf_op jit(solution)/shard_map/pallas_call | solution.py:199
  112.6 5.6 %shard_map.92 = (f32[256,768]{1,0:T(8,128)}, bf16[256,768]{1,0:T(8,128)(2,1)}) custom-call(s32[10]{0:T(128)} %stack.43.where_ref, bf16[256,10240]{1,0:T(8,128)(2,1)} %bitcast.33, bf16[256,10240]{1,0:T(8,128)(2,1)} %collective-permute-done.14.refs_1_, bf16[160,768]{1,0:T(8,128)(2,1)} %copy-done.11, bf16[160,768]{1,0:T(8,128)(2,1)} %copy-done.25, ...), custom_call_target="tpu_custom_call" | custom-call | flops 30000001024 | bytes 4849664 | tf_op jit(solution)/shard_map/pallas_call | solution.py:199
  118.2 8.3 %collective-permute-start.30 = (bf16[256,768]{1,0:T(8,128)(2,1)}, bf16[256,768]{1,0:T(8,128)(2,1)S(1)}, u32[]{:S(2)}, u32[]{:S(2)}) collective-permute-start(bf16[256,768]{1,0:T(8,128)(2,1)} %get-tuple-element.37), channel_id=1, source_target_pairs={{0,1},{1,0},{2,3},{3,2},{4,5},{5,4},{6,7},{7,6},{8,9},{9,8},{10,11... | collective-permute-start | bytes 1179656 | tf_op jit(solution)/shard_map/late/ppermute | solution.py:49
  126.5 1.6 %collective-permute-done.30 = bf16[256,768]{1,0:T(8,128)(2,1)S(1)} collective-permute-done((bf16[256,768]{1,0:T(8,128)(2,1)}, bf16[256,768]{1,0:T(8,128)(2,1)S(1)}, u32[]{:S(2)}, u32[]{:S(2)}) %collective-permute-start.30) | collective-permute-done | bytes 393248 | tf_op jit(solution)/shard_map/late/ppermute | solution.py:49
  128.1 2.0 %fusion.2 = bf16[1,256,768]{2,1,0:T(8,128)(2,1)} fusion(f32[256,768]{1,0:T(8,128)} %get-tuple-element.36, bf16[256,768]{1,0:T(8,128)(2,1)S(1)} %collective-permute-done.30), kind=kLoop, calls=%fused_computation.8 | loop fusion | flops 786432 | bytes 1572864 | tf_op jit(solution)/shard_map/broadcast_in_dim | solution.py:339
  (98 shorter events, 10.2 us)
Async XLA Ops:
  1.8 5.7 %collective-permute-start = (bf16[80,768]{1,0:T(8,128)(2,1)S(1)}, bf16[80,768]{1,0:T(8,128)(2,1)S(1)}, u32[]{:S(2)}, u32[]{:S(2)}) collective-permute-start(bf16[80,768]{1,0:T(8,128)(2,1)S(1)} %get-tuple-element.54), channel_id=1, source_target_pairs={{0,64},{32,96},{64,128},{96,160},{128,192},{160,224},{192,0},{224,... | collective-permute-start | bytes 368648 | tf_op jit(solution)/shard_map/quarters/ppermute | solution.py:38
  3.9 7.8 %collective-permute-start.1 = (bf16[80,768]{1,0:T(8,128)(2,1)S(1)}, bf16[80,768]{1,0:T(8,128)(2,1)S(1)}, u32[]{:S(2)}, u32[]{:S(2)}) collective-permute-start(bf16[80,768]{1,0:T(8,128)(2,1)S(1)} %get-tuple-element.53), channel_id=1, source_target_pairs={{0,128},{32,160},{64,192},{96,224},{128,0},{160,32},{192,64},{224,... | collective-permute-start | bytes 368648 | tf_op jit(solution)/shard_map/quarters/ppermute | solution.py:38
  6.3 5.4 %collective-permute-start.2 = (bf16[80,768]{1,0:T(8,128)(2,1)S(1)}, bf16[80,768]{1,0:T(8,128)(2,1)S(1)}, u32[]{:S(2)}, u32[]{:S(2)}) collective-permute-start(bf16[80,768]{1,0:T(8,128)(2,1)S(1)} %get-tuple-element.55), channel_id=1, source_target_pairs={{0,192},{32,224},{64,0},{96,32},{128,64},{160,96},{192,128},{224,1... | collective-permute-start | bytes 368648 | tf_op jit(solution)/shard_map/quarters/ppermute | solution.py:38
  12.8 7.1 %collective-permute-start.3 = (f32[80,768]{1,0:T(8,128)S(1)}, f32[80,768]{1,0:T(8,128)S(1)}, u32[]{:S(2)}, u32[]{:S(2)}) collective-permute-start(f32[80,768]{1,0:T(8,128)S(1)} %fusion.5), channel_id=1, source_target_pairs={{0,32},{32,0},{64,96},{96,64},{128,160},{160,128},{192,224},{224,1... | collective-permute-start | bytes 737288 | tf_op jit(solution)/shard_map/four/ppermute | solution.py:38
  21.2 5.5 %collective-permute-start.4 = (bf16[80,768]{1,0:T(8,128)(2,1)S(1)}, bf16[80,768]{1,0:T(8,128)(2,1)S(1)}, u32[]{:S(2)}, u32[]{:S(2)}) collective-permute-start(bf16[80,768]{1,0:T(8,128)(2,1)S(1)} %get-tuple-element.57), channel_id=1, source_target_pairs={{0,192},{32,224},{64,0},{96,32},{128,64},{160,96},{192,128},{224,1... | collective-permute-start | bytes 368648 | tf_op jit(solution)/shard_map/home/ppermute | solution.py:38
  23.6 5.3 %collective-permute-start.5 = (bf16[80,768]{1,0:T(8,128)(2,1)S(1)}, bf16[80,768]{1,0:T(8,128)(2,1)S(1)}, u32[]{:S(2)}, u32[]{:S(2)}) collective-permute-start(bf16[80,768]{1,0:T(8,128)(2,1)S(1)} %get-tuple-element.56), channel_id=1, source_target_pairs={{0,128},{32,160},{64,192},{96,224},{128,0},{160,32},{192,64},{224,... | collective-permute-start | bytes 368648 | tf_op jit(solution)/shard_map/home/ppermute | solution.py:38
  24.1 6.0 %collective-permute-start.6 = (bf16[80,768]{1,0:T(8,128)(2,1)S(1)}, bf16[80,768]{1,0:T(8,128)(2,1)S(1)}, u32[]{:S(2)}, u32[]{:S(2)}) collective-permute-start(bf16[80,768]{1,0:T(8,128)(2,1)S(1)} %get-tuple-element.43), channel_id=1, source_target_pairs={{0,64},{32,96},{64,128},{96,160},{128,192},{160,224},{192,0},{224,... | collective-permute-start | bytes 368648 | tf_op jit(solution)/shard_map/home/ppermute | solution.py:38
  32.0 13.7 %collective-permute-start.8 = (bf16[320,768]{1,0:T(8,128)(2,1)}, bf16[320,768]{1,0:T(8,128)(2,1)S(1)}, u32[]{:S(2)}, u32[]{:S(2)}) collective-permute-start(bf16[320,768]{1,0:T(8,128)(2,1)} %pad_maximum_fusion.1.refs_4_), channel_id=1, source_target_pairs={{0,1},{1,0},{2,3},{3,2},{4,5},{5,4},{6,7},{7,6},{8,9},{9,8},{10,11... | collective-permute-start | bytes 1474568 | tf_op jit(solution)/shard_map/b/ppermute | solution.py:49
  36.2 32.5 %collective-permute-start.14 = (bf16[256,10240]{1,0:T(8,128)(2,1)}, bf16[256,10240]{1,0:T(8,128)(2,1)}, u32[]{:S(2)}, u32[]{:S(2)}) collective-permute-start(bf16[256,10240]{1,0:T(8,128)(2,1)} %bitcast.29), channel_id=1, source_target_pairs={{0,1},{1,0},{2,3},{3,2},{4,5},{5,4},{6,7},{7,6},{8,9},{9,8},{10,11... | collective-permute-start | bytes 15728648 | tf_op jit(solution)/shard_map/other/ppermute | solution.py:49
  36.8 11.7 %collective-permute-start.7 = (bf16[320,768]{1,0:T(8,128)(2,1)}, bf16[320,768]{1,0:T(8,128)(2,1)}, u32[]{:S(2)}, u32[]{:S(2)}) collective-permute-start(bf16[320,768]{1,0:T(8,128)(2,1)} %pad_maximum_fusion.1.refs_4_), channel_id=1, source_target_pairs={{0,2},{1,15},{2,4},{3,1},{4,6},{5,3},{6,8},{7,5},{8,10},{9,7},{10,... | collective-permute-start | bytes 1474568 | tf_op jit(solution)/shard_map/a1/ppermute | solution.py:49
  42.5 14.1 %collective-permute-start.11 = (bf16[320,768]{1,0:T(8,128)(2,1)}, bf16[320,768]{1,0:T(8,128)(2,1)S(1)}, u32[]{:S(2)}, u32[]{:S(2)}) collective-permute-start(bf16[320,768]{1,0:T(8,128)(2,1)} %pad_maximum_fusion.1.refs_4_), channel_id=1, source_target_pairs={{0,17},{1,16},{2,19},{3,18},{4,21},{5,20},{6,23},{7,22},{8,25},{9,... | collective-permute-start | bytes 1474568 | tf_op jit(solution)/shard_map/part_b/ppermute | solution.py:49
  42.5 25.0 %collective-permute-start.15 = (bf16[320,768]{1,0:T(8,128)(2,1)}, bf16[320,768]{1,0:T(8,128)(2,1)}, u32[]{:S(2)}, u32[]{:S(2)}) collective-permute-start(bf16[320,768]{1,0:T(8,128)(2,1)} %pad_maximum_fusion.1.refs_4_), channel_id=1, source_target_pairs={{1,17},{3,19},{5,21},{7,23},{9,25},{11,27},{13,29},{15,31},{17,1},... | collective-permute-start | bytes 1474568 | tf_op jit(solution)/shard_map/side/ppermute | solution.py:49
  45.7 2.9 %copy-start.4 = (bf16[320,768]{1,0:T(8,128)(2,1)}, bf16[320,768]{1,0:T(8,128)(2,1)S(1)}, u32[]{:S(2)}) copy-start(bf16[320,768]{1,0:T(8,128)(2,1)S(1)} %shard_map.75.refs_1_.refs_5_) | copy-start | bytes 1474564
  45.7 12.3 %collective-permute-start.10 = (bf16[320,768]{1,0:T(8,128)(2,1)S(1)}, bf16[320,768]{1,0:T(8,128)(2,1)S(1)}, u32[]{:S(2)}, u32[]{:S(2)}) collective-permute-start(bf16[320,768]{1,0:T(8,128)(2,1)S(1)} %shard_map.75.refs_1_.refs_5_), channel_id=1, source_target_pairs={{0,2},{1,15},{2,4},{3,1},{4,6},{5,3},{6,8},{7,5},{8,10},{9,7},{10,... | collective-permute-start | bytes 1474568 | tf_op jit(solution)/shard_map/b1/ppermute | solution.py:49
  48.5 10.6 %collective-permute-start.9 = (bf16[320,768]{1,0:T(8,128)(2,1)}, bf16[320,768]{1,0:T(8,128)(2,1)}, u32[]{:S(2)}, u32[]{:S(2)}) collective-permute-start(bf16[320,768]{1,0:T(8,128)(2,1)} %shard_map.76.refs_1_.refs_2_), channel_id=1, source_target_pairs={{0,2},{1,15},{2,4},{3,1},{4,6},{5,3},{6,8},{7,5},{8,10},{9,7},{10,... | collective-permute-start | bytes 1474568 | tf_op jit(solution)/shard_map/a2/ppermute | solution.py:49
  56.5 25.7 %collective-permute-start.24 = (bf16[320,768]{1,0:T(8,128)(2,1)}, bf16[320,768]{1,0:T(8,128)(2,1)}, u32[]{:S(2)}, u32[]{:S(2)}) collective-permute-start(bf16[320,768]{1,0:T(8,128)(2,1)} %shard_map.76.refs_1_.refs_2_), channel_id=1, source_target_pairs={{0,16},{1,17},{2,18},{3,19},{4,20},{5,21},{6,22},{7,23},{8,24},{9,... | collective-permute-start | bytes 1474568 | tf_op jit(solution)/shard_map/side1/ppermute | solution.py:49
  58.0 8.1 %collective-permute-start.16 = (bf16[320,768]{1,0:T(8,128)(2,1)S(1)}, bf16[320,768]{1,0:T(8,128)(2,1)S(1)}, u32[]{:S(2)}, u32[]{:S(2)}) collective-permute-start(bf16[320,768]{1,0:T(8,128)(2,1)S(1)} %shard_map.77.refs_1_.refs_6_), channel_id=1, source_target_pairs={{0,2},{1,15},{2,4},{3,1},{4,6},{5,3},{6,8},{7,5},{8,10},{9,7},{10,... | collective-permute-start | bytes 1474568 | tf_op jit(solution)/shard_map/part_b1/ppermute | solution.py:49
  58.7 3.5 %copy-start.9 = (bf16[320,768]{1,0:T(8,128)(2,1)}, bf16[320,768]{1,0:T(8,128)(2,1)S(1)}, u32[]{:S(2)}) copy-start(bf16[320,768]{1,0:T(8,128)(2,1)S(1)} %shard_map.78.refs_1_.refs_3_) | copy-start | bytes 1474564
  59.1 15.2 %collective-permute-start.13 = (bf16[320,768]{1,0:T(8,128)(2,1)S(1)}, bf16[320,768]{1,0:T(8,128)(2,1)S(1)}, u32[]{:S(2)}, u32[]{:S(2)}) collective-permute-start(bf16[320,768]{1,0:T(8,128)(2,1)S(1)} %shard_map.78.refs_1_.refs_3_), channel_id=1, source_target_pairs={{0,2},{1,15},{2,4},{3,1},{4,6},{5,3},{6,8},{7,5},{8,10},{9,7},{10,... | collective-permute-start | bytes 1474568 | tf_op jit(solution)/shard_map/b2/ppermute | solution.py:49
  66.0 12.9 %collective-permute-start.12 = (bf16[320,768]{1,0:T(8,128)(2,1)}, bf16[320,768]{1,0:T(8,128)(2,1)S(1)}, u32[]{:S(2)}, u32[]{:S(2)}) collective-permute-start(bf16[320,768]{1,0:T(8,128)(2,1)} %shard_map.79.refs_1_.refs_2_), channel_id=1, source_target_pairs={{0,2},{1,15},{2,4},{3,1},{4,6},{5,3},{6,8},{7,5},{8,10},{9,7},{10,... | collective-permute-start | bytes 1474568 | tf_op jit(solution)/shard_map/a3/ppermute | solution.py:49
  67.5 6.8 %copy-start.10 = (bf16[320,768]{1,0:T(8,128)(2,1)}, bf16[320,768]{1,0:T(8,128)(2,1)S(1)}, u32[]{:S(2)}) copy-start(bf16[320,768]{1,0:T(8,128)(2,1)S(1)} %shard_map.81.refs_3_.refs_7_) | copy-start | bytes 1474564
  67.5 15.6 %collective-permute-start.22 = (bf16[320,768]{1,0:T(8,128)(2,1)}, bf16[320,768]{1,0:T(8,128)(2,1)}, u32[]{:S(2)}, u32[]{:S(2)}) collective-permute-start(bf16[320,768]{1,0:T(8,128)(2,1)} %shard_map.79.refs_1_.refs_2_), channel_id=1, source_target_pairs={{0,16},{1,17},{2,18},{3,19},{4,20},{5,21},{6,22},{7,23},{8,24},{9,... | collective-permute-start | bytes 1474568 | tf_op jit(solution)/shard_map/side2/ppermute | solution.py:49
  68.7 13.1 %collective-permute-start.23 = (bf16[320,768]{1,0:T(8,128)(2,1)S(1)}, bf16[320,768]{1,0:T(8,128)(2,1)S(1)}, u32[]{:S(2)}, u32[]{:S(2)}) collective-permute-start(bf16[320,768]{1,0:T(8,128)(2,1)S(1)} %shard_map.81.refs_3_.refs_7_), channel_id=1, source_target_pairs={{0,2},{1,15},{2,4},{3,1},{4,6},{5,3},{6,8},{7,5},{8,10},{9,7},{10,... | collective-permute-start | bytes 1474568 | tf_op jit(solution)/shard_map/part_b2/ppermute | solution.py:49
  74.3 1.1 copy-start.16
  75.4 1.1 copy-start.18
  78.3 13.6 %collective-permute-start.21 = (bf16[320,768]{1,0:T(8,128)(2,1)S(1)}, bf16[320,768]{1,0:T(8,128)(2,1)S(1)}, u32[]{:S(2)}, u32[]{:S(2)}) collective-permute-start(bf16[320,768]{1,0:T(8,128)(2,1)S(1)} %get-tuple-element.23.refs_1_.refs_3_), channel_id=1, source_target_pairs={{0,2},{1,15},{2,4},{3,1},{4,6},{5,3},{6,8},{7,5},{8,10},{9,7},{10,... | collective-permute-start | bytes 1474568 | tf_op jit(solution)/shard_map/b3/ppermute | solution.py:49
  79.1 18.0 %copy-start.2 = (bf16[320,768]{1,0:T(8,128)(2,1)}, bf16[320,768]{1,0:T(8,128)(2,1)S(1)}, u32[]{:S(2)}) copy-start(bf16[320,768]{1,0:T(8,128)(2,1)S(1)} %shard_map.83.refs_1_.refs_2_) | copy-start | bytes 1474564
  79.1 19.2 %collective-permute-start.17 = (f32[80,768]{1,0:T(8,128)S(1)}, f32[80,768]{1,0:T(8,128)S(1)}, u32[]{:S(2)}, u32[]{:S(2)}) collective-permute-start(f32[80,768]{1,0:T(8,128)S(1)} %shard_map.84), channel_id=1, source_target_pairs={{0,64},{32,96},{64,128},{96,160},{128,192},{160,224},{192,0},{224,... | collective-permute-start | bytes 737288 | tf_op jit(solution)/shard_map/gradient/ppermute | solution.py:38
  81.7 17.0 %collective-permute-start.18 = (f32[80,768]{1,0:T(8,128)S(1)}, f32[80,768]{1,0:T(8,128)S(1)}, u32[]{:S(2)}, u32[]{:S(2)}) collective-permute-start(f32[80,768]{1,0:T(8,128)S(1)} %shard_map.84), channel_id=1, source_target_pairs={{0,128},{32,160},{64,192},{96,224},{128,0},{160,32},{192,64},{224,... | collective-permute-start | bytes 737288 | tf_op jit(solution)/shard_map/gradient/ppermute | solution.py:38
  82.2 2.5 %copy-start.5 = (bf16[320,768]{1,0:T(8,128)(2,1)}, bf16[320,768]{1,0:T(8,128)(2,1)S(1)}, u32[]{:S(2)}) copy-start(bf16[320,768]{1,0:T(8,128)(2,1)S(1)} %shard_map.85.refs_5_.refs_3_) | copy-start | bytes 1474564
  82.2 16.4 %collective-permute-start.19 = (f32[80,768]{1,0:T(8,128)S(1)}, f32[80,768]{1,0:T(8,128)S(1)}, u32[]{:S(2)}, u32[]{:S(2)}) collective-permute-start(f32[80,768]{1,0:T(8,128)S(1)} %shard_map.84), channel_id=1, source_target_pairs={{0,192},{32,224},{64,0},{96,32},{128,64},{160,96},{192,128},{224,1... | collective-permute-start | bytes 737288 | tf_op jit(solution)/shard_map/gradient/ppermute | solution.py:38
  83.1 18.4 %collective-permute-start.27 = (bf16[320,768]{1,0:T(8,128)(2,1)S(1)}, bf16[320,768]{1,0:T(8,128)(2,1)S(1)}, u32[]{:S(2)}, u32[]{:S(2)}) collective-permute-start(bf16[320,768]{1,0:T(8,128)(2,1)S(1)} %shard_map.85.refs_5_.refs_3_), channel_id=1, source_target_pairs={{0,2},{1,15},{2,4},{3,1},{4,6},{5,3},{6,8},{7,5},{8,10},{9,7},{10,... | collective-permute-start | bytes 1474568 | tf_op jit(solution)/shard_map/part_b3/ppermute | solution.py:49
  92.0 5.1 %collective-permute-start.20 = (bf16[160,768]{1,0:T(8,128)(2,1)S(1)}, bf16[160,768]{1,0:T(8,128)(2,1)S(1)}, u32[]{:S(2)}, u32[]{:S(2)}) collective-permute-start(bf16[160,768]{1,0:T(8,128)(2,1)S(1)} %slice_select_fusion.1), channel_id=1, source_target_pairs={{0,2},{1,15},{2,4},{3,1},{4,6},{5,3},{6,8},{7,5},{8,10},{9,7},{10,... | collective-permute-start | bytes 737288 | tf_op jit(solution)/shard_map/a4/ppermute | solution.py:49
  92.1 1.0 copy-start.6
  93.1 1.1 copy-start.12
  94.2 1.1 copy-start.14
  95.4 1.0 copy-start.13
  96.3 2.0 %copy-start.15 = (f32[256,768]{1,0:T(8,128)}, f32[256,768]{1,0:T(8,128)S(1)}, u32[]{:S(2)}) copy-start(f32[256,768]{1,0:T(8,128)S(1)} %get-tuple-element.33.refs_7_) | copy-start | bytes 2359300
  96.3 7.4 %copy-start.1 = (bf16[320,768]{1,0:T(8,128)(2,1)}, bf16[320,768]{1,0:T(8,128)(2,1)S(1)}, u32[]{:S(2)}) copy-start(bf16[320,768]{1,0:T(8,128)(2,1)S(1)} %get-tuple-element.28.refs_1_.refs_3_) | copy-start | bytes 1474564
  97.1 8.0 %collective-permute-start.29 = (bf16[320,768]{1,0:T(8,128)(2,1)S(1)}, bf16[320,768]{1,0:T(8,128)(2,1)S(1)}, u32[]{:S(2)}, u32[]{:S(2)}) collective-permute-start(bf16[320,768]{1,0:T(8,128)(2,1)S(1)} %shard_map.83.refs_1_.refs_2_), channel_id=1, source_target_pairs={{0,16},{1,17},{2,18},{3,19},{4,20},{5,21},{6,22},{7,23},{8,24},{9,... | collective-permute-start | bytes 1474568 | tf_op jit(solution)/shard_map/side3/ppermute | solution.py:49
  98.3 1.1 copy-start.20
  98.3 1.4 %copy-start.21 = (f32[320,768]{1,0:T(8,128)S(1)}, f32[320,768]{1,0:T(8,128)}, u32[]{:S(2)}) copy-start(f32[320,768]{1,0:T(8,128)} %param.4) | copy-start | bytes 2949124
  98.3 1.7 %copy-start.22 = (f32[320,768]{1,0:T(8,128)S(1)}, f32[320,768]{1,0:T(8,128)}, u32[]{:S(2)}) copy-start(f32[320,768]{1,0:T(8,128)} %param.5) | copy-start | bytes 2949124
  98.3 13.5 %collective-permute-start.26 = (bf16[160,768]{1,0:T(8,128)(2,1)S(1)}, bf16[160,768]{1,0:T(8,128)(2,1)}, u32[]{:S(2)}, u32[]{:S(2)}) collective-permute-start(bf16[160,768]{1,0:T(8,128)(2,1)S(1)} %shard_map.88.refs_3_.refs_2_), channel_id=1, source_target_pairs={{0,16},{1,17},{2,18},{3,19},{4,20},{5,21},{6,22},{7,23},{8,24},{9,... | collective-permute-start | bytes 737288 | tf_op jit(solution)/shard_map/far_side/ppermute | solution.py:49
  102.4 2.8 %copy-start = (bf16[320,768]{1,0:T(8,128)(2,1)}, bf16[320,768]{1,0:T(8,128)(2,1)S(1)}, u32[]{:S(2)}) copy-start(bf16[320,768]{1,0:T(8,128)(2,1)S(1)} %shard_map.90.refs_5_) | copy-start | bytes 1474564
  102.4 9.4 %collective-permute-start.28 = (bf16[160,768]{1,0:T(8,128)(2,1)S(1)}, bf16[160,768]{1,0:T(8,128)(2,1)S(1)}, u32[]{:S(2)}, u32[]{:S(2)}) collective-permute-start(bf16[160,768]{1,0:T(8,128)(2,1)S(1)} %slice_select_fusion), channel_id=1, source_target_pairs={{0,2},{1,15},{2,4},{3,1},{4,6},{5,3},{6,8},{7,5},{8,10},{9,7},{10,... | collective-permute-start | bytes 737288 | tf_op jit(solution)/shard_map/part_b4/ppermute | solution.py:49
  103.7 8.1 %collective-permute-start.25 = (bf16[160,768]{1,0:T(8,128)(2,1)S(1)}, bf16[160,768]{1,0:T(8,128)(2,1)S(1)}, u32[]{:S(2)}, u32[]{:S(2)}) collective-permute-start(bf16[160,768]{1,0:T(8,128)(2,1)S(1)} %slice_select_fusion.2), channel_id=1, source_target_pairs={{0,2},{1,15},{2,4},{3,1},{4,6},{5,3},{6,8},{7,5},{8,10},{9,7},{10,... | collective-permute-start | bytes 737288 | tf_op jit(solution)/shard_map/b4/ppermute | solution.py:49
  118.2 9.9 %collective-permute-start.30 = (bf16[256,768]{1,0:T(8,128)(2,1)}, bf16[256,768]{1,0:T(8,128)(2,1)S(1)}, u32[]{:S(2)}, u32[]{:S(2)}) collective-permute-start(bf16[256,768]{1,0:T(8,128)(2,1)} %get-tuple-element.37), channel_id=1, source_target_pairs={{0,1},{1,0},{2,3},{3,2},{4,5},{5,4},{6,7},{7,6},{8,9},{9,8},{10,11... | collective-permute-start | bytes 1179656 | tf_op jit(solution)/shard_map/late/ppermute | solution.py:49
  (9 other events, 7.1 us)

commit v3 on v2

v3 whole, which is shorter than its diff:
```python
import functools
import math

import jax
import jax.numpy as jnp
from jax import lax
from jax.experimental import pallas as pl
from jax.experimental.pallas import tpu as pltpu
from jax.sharding import PartitionSpec as P

D = 10240
COLS = 768
REPS = 8
OUTER_RATE = 0.7
MOMENT_DECAY = 0.9
KEEP_LOCAL = 0.5
SCALE = 1.0 / math.sqrt(D)

NX, NYH, NYL, NZ, NC = 4, 2, 2, 8, 2
ROWS = D // (NYL * NZ * NC)
CHIP = ROWS * NC
SLICE = ROWS // NX
FAR = ROWS // 2
BIG = 24 * 1024 * 1024
LONG = 30_000_000_000
CHUNKS = 1
WIDTH = COLS // CHUNKS


def rep_perm(dx, dy):
    return [
        (x * NYH + y, ((x + dx) % NX) * NYH + (y ^ dy)) for x in range(NX) for y in range(NYH)
    ]


def send_rep(v, dx, dy, name):
    with jax.named_scope(name):
        return lax.ppermute(v, "rep", rep_perm(dx, dy))


def send(v, to, name, cores=(0, 1)):
    perm = []
    for y in range(NYL):
        for z in range(NZ):
            for c in cores:
                ty, tz, tc = to(y, z, c)
                perm.append(((y * NZ + z) * NC + c, (ty * NZ + tz % NZ) * NC + tc))
    with jax.named_scope(name):
        return lax.ppermute(v, "fsdp", perm)


def to_core(y, z, c):
    return y, z, 1 - c


def to_side(y, z, c):
    return 1 - y, z, c


def to_cross(y, z, c):
    return 1 - y, z, 1 - c


def to_ring(y, z, c):
    return y, (z - 1 if c else z + 1), c


def fence_kernel(*refs):
    del refs


def fence(values, *earlier):
    anywhere = pl.BlockSpec(memory_space=pl.ANY)
    operands = tuple(values) + earlier
    return pl.pallas_call(
        fence_kernel,
        out_shape=[jax.ShapeDtypeStruct(v.shape, v.dtype) for v in values],
        in_specs=[anywhere] * len(operands),
        out_specs=[anywhere] * len(values),
        input_output_aliases={i: i for i in range(len(values))},
        compiler_params=pltpu.CompilerParams(vmem_limit_bytes=1024 * 1024),
        cost_estimate=pl.CostEstimate(flops=LONG, bytes_accessed=4096, transcendentals=0),
    )(*operands)


def in_order_kernel(*refs):
    slices, out, sems = refs[:NX], refs[NX], refs[NX + 1]
    x = lax.axis_index("rep") // NYH
    started = []
    for k, ref in enumerate(slices):
        at = ((x + NX - k) % NX) * SLICE
        copy = pltpu.make_async_copy(
            ref, out.at[pl.ds(pl.multiple_of(at, 16), SLICE)], sems.at[k]
        )
        copy.start()
        started.append(copy)
    for copy in started:
        copy.wait()


def in_order(slices):
    anywhere = pl.BlockSpec(memory_space=pl.ANY)
    return pl.pallas_call(
        in_order_kernel,
        out_shape=jax.ShapeDtypeStruct((ROWS, COLS), slices[0].dtype),
        in_specs=[anywhere] * NX,
        out_specs=anywhere,
        scratch_shapes=[pltpu.SemaphoreType.DMA((NX,))],
        compiler_params=pltpu.CompilerParams(vmem_limit_bytes=1024 * 1024),
        cost_estimate=pl.CostEstimate(
            flops=0, bytes_accessed=4 * ROWS * COLS, transcendentals=0
        ),
    )(*slices)


def either(core, first, second):
    return jnp.where(core == 0, first, second)


def stack(*rows):
    return jnp.concatenate(rows, axis=0)


HERE = pl.BlockSpec(memory_space=pl.ANY)
WHOLE = pl.BlockSpec(memory_space=pltpu.VMEM)

A_ROWS, B_ROWS = (0, ROWS), (ROWS, 0)
A_NEAR, A_REST = (0, ROWS + FAR), (FAR, ROWS)
B_NEAR, B_REST = (ROWS, FAR), (ROWS + FAR, 0)


def product_kernel(slots, parts, empty, totals, counts, *refs):
    me = lax.axis_index("fsdp")
    core, z, y = me % NC, (me // NC) % NZ, me // (NC * NZ)
    split = [0]
    for count in counts:
        split.append(split[-1] + count)
    tokens, arrays, before, _, outs = (refs[i:j] for i, j in zip(split, split[1:]))
    mark, tok, weight, total, sems = refs[split[-1] :]
    mark[...] = jnp.zeros(mark.shape, mark.dtype)
    rows = tokens[0].shape[0]
    started = []

    def start(source, target):
        copy = pltpu.make_async_copy(source, target, sems.at[len(started)])
        copy.start()
        started.append(copy)

    def spot(slot, place, size):
        at = slot * CHIP + either(core, place[0], place[1])
        return pl.ds(pl.multiple_of(at, 16), size)

    for s, slot in enumerate(slots):
        flip, d = slot
        shard = (1 - y if flip else y) * NZ + (z + either(core, NZ - d, d)) % NZ
        span = pl.ds(pl.multiple_of(shard * CHIP, 128), CHIP)
        for i, ref in enumerate(tokens):
            start(ref.at[:, span], tok.at[pl.ds(i * rows, rows), pl.ds(s * CHIP, CHIP)])
    ends = []
    for n in range(CHUNKS):
        cols = pl.ds(n * WIDTH, WIDTH)
        for array, first, size, slot, place in parts:
            start(
                arrays[array].at[pl.ds(first, size), cols],
                weight.at[n, spot(slot, place, size)],
            )
        for i, ref in enumerate(before):
            start(ref.at[:, cols], total.at[n, pl.ds(i * rows, rows)])
        ends.append(len(started))
    for n in range(CHUNKS):
        for slot, place, size in empty:
            weight[n, spot(slot, place, size), :] = jnp.zeros((size, WIDTH), jnp.bfloat16)
    done = 0
    for n in range(CHUNKS):
        for copy in started[done : ends[n]]:
            copy.wait()
        done = ends[n]
        value = jnp.dot(tok[...], weight[n], preferred_element_type=jnp.float32)
        if totals:
            value = value + total[n]
        for i, out in enumerate(outs):
            out[:, n * WIDTH : (n + 1) * WIDTH] = value[i * rows : (i + 1) * rows].astype(out.dtype)


def product_step(slots, tokens, arrays, parts, empty, totals, earlier=(), final=False):
    rows, outs, depth = tokens[0].shape[0], len(tokens), len(slots) * CHIP
    kinds = (jnp.float32, jnp.bfloat16 if final else jnp.float32)
    operands = tuple(tokens) + tuple(arrays) + tuple(totals) + tuple(earlier)
    counts = (outs, len(arrays), len(totals), len(earlier), outs)
    copies = len(slots) * outs + CHUNKS * (len(parts) + len(totals))
    return pl.pallas_call(
        functools.partial(product_kernel, slots, parts, empty, bool(totals), counts),
        out_shape=[jax.ShapeDtypeStruct((rows, COLS), k) for k in kinds]
        + [jax.ShapeDtypeStruct((8, 128), jnp.float32)],
        in_specs=[HERE] * len(operands),
        out_specs=[WHOLE] * (outs + 1),
        scratch_shapes=[
            pltpu.VMEM((outs * rows, depth), jnp.bfloat16),
            pltpu.VMEM((CHUNKS, depth, WIDTH), jnp.bfloat16),
            pltpu.VMEM((CHUNKS, outs * rows, WIDTH), jnp.float32),
            pltpu.SemaphoreType.DMA((copies,)),
        ],
        compiler_params=pltpu.CompilerParams(vmem_limit_bytes=BIG),
        cost_estimate=pl.CostEstimate(
            flops=LONG,
            bytes_accessed=depth * (2 * outs * rows + 2 * COLS) + 8 * rows * COLS,
            transcendentals=0,
        ),
    )(*operands)


def update(global_rows, moment_rows, gradient):
    new_moment = MOMENT_DECAY * moment_rows + gradient
    return global_rows - OUTER_RATE * (gradient + MOMENT_DECAY * new_moment), new_moment


def blend(local_rows, new_rows):
    return (
        KEEP_LOCAL * local_rows.astype(jnp.float32) + (1.0 - KEEP_LOCAL) * new_rows
    ).astype(jnp.bfloat16)


def blend_kernel(one, two, global_ref, moment_ref, *refs):
    raw, homes, gradient_ref = refs[:NX], refs[NX : 2 * NX], refs[2 * NX]
    gradient = (one[...] + two[...]) / REPS
    gradient_ref[...] = gradient
    new_part, _ = update(global_ref[...], moment_ref[...], gradient)
    for local_ref, home in zip(raw, homes):
        home[...] = blend(local_ref[...], new_part)


def local_call(kernel, kinds, *operands):
    whole = pl.BlockSpec(memory_space=pltpu.VMEM)
    return pl.pallas_call(
        kernel,
        out_shape=[jax.ShapeDtypeStruct((SLICE, COLS), kind) for kind in kinds],
        in_specs=[whole] * len(operands),
        out_specs=[whole] * len(kinds),
        compiler_params=pltpu.CompilerParams(vmem_limit_bytes=8 * 1024 * 1024),
    )(*operands)


def on_device(global_w, momentum, local_w, tokens):
    local = local_w[0]
    core = lax.axis_index("fsdp") % NC

    x = lax.axis_index("rep") // NYH

    def quarter(v, place):
        return lax.dynamic_slice(v, (place * SLICE, 0), (SLICE, COLS))

    raw = [quarter(local, x)] + [
        send_rep(quarter(local, (x + k) % NX), k, 0, "quarters") for k in range(1, NX)
    ]
    global_part, moment_part = quarter(global_w, x), quarter(momentum, x)
    four = sum(global_part - r.astype(jnp.float32) for r in raw)
    four, global_part, moment_part, raw[0] = lax.optimization_barrier(
        (four, global_part, moment_part, raw[0])
    )
    other_four = send_rep(four, 0, 1, "four")
    mine = tokens[0]
    other = send(mine, to_core, "other")
    *home, gradient = local_call(
        blend_kernel, [jnp.bfloat16] * NX + [jnp.float32],
        four, other_four, global_part, moment_part, *raw,
    )
    back = [home[0]] + [send_rep(home[NX - k], k, 0, "home") for k in range(1, NX)]
    shard = in_order(back)

    def near_half(v):
        return either(core, v[:FAR], v[FAR:])

    tokens = (mine, other)
    a = shard
    b = send(shard, to_core, "b")
    a1 = send(a, to_ring, "a1")
    part_b = send(shard, to_cross, "part_b")
    (b,) = fence((b,))
    b1 = send(b, to_ring, "b1")
    (a1,) = fence((a1,), b)
    a2 = send(a1, to_ring, "a2")
    side1 = send(a1, to_side, "side1")
    (part_b,) = fence((part_b,), a1)
    part_b1 = send(part_b, to_ring, "part_b1")
    (b1,) = fence((b1,), part_b)
    b2 = send(b1, to_ring, "b2")
    (a2,) = fence((a2,), b1)
    a3 = send(a2, to_ring, "a3")
    side2 = send(a2, to_side, "side2")
    (part_b1,) = fence((part_b1,), a2)
    part_b2 = send(part_b1, to_ring, "part_b2")
    *totals, mark = product_step(
        ((0, 1), (0, 0), (1, 0)), tokens, (a1, b1, a, part_b),
        ((0, 0, ROWS, 0, A_ROWS), (1, 0, ROWS, 0, B_ROWS), (2, 0, ROWS, 1, A_ROWS), (3, 0, ROWS, 2, B_ROWS)),
        ((1, B_ROWS, ROWS), (2, A_ROWS, ROWS)), (),
    )
    (b2,) = fence((b2,), part_b1, mark)
    b3 = send(b2, to_ring, "b3")
    (a3,) = fence((a3,), b2)
    a4 = send(near_half(a3), to_ring, "a4")
    side3 = send(a3, to_side, "side3")
    (gradient,) = fence((gradient,), a3)
    sums = [send_rep(gradient, k, 0, "gradient") for k in range(1, NX)]
    (part_b2,) = fence((part_b2,), a3)
    part_b3 = send(part_b2, to_ring, "part_b3")
    *totals, mark = product_step(
        ((0, 2), (1, 2), (1, 1)), tokens,
        (a2, b2, side2, part_b2, side1, part_b1),
        (
            (0, 0, ROWS, 0, A_ROWS), (1, 0, ROWS, 0, B_ROWS),
            (2, 0, ROWS, 1, A_ROWS), (3, 0, ROWS, 1, B_ROWS),
            (4, 0, ROWS, 2, A_ROWS), (5, 0, ROWS, 2, B_ROWS),
        ),
        (), totals,
    )
    (b3,) = fence((b3,), part_b2, a4, mark)
    b4 = send(near_half(b3), to_ring, "b4")
    far_side = send(a4, to_side, "far_side")
    (part_b3,) = fence((part_b3,), b3, side3)
    part_b4 = send(near_half(part_b3), to_ring, "part_b4")
    *totals, mark = product_step(
        ((0, 3), (1, 3)), tokens, (a3, b3, side3, part_b3),
        (
            (0, 0, ROWS, 0, A_ROWS), (1, 0, ROWS, 0, B_ROWS),
            (2, 0, ROWS, 1, A_ROWS), (3, 0, ROWS, 1, B_ROWS),
        ),
        (), totals,
    )
    total, late, _ = product_step(
        ((0, 4), (1, 4)), tokens, (a4, b4, far_side, part_b4),
        (
            (0, 0, FAR, 0, A_NEAR), (1, 0, FAR, 0, B_NEAR),
            (2, 0, FAR, 1, A_NEAR), (3, 0, FAR, 1, B_NEAR),
        ),
        tuple((s, place, FAR) for s in range(2) for place in (A_REST, B_REST)), totals, final=True,
    )
    late = send(late, to_core, "late")

    new_global, new_moment = update(global_w, momentum, in_order([gradient, *sums]))
    new_local = blend(local, new_global)
    projected = ((total + late.astype(jnp.float32)) * SCALE).astype(jnp.bfloat16)
    return (new_global, new_moment, new_local[None], projected[None])


def solution(mesh):
    return jax.shard_map(
        on_device,
        mesh=mesh,
        in_specs=(P("fsdp", None), P("fsdp", None), P("rep", "fsdp", None), P("rep", "fsdp", None)),
        out_specs=(
            P("fsdp", None),
            P("fsdp", None),
            P("rep", "fsdp", None),
            P("rep", "fsdp", None),
        ),
        check_vma=False,
    )
```

time: 131 us -> 108 us (0.82)
  local copies, waits for them, and re-layouts: 13.9 us -> 2.03 us
  Pallas kernels: 24.1 us -> 15.3 us
  other arithmetic: 7.96 us -> 3.79 us
  waiting for transfers between devices: 31.4 us -> 32.9 us
  starting transfers between devices: 51.7 us -> 53.1 us
    unnamed x52 -> x10, local copies, waits for them, and re-layouts: 12.2 us -> 0.02 us
    pallas_call x4 -> x7, Pallas kernels: 24.1 us -> 15.3 us  [the longest x4 12.7 us: product_step(): pl.pallas_call(functools.partial(product_kernel, slots, parts, empty, boo...]
    ppermute x21 -> x20, waiting for transfers between devices: 17.2 us -> 21.6 us  [send(): return lax.ppermute(v, 'fsdp', perm)]
    ppermute x10, starting transfers between devices: 13.2 us -> 16.4 us  [send_rep(): return lax.ppermute(v, 'rep', rep_perm(dx, dy))]
    ppermute x10, waiting for transfers between devices: 14.2 us -> 11.4 us  [send_rep(): return lax.ppermute(v, 'rep', rep_perm(dx, dy))]
    convert_element_type x3 -> x0, other arithmetic: 2.82 us -> none  [blend(): return (KEEP_LOCAL * local_rows.astype(jnp.float32) + (1.0 - KEEP_LOCAL)...]
    ppermute x21 -> x20, starting transfers between devices: 38.5 us -> 36.7 us  [send(): return lax.ppermute(v, 'fsdp', perm)]
  transfers between devices with their start and end apart: 31 -> 30, of which waited for: 13 -> 14; matrix products, arithmetic and copies ran while one was open for 2% -> 3% of each run, Pallas kernels for 14% -> 13%
where the time goes in v3:
time: 108 us
  starting transfers between devices  53.1 us (49%)
  waiting for transfers between devices  32.9 us (30%)
  Pallas kernels  15.3 us (14%)
  other arithmetic  3.79 us (4%)
  local copies, waits for them, and re-layouts  2.03 us (2%)
    ppermute x20, starting transfers between devices, send(): return lax.ppermute(v, 'fsdp', perm)  36.7 us
    ppermute x20, waiting for transfers between devices, send(): return lax.ppermute(v, 'fsdp', perm)  21.6 us
    ppermute x10, starting transfers between devices, send_rep(): return lax.ppermute(v, 'rep', rep_perm(dx, dy))  16.4 us
    pallas_call x4, Pallas kernels, product_step(): pl.pallas_call(functools.partial(product_kernel, slots, parts, empty, boo...  12.7 us
    ppermute x10, waiting for transfers between devices, send_rep(): return lax.ppermute(v, 'rep', rep_perm(dx, dy))  11.4 us
    broadcast_in_dim x2, other arithmetic, on_device(): return (new_global, new_moment, new_local[None], projected[None])  2.62 us
  transfers between devices with their start and end apart: 30, of which 14 were waited for; matrix products, arithmetic and copies ran while one was open for 3% of the time, Pallas kernels for 13%

profile of v3, /device:TPU:1, one launch (start us, length us, event | category | flops | bytes accessed | tf_op | source)
XLA Modules:
  0.0 108.1 jit_solution(1383253662181264860)
XLA Ops:
  0.7 1.1 dynamic-slice_bitcast_fusion.2
  1.8 2.1 %collective-permute-start = (bf16[80,768]{1,0:T(8,128)(2,1)S(1)}, bf16[80,768]{1,0:T(8,128)(2,1)S(1)}, u32[]{:S(2)}, u32[]{:S(2)}) collective-permute-start(bf16[80,768]{1,0:T(8,128)(2,1)S(1)} %get-tuple-element.48), channel_id=1, source_target_pairs={{0,64},{32,96},{64,128},{96,160},{128,192},{160,224},{192,0},{224,... | collective-permute-start | bytes 368648 | tf_op jit(solution)/shard_map/quarters/ppermute | solution.py:38
  3.9 2.5 %collective-permute-start.1 = (bf16[80,768]{1,0:T(8,128)(2,1)S(1)}, bf16[80,768]{1,0:T(8,128)(2,1)S(1)}, u32[]{:S(2)}, u32[]{:S(2)}) collective-permute-start(bf16[80,768]{1,0:T(8,128)(2,1)S(1)} %get-tuple-element.49), channel_id=1, source_target_pairs={{0,128},{32,160},{64,192},{96,224},{128,0},{160,32},{192,64},{224,... | collective-permute-start | bytes 368648 | tf_op jit(solution)/shard_map/quarters/ppermute | solution.py:38
  6.3 1.2 %collective-permute-start.2 = (bf16[80,768]{1,0:T(8,128)(2,1)S(1)}, bf16[80,768]{1,0:T(8,128)(2,1)S(1)}, u32[]{:S(2)}, u32[]{:S(2)}) collective-permute-start(bf16[80,768]{1,0:T(8,128)(2,1)S(1)} %get-tuple-element.50), channel_id=1, source_target_pairs={{0,192},{32,224},{64,0},{96,32},{128,64},{160,96},{192,128},{224,1... | collective-permute-start | bytes 368648 | tf_op jit(solution)/shard_map/quarters/ppermute | solution.py:38
  7.5 1.0 constant_dynamic-slice_fusion.moment_ref
  8.5 3.2 %collective-permute-done.1.refs_2_ = bf16[80,768]{1,0:T(8,128)(2,1)S(1)} collective-permute-done((bf16[80,768]{1,0:T(8,128)(2,1)S(1)}, bf16[80,768]{1,0:T(8,128)(2,1)S(1)}, u32[]{:S(2)}, u32[]{:S(2)}) %collective-permute-start.1) | collective-permute-done | bytes 122912 | tf_op jit(solution)/shard_map/quarters/ppermute | solution.py:38
  11.7 1.1 %subtract_add_fusion = (f32[80,768]{1,0:T(8,128)S(1)}, bf16[80,768]{1,0:T(8,128)(2,1)S(1)}, f32[80,768]{1,0:T(8,128)S(1)}) fusion(bf16[80,768]{1,0:T(8,128)(2,1)S(1)} %collective-permute-done.2.refs_3_, bf16[80,768]{1,0:T(8,128)(2,1)S(1)} %collective-permute-done.1.refs_2_, bf16[80,768]{1,0:T(8,128)(2,1)S(1)} %collective-permute-done.refs_1_, ...), kind=kLoop, calls=%fused_computation.11 | loop fusion | flops 675840 | bytes 1351684 | tf_op jit(solution)/shard_map/add | solution.py:256
  12.8 3.0 %collective-permute-start.3 = (f32[80,768]{1,0:T(8,128)S(1)}, f32[80,768]{1,0:T(8,128)S(1)}, u32[]{:S(2)}, u32[]{:S(2)}) collective-permute-start(f32[80,768]{1,0:T(8,128)S(1)} %get-tuple-element.23.one), channel_id=1, source_target_pairs={{0,32},{32,0},{64,96},{96,64},{128,160},{160,128},{192,224},{224,1... | collective-permute-start | bytes 737288 | tf_op jit(solution)/shard_map/four/ppermute | solution.py:38
  15.8 4.1 %collective-permute-done.3.two = f32[80,768]{1,0:T(8,128)S(1)} collective-permute-done((f32[80,768]{1,0:T(8,128)S(1)}, f32[80,768]{1,0:T(8,128)S(1)}, u32[]{:S(2)}, u32[]{:S(2)}) %collective-permute-start.3) | collective-permute-done | bytes 245792 | tf_op jit(solution)/shard_map/four/ppermute | solution.py:38
  19.9 0.8 shard_map.75
  20.7 1.1 %collective-permute-start.4 = (bf16[80,768]{1,0:T(8,128)(2,1)S(1)}, bf16[80,768]{1,0:T(8,128)(2,1)S(1)}, u32[]{:S(2)}, u32[]{:S(2)}) collective-permute-start(bf16[80,768]{1,0:T(8,128)(2,1)S(1)} %get-tuple-element.29), channel_id=1, source_target_pairs={{0,64},{32,96},{64,128},{96,160},{128,192},{160,224},{192,0},{224,... | collective-permute-start | bytes 368648 | tf_op jit(solution)/shard_map/home/ppermute | solution.py:38
  21.8 2.4 %collective-permute-start.5 = (bf16[80,768]{1,0:T(8,128)(2,1)S(1)}, bf16[80,768]{1,0:T(8,128)(2,1)S(1)}, u32[]{:S(2)}, u32[]{:S(2)}) collective-permute-start(bf16[80,768]{1,0:T(8,128)(2,1)S(1)} %get-tuple-element.30), channel_id=1, source_target_pairs={{0,128},{32,160},{64,192},{96,224},{128,0},{160,32},{192,64},{224,... | collective-permute-start | bytes 368648 | tf_op jit(solution)/shard_map/home/ppermute | solution.py:38
  24.2 1.4 %collective-permute-done.4.refs_1_ = bf16[80,768]{1,0:T(8,128)(2,1)S(1)} collective-permute-done((bf16[80,768]{1,0:T(8,128)(2,1)S(1)}, bf16[80,768]{1,0:T(8,128)(2,1)S(1)}, u32[]{:S(2)}, u32[]{:S(2)}) %collective-permute-start.4) | collective-permute-done | bytes 122912 | tf_op jit(solution)/shard_map/home/ppermute | solution.py:38
  25.6 2.2 %collective-permute-done.5.refs_2_ = bf16[80,768]{1,0:T(8,128)(2,1)S(1)} collective-permute-done((bf16[80,768]{1,0:T(8,128)(2,1)S(1)}, bf16[80,768]{1,0:T(8,128)(2,1)S(1)}, u32[]{:S(2)}, u32[]{:S(2)}) %collective-permute-start.5) | collective-permute-done | bytes 122912 | tf_op jit(solution)/shard_map/home/ppermute | solution.py:38
  28.2 0.7 shard_map.76.refs_4_
  28.9 4.3 %collective-permute-start.8 = (bf16[320,768]{1,0:T(8,128)(2,1)S(1)}, bf16[320,768]{1,0:T(8,128)(2,1)S(1)}, u32[]{:S(2)}, u32[]{:S(2)}) collective-permute-start(bf16[320,768]{1,0:T(8,128)(2,1)S(1)} %shard_map.76.refs_4_), channel_id=1, source_target_pairs={{0,1},{1,0},{2,3},{3,2},{4,5},{5,4},{6,7},{7,6},{8,9},{9,8},{10,11... | collective-permute-start | bytes 1474568 | tf_op jit(solution)/shard_map/b/ppermute | solution.py:49
  33.3 5.6 %collective-permute-start.7 = (bf16[320,768]{1,0:T(8,128)(2,1)S(1)}, bf16[320,768]{1,0:T(8,128)(2,1)}, u32[]{:S(2)}, u32[]{:S(2)}) collective-permute-start(bf16[320,768]{1,0:T(8,128)(2,1)S(1)} %shard_map.76.refs_4_), channel_id=1, source_target_pairs={{0,2},{1,15},{2,4},{3,1},{4,6},{5,3},{6,8},{7,5},{8,10},{9,7},{10,... | collective-permute-start | bytes 1474568 | tf_op jit(solution)/shard_map/a1/ppermute | solution.py:49
  38.9 1.6 %collective-permute-start.10 = (bf16[320,768]{1,0:T(8,128)(2,1)S(1)}, bf16[320,768]{1,0:T(8,128)(2,1)S(1)}, u32[]{:S(2)}, u32[]{:S(2)}) collective-permute-start(bf16[320,768]{1,0:T(8,128)(2,1)S(1)} %shard_map.77.refs_1_), channel_id=1, source_target_pairs={{0,2},{1,15},{2,4},{3,1},{4,6},{5,3},{6,8},{7,5},{8,10},{9,7},{10,... | collective-permute-start | bytes 1474568 | tf_op jit(solution)/shard_map/b1/ppermute | solution.py:49
  40.5 4.2 %collective-permute-done.7.refs_0_ = bf16[320,768]{1,0:T(8,128)(2,1)} collective-permute-done((bf16[320,768]{1,0:T(8,128)(2,1)S(1)}, bf16[320,768]{1,0:T(8,128)(2,1)}, u32[]{:S(2)}, u32[]{:S(2)}) %collective-permute-start.7) | collective-permute-done | bytes 491552 | tf_op jit(solution)/shard_map/a1/ppermute | solution.py:49
  44.7 3.2 %collective-permute-start.9 = (bf16[320,768]{1,0:T(8,128)(2,1)}, bf16[320,768]{1,0:T(8,128)(2,1)}, u32[]{:S(2)}, u32[]{:S(2)}) collective-permute-start(bf16[320,768]{1,0:T(8,128)(2,1)} %shard_map.78.refs_1_.refs_2_), channel_id=1, source_target_pairs={{0,2},{1,15},{2,4},{3,1},{4,6},{5,3},{6,8},{7,5},{8,10},{9,7},{10,... | collective-permute-start | bytes 1474568 | tf_op jit(solution)/shard_map/a2/ppermute | solution.py:49
  47.9 1.3 %collective-permute-start.23 = (bf16[320,768]{1,0:T(8,128)(2,1)}, bf16[320,768]{1,0:T(8,128)(2,1)}, u32[]{:S(2)}, u32[]{:S(2)}) collective-permute-start(bf16[320,768]{1,0:T(8,128)(2,1)} %shard_map.78.refs_1_.refs_2_), channel_id=1, source_target_pairs={{0,16},{1,17},{2,18},{3,19},{4,20},{5,21},{6,22},{7,23},{8,24},{9,... | collective-permute-start | bytes 1474568 | tf_op jit(solution)/shard_map/side1/ppermute | solution.py:49
  49.2 3.6 %collective-permute-done.11.refs_0_ = bf16[320,768]{1,0:T(8,128)(2,1)S(1)} collective-permute-done((bf16[320,768]{1,0:T(8,128)(2,1)S(1)}, bf16[320,768]{1,0:T(8,128)(2,1)S(1)}, u32[]{:S(2)}, u32[]{:S(2)}) %collective-permute-start.11) | collective-permute-done | bytes 491552 | tf_op jit(solution)/shard_map/part_b/ppermute | solution.py:49
  52.8 0.7 collective-permute-start.14
  53.5 0.9 collective-permute-start.13
  54.4 0.9 collective-permute-done.9.refs_0_
  55.3 3.1 %collective-permute-start.12 = (bf16[320,768]{1,0:T(8,128)(2,1)}, bf16[320,768]{1,0:T(8,128)(2,1)S(1)}, u32[]{:S(2)}, u32[]{:S(2)}) collective-permute-start(bf16[320,768]{1,0:T(8,128)(2,1)} %shard_map.81.refs_1_.refs_2_), channel_id=1, source_target_pairs={{0,2},{1,15},{2,4},{3,1},{4,6},{5,3},{6,8},{7,5},{8,10},{9,7},{10,... | collective-permute-start | bytes 1474568 | tf_op jit(solution)/shard_map/a3/ppermute | solution.py:49
  58.4 2.4 %collective-permute-done.14.refs_0_ = bf16[320,768]{1,0:T(8,128)(2,1)S(1)} collective-permute-done((bf16[320,768]{1,0:T(8,128)(2,1)S(1)}, bf16[320,768]{1,0:T(8,128)(2,1)S(1)}, u32[]{:S(2)}, u32[]{:S(2)}) %collective-permute-start.14) | collective-permute-done | bytes 491552 | tf_op jit(solution)/shard_map/part_b1/ppermute | solution.py:49
  60.9 0.9 collective-permute-start.22
  61.8 3.1 %collective-permute-start.21 = (bf16[320,768]{1,0:T(8,128)(2,1)S(1)}, bf16[320,768]{1,0:T(8,128)(2,1)S(1)}, u32[]{:S(2)}, u32[]{:S(2)}) collective-permute-start(bf16[320,768]{1,0:T(8,128)(2,1)S(1)} %shard_map.82.refs_1_.refs_7_), channel_id=1, source_target_pairs={{0,2},{1,15},{2,4},{3,1},{4,6},{5,3},{6,8},{7,5},{8,10},{9,7},{10,... | collective-permute-start | bytes 1474568 | tf_op jit(solution)/shard_map/part_b2/ppermute | solution.py:49
  64.9 3.3 %shard_map.83 = (f32[256,768]{1,0:T(8,128)S(1)}, f32[256,768]{1,0:T(8,128)S(1)}, f32[8,128]{1,0:T(8,128)S(1)}) custom-call(bf16[256,10240]{1,0:T(8,128)(2,1)S(1)} %bitcast.20, bf16[256,10240]{1,0:T(8,128)(2,1)} %collective-permute-done.15.refs_1_, bf16[320,768]{1,0:T(8,128)(2,1)} %shard_map.78.refs_1_.refs_2_, ...), custom_call_target="tpu_custom_call" | custom-call | flops 30000001024 | bytes 6488064 | tf_op jit(solution)/shard_map/pallas_call | solution.py:191
  68.9 2.5 %collective-permute-done.12.refs_0_ = bf16[320,768]{1,0:T(8,128)(2,1)S(1)} collective-permute-done((bf16[320,768]{1,0:T(8,128)(2,1)}, bf16[320,768]{1,0:T(8,128)(2,1)S(1)}, u32[]{:S(2)}, u32[]{:S(2)}) %collective-permute-start.12) | collective-permute-done | bytes 491552 | tf_op jit(solution)/shard_map/a3/ppermute | solution.py:49
  71.4 1.0 collective-permute-start.27
  72.4 4.1 %collective-permute-done.21.refs_0_ = bf16[320,768]{1,0:T(8,128)(2,1)S(1)} collective-permute-done((bf16[320,768]{1,0:T(8,128)(2,1)S(1)}, bf16[320,768]{1,0:T(8,128)(2,1)S(1)}, u32[]{:S(2)}, u32[]{:S(2)}) %collective-permute-start.21) | collective-permute-done | bytes 491552 | tf_op jit(solution)/shard_map/part_b2/ppermute | solution.py:49
  76.6 2.8 %collective-permute-start.19 = (bf16[160,768]{1,0:T(8,128)(2,1)S(1)}, bf16[160,768]{1,0:T(8,128)(2,1)S(1)}, u32[]{:S(2)}, u32[]{:S(2)}) collective-permute-start(bf16[160,768]{1,0:T(8,128)(2,1)S(1)} %slice_select_fusion.2), channel_id=1, source_target_pairs={{0,2},{1,15},{2,4},{3,1},{4,6},{5,3},{6,8},{7,5},{8,10},{9,7},{10,... | collective-permute-start | bytes 737288 | tf_op jit(solution)/shard_map/a4/ppermute | solution.py:49
  80.0 3.9 %shard_map.89 = (f32[256,768]{1,0:T(8,128)S(1)}, f32[256,768]{1,0:T(8,128)S(1)}, f32[8,128]{1,0:T(8,128)S(1)}) custom-call(bf16[256,10240]{1,0:T(8,128)(2,1)S(1)} %bitcast.21, bf16[256,10240]{1,0:T(8,128)(2,1)} %collective-permute-done.15.refs_1_, bf16[320,768]{1,0:T(8,128)(2,1)} %shard_map.81.refs_1_.refs_2_, ...), custom_call_target="tpu_custom_call" | custom-call | flops 30000001024 | bytes 6488064 | tf_op jit(solution)/shard_map/pallas_call | solution.py:191
  83.9 0.7 collective-permute-done.19.refs_2_
  84.6 1.8 %collective-permute-start.17 = (f32[80,768]{1,0:T(8,128)}, f32[80,768]{1,0:T(8,128)S(1)}, u32[]{:S(2)}, u32[]{:S(2)}) collective-permute-start(f32[80,768]{1,0:T(8,128)} %shard_map.86.refs_0_), channel_id=1, source_target_pairs={{0,128},{32,160},{64,192},{96,224},{128,0},{160,32},{192,64},{224,... | collective-permute-start | bytes 737288 | tf_op jit(solution)/shard_map/gradient/ppermute | solution.py:38
  86.4 1.3 %collective-permute-start.25 = (bf16[160,768]{1,0:T(8,128)(2,1)S(1)}, bf16[160,768]{1,0:T(8,128)(2,1)S(1)}, u32[]{:S(2)}, u32[]{:S(2)}) collective-permute-start(bf16[160,768]{1,0:T(8,128)(2,1)S(1)} %collective-permute-done.19.refs_2_), channel_id=1, source_target_pairs={{0,16},{1,17},{2,18},{3,19},{4,20},{5,21},{6,22},{7,23},{8,24},{9,... | collective-permute-start | bytes 737288 | tf_op jit(solution)/shard_map/far_side/ppermute | solution.py:49
  87.7 2.0 %collective-permute-done.26.refs_0_ = bf16[320,768]{1,0:T(8,128)(2,1)S(1)} collective-permute-done((bf16[320,768]{1,0:T(8,128)(2,1)S(1)}, bf16[320,768]{1,0:T(8,128)(2,1)S(1)}, u32[]{:S(2)}, u32[]{:S(2)}) %collective-permute-start.26) | collective-permute-done | bytes 491552 | tf_op jit(solution)/shard_map/part_b3/ppermute | solution.py:49
  89.8 3.2 %collective-permute-start.28 = (bf16[160,768]{1,0:T(8,128)(2,1)S(1)}, bf16[160,768]{1,0:T(8,128)(2,1)S(1)}, u32[]{:S(2)}, u32[]{:S(2)}) collective-permute-start(bf16[160,768]{1,0:T(8,128)(2,1)S(1)} %slice_select_fusion), channel_id=1, source_target_pairs={{0,2},{1,15},{2,4},{3,1},{4,6},{5,3},{6,8},{7,5},{8,10},{9,7},{10,... | collective-permute-start | bytes 737288 | tf_op jit(solution)/shard_map/part_b4/ppermute | solution.py:49
  93.1 2.7 %shard_map.92 = (f32[256,768]{1,0:T(8,128)S(1)}, f32[256,768]{1,0:T(8,128)S(1)}, f32[8,128]{1,0:T(8,128)}) custom-call(bf16[256,10240]{1,0:T(8,128)(2,1)S(1)} %bitcast.22, bf16[256,10240]{1,0:T(8,128)(2,1)} %collective-permute-done.15.refs_1_, bf16[320,768]{1,0:T(8,128)(2,1)S(1)} %shard_map.85.refs_1_.refs_2_, ...), custom_call_target="tpu_custom_call" | custom-call | flops 30000001024 | bytes 4849664 | tf_op jit(solution)/shard_map/pallas_call | solution.py:191
  95.8 1.8 %collective-permute-start.18 = (f32[80,768]{1,0:T(8,128)}, f32[80,768]{1,0:T(8,128)S(1)}, u32[]{:S(2)}, u32[]{:S(2)}) collective-permute-start(f32[80,768]{1,0:T(8,128)} %shard_map.86.refs_0_), channel_id=1, source_target_pairs={{0,192},{32,224},{64,0},{96,32},{128,64},{160,96},{192,128},{224,1... | collective-permute-start | bytes 737288 | tf_op jit(solution)/shard_map/gradient/ppermute | solution.py:38
  97.6 1.1 %collective-permute-done.24.refs_3_ = bf16[160,768]{1,0:T(8,128)(2,1)S(1)} collective-permute-done((bf16[160,768]{1,0:T(8,128)(2,1)S(1)}, bf16[160,768]{1,0:T(8,128)(2,1)S(1)}, u32[]{:S(2)}, u32[]{:S(2)}) %collective-permute-start.24) | collective-permute-done | bytes 245792 | tf_op jit(solution)/shard_map/b4/ppermute | solution.py:49
  98.7 2.8 %shard_map.93 = (f32[256,768]{1,0:T(8,128)S(1)}, bf16[256,768]{1,0:T(8,128)(2,1)S(1)}, f32[8,128]{1,0:T(8,128)}) custom-call(bf16[256,10240]{1,0:T(8,128)(2,1)S(1)} %bitcast.23, bf16[256,10240]{1,0:T(8,128)(2,1)} %collective-permute-done.15.refs_1_, bf16[160,768]{1,0:T(8,128)(2,1)S(1)} %collective-permute-done.19.refs_2_, ...), custom_call_target="tpu_custom_call" | custom-call | flops 30000001024 | bytes 4849664 | tf_op jit(solution)/shard_map/pallas_call | solution.py:191
  101.6 2.7 %collective-permute-start.29 = (bf16[256,768]{1,0:T(8,128)(2,1)S(1)}, bf16[256,768]{1,0:T(8,128)(2,1)S(1)}, u32[]{:S(2)}, u32[]{:S(2)}) collective-permute-start(bf16[256,768]{1,0:T(8,128)(2,1)S(1)} %get-tuple-element.41), channel_id=1, source_target_pairs={{0,1},{1,0},{2,3},{3,2},{4,5},{5,4},{6,7},{7,6},{8,9},{9,8},{10,11... | collective-permute-start | bytes 1179656 | tf_op jit(solution)/shard_map/late/ppermute | solution.py:49
  104.3 1.1 %shard_map.87 = f32[320,768]{1,0:T(8,128)S(1)} custom-call(f32[80,768]{1,0:T(8,128)} %shard_map.86.refs_0_, f32[80,768]{1,0:T(8,128)} %collective-permute-done.16.refs_1_, f32[80,768]{1,0:T(8,128)S(1)} %collective-permute-done.17.refs_2_, f32[80,768]{1,0:T(8,128)S(1)} %collective-permute-done.18.refs_3_), custom_call_target="tpu_custom_call" | custom-call | bytes 983040 | tf_op jit(solution)/shard_map/pallas_call | solution.py:103
  105.4 1.8 %fusion.2 = (bf16[1,320,768]{2,1,0:T(8,128)(2,1)}, f32[320,768]{1,0:T(8,128)}, f32[320,768]{1,0:T(8,128)}) fusion(bf16[1,320,768]{2,1,0:T(8,128)(2,1)S(1)} %copy-done, f32[320,768]{1,0:T(8,128)S(1)} %copy-done.1, f32[320,768]{1,0:T(8,128)S(1)} %shard_map.87, f32[320,768]{1,0:T(8,128)S(1)} %copy-done.2), kind=kLoop, calls=%fused_computation.6 | loop fusion | flops 2457600 | bytes 5898240 | tf_op jit(solution)/shard_map/broadcast_in_dim | solution.py:342
  107.2 0.9 fusion.3
  (50 shorter events, 2.1 us)
Async XLA Ops:
  1.8 6.7 %collective-permute-start = (bf16[80,768]{1,0:T(8,128)(2,1)S(1)}, bf16[80,768]{1,0:T(8,128)(2,1)S(1)}, u32[]{:S(2)}, u32[]{:S(2)}) collective-permute-start(bf16[80,768]{1,0:T(8,128)(2,1)S(1)} %get-tuple-element.48), channel_id=1, source_target_pairs={{0,64},{32,96},{64,128},{96,160},{128,192},{160,224},{192,0},{224,... | collective-permute-start | bytes 368648 | tf_op jit(solution)/shard_map/quarters/ppermute | solution.py:38
  3.9 7.8 %collective-permute-start.1 = (bf16[80,768]{1,0:T(8,128)(2,1)S(1)}, bf16[80,768]{1,0:T(8,128)(2,1)S(1)}, u32[]{:S(2)}, u32[]{:S(2)}) collective-permute-start(bf16[80,768]{1,0:T(8,128)(2,1)S(1)} %get-tuple-element.49), channel_id=1, source_target_pairs={{0,128},{32,160},{64,192},{96,224},{128,0},{160,32},{192,64},{224,... | collective-permute-start | bytes 368648 | tf_op jit(solution)/shard_map/quarters/ppermute | solution.py:38
  6.3 5.4 %collective-permute-start.2 = (bf16[80,768]{1,0:T(8,128)(2,1)S(1)}, bf16[80,768]{1,0:T(8,128)(2,1)S(1)}, u32[]{:S(2)}, u32[]{:S(2)}) collective-permute-start(bf16[80,768]{1,0:T(8,128)(2,1)S(1)} %get-tuple-element.50), channel_id=1, source_target_pairs={{0,192},{32,224},{64,0},{96,32},{128,64},{160,96},{192,128},{224,1... | collective-permute-start | bytes 368648 | tf_op jit(solution)/shard_map/quarters/ppermute | solution.py:38
  12.8 7.1 %collective-permute-start.3 = (f32[80,768]{1,0:T(8,128)S(1)}, f32[80,768]{1,0:T(8,128)S(1)}, u32[]{:S(2)}, u32[]{:S(2)}) collective-permute-start(f32[80,768]{1,0:T(8,128)S(1)} %get-tuple-element.23.one), channel_id=1, source_target_pairs={{0,32},{32,0},{64,96},{96,64},{128,160},{160,128},{192,224},{224,1... | collective-permute-start | bytes 737288 | tf_op jit(solution)/shard_map/four/ppermute | solution.py:38
  20.7 4.9 %collective-permute-start.4 = (bf16[80,768]{1,0:T(8,128)(2,1)S(1)}, bf16[80,768]{1,0:T(8,128)(2,1)S(1)}, u32[]{:S(2)}, u32[]{:S(2)}) collective-permute-start(bf16[80,768]{1,0:T(8,128)(2,1)S(1)} %get-tuple-element.29), channel_id=1, source_target_pairs={{0,64},{32,96},{64,128},{96,160},{128,192},{160,224},{192,0},{224,... | collective-permute-start | bytes 368648 | tf_op jit(solution)/shard_map/home/ppermute | solution.py:38
  21.8 6.0 %collective-permute-start.5 = (bf16[80,768]{1,0:T(8,128)(2,1)S(1)}, bf16[80,768]{1,0:T(8,128)(2,1)S(1)}, u32[]{:S(2)}, u32[]{:S(2)}) collective-permute-start(bf16[80,768]{1,0:T(8,128)(2,1)S(1)} %get-tuple-element.30), channel_id=1, source_target_pairs={{0,128},{32,160},{64,192},{96,224},{128,0},{160,32},{192,64},{224,... | collective-permute-start | bytes 368648 | tf_op jit(solution)/shard_map/home/ppermute | solution.py:38
  24.2 4.0 %collective-permute-start.6 = (bf16[80,768]{1,0:T(8,128)(2,1)S(1)}, bf16[80,768]{1,0:T(8,128)(2,1)S(1)}, u32[]{:S(2)}, u32[]{:S(2)}) collective-permute-start(bf16[80,768]{1,0:T(8,128)(2,1)S(1)} %get-tuple-element.31), channel_id=1, source_target_pairs={{0,192},{32,224},{64,0},{96,32},{128,64},{160,96},{192,128},{224,1... | collective-permute-start | bytes 368648 | tf_op jit(solution)/shard_map/home/ppermute | solution.py:38
  28.9 10.0 %collective-permute-start.8 = (bf16[320,768]{1,0:T(8,128)(2,1)S(1)}, bf16[320,768]{1,0:T(8,128)(2,1)S(1)}, u32[]{:S(2)}, u32[]{:S(2)}) collective-permute-start(bf16[320,768]{1,0:T(8,128)(2,1)S(1)} %shard_map.76.refs_4_), channel_id=1, source_target_pairs={{0,1},{1,0},{2,3},{3,2},{4,5},{5,4},{6,7},{7,6},{8,9},{9,8},{10,11... | collective-permute-start | bytes 1474568 | tf_op jit(solution)/shard_map/b/ppermute | solution.py:49
  33.2 28.6 %collective-permute-start.15 = (bf16[256,10240]{1,0:T(8,128)(2,1)}, bf16[256,10240]{1,0:T(8,128)(2,1)}, u32[]{:S(2)}, u32[]{:S(2)}) collective-permute-start(bf16[256,10240]{1,0:T(8,128)(2,1)} %bitcast.17), channel_id=1, source_target_pairs={{0,1},{1,0},{2,3},{3,2},{4,5},{5,4},{6,7},{7,6},{8,9},{9,8},{10,11... | collective-permute-start | bytes 15728648 | tf_op jit(solution)/shard_map/other/ppermute | solution.py:49
  33.3 11.4 %collective-permute-start.7 = (bf16[320,768]{1,0:T(8,128)(2,1)S(1)}, bf16[320,768]{1,0:T(8,128)(2,1)}, u32[]{:S(2)}, u32[]{:S(2)}) collective-permute-start(bf16[320,768]{1,0:T(8,128)(2,1)S(1)} %shard_map.76.refs_4_), channel_id=1, source_target_pairs={{0,2},{1,15},{2,4},{3,1},{4,6},{5,3},{6,8},{7,5},{8,10},{9,7},{10,... | collective-permute-start | bytes 1474568 | tf_op jit(solution)/shard_map/a1/ppermute | solution.py:49
  38.9 13.9 %collective-permute-start.11 = (bf16[320,768]{1,0:T(8,128)(2,1)S(1)}, bf16[320,768]{1,0:T(8,128)(2,1)S(1)}, u32[]{:S(2)}, u32[]{:S(2)}) collective-permute-start(bf16[320,768]{1,0:T(8,128)(2,1)S(1)} %shard_map.76.refs_4_), channel_id=1, source_target_pairs={{0,17},{1,16},{2,19},{3,18},{4,21},{5,20},{6,23},{7,22},{8,25},{9,... | collective-permute-start | bytes 1474568 | tf_op jit(solution)/shard_map/part_b/ppermute | solution.py:49
  38.9 14.6 %collective-permute-start.10 = (bf16[320,768]{1,0:T(8,128)(2,1)S(1)}, bf16[320,768]{1,0:T(8,128)(2,1)S(1)}, u32[]{:S(2)}, u32[]{:S(2)}) collective-permute-start(bf16[320,768]{1,0:T(8,128)(2,1)S(1)} %shard_map.77.refs_1_), channel_id=1, source_target_pairs={{0,2},{1,15},{2,4},{3,1},{4,6},{5,3},{6,8},{7,5},{8,10},{9,7},{10,... | collective-permute-start | bytes 1474568 | tf_op jit(solution)/shard_map/b1/ppermute | solution.py:49
  44.7 10.6 %collective-permute-start.9 = (bf16[320,768]{1,0:T(8,128)(2,1)}, bf16[320,768]{1,0:T(8,128)(2,1)}, u32[]{:S(2)}, u32[]{:S(2)}) collective-permute-start(bf16[320,768]{1,0:T(8,128)(2,1)} %shard_map.78.refs_1_.refs_2_), channel_id=1, source_target_pairs={{0,2},{1,15},{2,4},{3,1},{4,6},{5,3},{6,8},{7,5},{8,10},{9,7},{10,... | collective-permute-start | bytes 1474568 | tf_op jit(solution)/shard_map/a2/ppermute | solution.py:49
  47.9 31.5 %collective-permute-start.23 = (bf16[320,768]{1,0:T(8,128)(2,1)}, bf16[320,768]{1,0:T(8,128)(2,1)}, u32[]{:S(2)}, u32[]{:S(2)}) collective-permute-start(bf16[320,768]{1,0:T(8,128)(2,1)} %shard_map.78.refs_1_.refs_2_), channel_id=1, source_target_pairs={{0,16},{1,17},{2,18},{3,19},{4,20},{5,21},{6,22},{7,23},{8,24},{9,... | collective-permute-start | bytes 1474568 | tf_op jit(solution)/shard_map/side1/ppermute | solution.py:49
  52.8 8.1 %collective-permute-start.14 = (bf16[320,768]{1,0:T(8,128)(2,1)S(1)}, bf16[320,768]{1,0:T(8,128)(2,1)S(1)}, u32[]{:S(2)}, u32[]{:S(2)}) collective-permute-start(bf16[320,768]{1,0:T(8,128)(2,1)S(1)} %shard_map.79.refs_1_.refs_5_), channel_id=1, source_target_pairs={{0,2},{1,15},{2,4},{3,1},{4,6},{5,3},{6,8},{7,5},{8,10},{9,7},{10,... | collective-permute-start | bytes 1474568 | tf_op jit(solution)/shard_map/part_b1/ppermute | solution.py:49
  53.5 14.7 %collective-permute-start.13 = (bf16[320,768]{1,0:T(8,128)(2,1)S(1)}, bf16[320,768]{1,0:T(8,128)(2,1)S(1)}, u32[]{:S(2)}, u32[]{:S(2)}) collective-permute-start(bf16[320,768]{1,0:T(8,128)(2,1)S(1)} %shard_map.80.refs_1_.refs_3_), channel_id=1, source_target_pairs={{0,2},{1,15},{2,4},{3,1},{4,6},{5,3},{6,8},{7,5},{8,10},{9,7},{10,... | collective-permute-start | bytes 1474568 | tf_op jit(solution)/shard_map/b2/ppermute | solution.py:49
  55.3 9.6 %slice-start = ((s8[5242880]{0:T(1024)(128)(4,1)}), s8[4194304]{0:T(1024)(128)(4,1)S(1)}, s32[]{:S(2)}) async-start(s8[5242880]{0:T(1024)(128)(4,1)} %bitcast.18), calls=%async_computation | async-start | bytes 8388608
  55.3 9.6 %slice-start.1 = ((s8[5242880]{0:T(1024)(128)(4,1)}), s8[1048576]{0:T(1024)(128)(4,1)S(1)}, s32[]{:S(2)}) async-start(s8[5242880]{0:T(1024)(128)(4,1)} %bitcast.18), calls=%async_computation.1 | async-start | bytes 2097152
  55.3 16.1 %collective-permute-start.12 = (bf16[320,768]{1,0:T(8,128)(2,1)}, bf16[320,768]{1,0:T(8,128)(2,1)S(1)}, u32[]{:S(2)}, u32[]{:S(2)}) collective-permute-start(bf16[320,768]{1,0:T(8,128)(2,1)} %shard_map.81.refs_1_.refs_2_), channel_id=1, source_target_pairs={{0,2},{1,15},{2,4},{3,1},{4,6},{5,3},{6,8},{7,5},{8,10},{9,7},{10,... | collective-permute-start | bytes 1474568 | tf_op jit(solution)/shard_map/a3/ppermute | solution.py:49
  60.9 18.6 %collective-permute-start.22 = (bf16[320,768]{1,0:T(8,128)(2,1)}, bf16[320,768]{1,0:T(8,128)(2,1)}, u32[]{:S(2)}, u32[]{:S(2)}) collective-permute-start(bf16[320,768]{1,0:T(8,128)(2,1)} %shard_map.81.refs_1_.refs_2_), channel_id=1, source_target_pairs={{0,16},{1,17},{2,18},{3,19},{4,20},{5,21},{6,22},{7,23},{8,24},{9,... | collective-permute-start | bytes 1474568 | tf_op jit(solution)/shard_map/side2/ppermute | solution.py:49
  61.8 14.8 %collective-permute-start.21 = (bf16[320,768]{1,0:T(8,128)(2,1)S(1)}, bf16[320,768]{1,0:T(8,128)(2,1)S(1)}, u32[]{:S(2)}, u32[]{:S(2)}) collective-permute-start(bf16[320,768]{1,0:T(8,128)(2,1)S(1)} %shard_map.82.refs_1_.refs_7_), channel_id=1, source_target_pairs={{0,2},{1,15},{2,4},{3,1},{4,6},{5,3},{6,8},{7,5},{8,10},{9,7},{10,... | collective-permute-start | bytes 1474568 | tf_op jit(solution)/shard_map/part_b2/ppermute | solution.py:49
  68.2 18.2 %collective-permute-start.20 = (bf16[320,768]{1,0:T(8,128)(2,1)S(1)}, bf16[320,768]{1,0:T(8,128)(2,1)S(1)}, u32[]{:S(2)}, u32[]{:S(2)}) collective-permute-start(bf16[320,768]{1,0:T(8,128)(2,1)S(1)} %shard_map.84.refs_1_.refs_3_), channel_id=1, source_target_pairs={{0,2},{1,15},{2,4},{3,1},{4,6},{5,3},{6,8},{7,5},{8,10},{9,7},{10,... | collective-permute-start | bytes 1474568 | tf_op jit(solution)/shard_map/b3/ppermute | solution.py:49
  71.4 18.3 %collective-permute-start.27 = (bf16[320,768]{1,0:T(8,128)(2,1)S(1)}, bf16[320,768]{1,0:T(8,128)(2,1)S(1)}, u32[]{:S(2)}, u32[]{:S(2)}) collective-permute-start(bf16[320,768]{1,0:T(8,128)(2,1)S(1)} %shard_map.85.refs_1_.refs_2_), channel_id=1, source_target_pairs={{0,16},{1,17},{2,18},{3,19},{4,20},{5,21},{6,22},{7,23},{8,24},{9,... | collective-permute-start | bytes 1474568 | tf_op jit(solution)/shard_map/side3/ppermute | solution.py:49
  76.6 8.0 %collective-permute-start.19 = (bf16[160,768]{1,0:T(8,128)(2,1)S(1)}, bf16[160,768]{1,0:T(8,128)(2,1)S(1)}, u32[]{:S(2)}, u32[]{:S(2)}) collective-permute-start(bf16[160,768]{1,0:T(8,128)(2,1)S(1)} %slice_select_fusion.2), channel_id=1, source_target_pairs={{0,2},{1,15},{2,4},{3,1},{4,6},{5,3},{6,8},{7,5},{8,10},{9,7},{10,... | collective-permute-start | bytes 737288 | tf_op jit(solution)/shard_map/a4/ppermute | solution.py:49
  79.4 10.3 %collective-permute-start.26 = (bf16[320,768]{1,0:T(8,128)(2,1)S(1)}, bf16[320,768]{1,0:T(8,128)(2,1)S(1)}, u32[]{:S(2)}, u32[]{:S(2)}) collective-permute-start(bf16[320,768]{1,0:T(8,128)(2,1)S(1)} %shard_map.88.refs_5_.refs_1_), channel_id=1, source_target_pairs={{0,2},{1,15},{2,4},{3,1},{4,6},{5,3},{6,8},{7,5},{8,10},{9,7},{10,... | collective-permute-start | bytes 1474568 | tf_op jit(solution)/shard_map/part_b3/ppermute | solution.py:49
  79.5 24.8 %collective-permute-start.16 = (f32[80,768]{1,0:T(8,128)}, f32[80,768]{1,0:T(8,128)}, u32[]{:S(2)}, u32[]{:S(2)}) collective-permute-start(f32[80,768]{1,0:T(8,128)} %shard_map.86.refs_0_), channel_id=1, source_target_pairs={{0,64},{32,96},{64,128},{96,160},{128,192},{160,224},{192,0},{224,... | collective-permute-start | bytes 737288 | tf_op jit(solution)/shard_map/gradient/ppermute | solution.py:38
  84.6 19.7 %collective-permute-start.17 = (f32[80,768]{1,0:T(8,128)}, f32[80,768]{1,0:T(8,128)S(1)}, u32[]{:S(2)}, u32[]{:S(2)}) collective-permute-start(f32[80,768]{1,0:T(8,128)} %shard_map.86.refs_0_), channel_id=1, source_target_pairs={{0,128},{32,160},{64,192},{96,224},{128,0},{160,32},{192,64},{224,... | collective-permute-start | bytes 737288 | tf_op jit(solution)/shard_map/gradient/ppermute | solution.py:38
  86.4 9.4 %collective-permute-start.25 = (bf16[160,768]{1,0:T(8,128)(2,1)S(1)}, bf16[160,768]{1,0:T(8,128)(2,1)S(1)}, u32[]{:S(2)}, u32[]{:S(2)}) collective-permute-start(bf16[160,768]{1,0:T(8,128)(2,1)S(1)} %collective-permute-done.19.refs_2_), channel_id=1, source_target_pairs={{0,16},{1,17},{2,18},{3,19},{4,20},{5,21},{6,22},{7,23},{8,24},{9,... | collective-permute-start | bytes 737288 | tf_op jit(solution)/shard_map/far_side/ppermute | solution.py:49
  89.8 7.9 %collective-permute-start.28 = (bf16[160,768]{1,0:T(8,128)(2,1)S(1)}, bf16[160,768]{1,0:T(8,128)(2,1)S(1)}, u32[]{:S(2)}, u32[]{:S(2)}) collective-permute-start(bf16[160,768]{1,0:T(8,128)(2,1)S(1)} %slice_select_fusion), channel_id=1, source_target_pairs={{0,2},{1,15},{2,4},{3,1},{4,6},{5,3},{6,8},{7,5},{8,10},{9,7},{10,... | collective-permute-start | bytes 737288 | tf_op jit(solution)/shard_map/part_b4/ppermute | solution.py:49
  93.0 5.8 %collective-permute-start.24 = (bf16[160,768]{1,0:T(8,128)(2,1)S(1)}, bf16[160,768]{1,0:T(8,128)(2,1)S(1)}, u32[]{:S(2)}, u32[]{:S(2)}) collective-permute-start(bf16[160,768]{1,0:T(8,128)(2,1)S(1)} %slice_select_fusion.1), channel_id=1, source_target_pairs={{0,2},{1,15},{2,4},{3,1},{4,6},{5,3},{6,8},{7,5},{8,10},{9,7},{10,... | collective-permute-start | bytes 737288 | tf_op jit(solution)/shard_map/b4/ppermute | solution.py:49
  95.8 8.5 %collective-permute-start.18 = (f32[80,768]{1,0:T(8,128)}, f32[80,768]{1,0:T(8,128)S(1)}, u32[]{:S(2)}, u32[]{:S(2)}) collective-permute-start(f32[80,768]{1,0:T(8,128)} %shard_map.86.refs_0_), channel_id=1, source_target_pairs={{0,192},{32,224},{64,0},{96,32},{128,64},{160,96},{192,128},{224,1... | collective-permute-start | bytes 737288 | tf_op jit(solution)/shard_map/gradient/ppermute | solution.py:38
  98.7 6.7 %copy-start = (bf16[1,320,768]{2,1,0:T(8,128)(2,1)S(1)}, bf16[1,320,768]{2,1,0:T(8,128)(2,1)}, u32[]{:S(2)}) copy-start(bf16[1,320,768]{2,1,0:T(8,128)(2,1)} %param.6) | copy-start | bytes 1474564
  98.7 6.7 %copy-start.1 = (f32[320,768]{1,0:T(8,128)S(1)}, f32[320,768]{1,0:T(8,128)}, u32[]{:S(2)}) copy-start(f32[320,768]{1,0:T(8,128)} %param.4) | copy-start | bytes 2949124
  98.7 6.7 %copy-start.2 = (f32[320,768]{1,0:T(8,128)S(1)}, f32[320,768]{1,0:T(8,128)}, u32[]{:S(2)}) copy-start(f32[320,768]{1,0:T(8,128)} %param.5) | copy-start | bytes 2949124
  101.6 5.6 %collective-permute-start.29 = (bf16[256,768]{1,0:T(8,128)(2,1)S(1)}, bf16[256,768]{1,0:T(8,128)(2,1)S(1)}, u32[]{:S(2)}, u32[]{:S(2)}) collective-permute-start(bf16[256,768]{1,0:T(8,128)(2,1)S(1)} %get-tuple-element.41), channel_id=1, source_target_pairs={{0,1},{1,0},{2,3},{3,2},{4,5},{5,4},{6,7},{7,6},{8,9},{9,8},{10,11... | collective-permute-start | bytes 1179656 | tf_op jit(solution)/shard_map/late/ppermute | solution.py:49

commit v4 on v3

--- a/solution.py
+++ b/solution.py
@@ -313,10 +313,10 @@
         ),
         (), totals,
     )
-    (b3,) = fence((b3,), part_b2, a4, mark)
+    (b3,) = fence((b3,), part_b2, mark)
     b4 = send(near_half(b3), to_ring, "b4")
     far_side = send(a4, to_side, "far_side")
-    (part_b3,) = fence((part_b3,), b3, side3)
+    (part_b3,) = fence((part_b3,), b3, b4)
     part_b4 = send(near_half(part_b3), to_ring, "part_b4")
     *totals, mark = product_step(
         ((0, 3), (1, 3)), tokens, (a3, b3, side3, part_b3),

time: 108 us -> 111 us (1.028)
    ppermute x20, starting transfers between devices: 36.7 us -> 38.3 us  [send(): return lax.ppermute(v, 'fsdp', perm)]
  transfers between devices with their start and end apart: 30 -> 30, of which waited for: 14 -> 13; matrix products, arithmetic and copies ran while one was open for 3% -> 4% of each run, Pallas kernels for 13% -> 13%
where the time goes in v4:
time: 111 us; the launch traced here: 110 us
  starting transfers between devices  54.2 us (49%)
  waiting for transfers between devices  33.5 us (30%)
  Pallas kernels  15 us (14%)
  other arithmetic  4.84 us (4%)
  local copies, waits for them, and re-layouts  2.03 us (2%)
    ppermute x20, starting transfers between devices, send(): return lax.ppermute(v, 'fsdp', perm)  38.3 us
    ppermute x20, waiting for transfers between devices, send(): return lax.ppermute(v, 'fsdp', perm)  22.2 us
    ppermute x10, starting transfers between devices, send_rep(): return lax.ppermute(v, 'rep', rep_perm(dx, dy))  15.9 us
    pallas_call x4, Pallas kernels, product_step(): pl.pallas_call(functools.partial(product_kernel, slots, parts, empty, boo...  12.8 us
    ppermute x10, waiting for transfers between devices, send_rep(): return lax.ppermute(v, 'rep', rep_perm(dx, dy))  11.3 us
    broadcast_in_dim x2, other arithmetic, on_device(): return (new_global, new_moment, new_local[None], projected[None])  2.6 us
  transfers between devices with their start and end apart: 30, of which 13 were waited for; matrix products, arithmetic and copies ran while one was open for 4% of the time, Pallas kernels for 13%

profile of v4, /device:TPU:1, one launch (start us, length us, event | category | flops | bytes accessed | tf_op | source)
XLA Modules:
  0.0 110.4 jit_solution(9787945600894833)
XLA Ops:
  0.7 1.1 dynamic-slice_bitcast_fusion.2
  1.8 2.1 %collective-permute-start = (bf16[80,768]{1,0:T(8,128)(2,1)S(1)}, bf16[80,768]{1,0:T(8,128)(2,1)S(1)}, u32[]{:S(2)}, u32[]{:S(2)}) collective-permute-start(bf16[80,768]{1,0:T(8,128)(2,1)S(1)} %get-tuple-element.48), channel_id=1, source_target_pairs={{0,64},{32,96},{64,128},{96,160},{128,192},{160,224},{192,0},{224,... | collective-permute-start | bytes 368648 | tf_op jit(solution)/shard_map/quarters/ppermute | solution.py:38
  3.9 2.5 %collective-permute-start.1 = (bf16[80,768]{1,0:T(8,128)(2,1)S(1)}, bf16[80,768]{1,0:T(8,128)(2,1)S(1)}, u32[]{:S(2)}, u32[]{:S(2)}) collective-permute-start(bf16[80,768]{1,0:T(8,128)(2,1)S(1)} %get-tuple-element.49), channel_id=1, source_target_pairs={{0,128},{32,160},{64,192},{96,224},{128,0},{160,32},{192,64},{224,... | collective-permute-start | bytes 368648 | tf_op jit(solution)/shard_map/quarters/ppermute | solution.py:38
  6.3 1.2 %collective-permute-start.2 = (bf16[80,768]{1,0:T(8,128)(2,1)S(1)}, bf16[80,768]{1,0:T(8,128)(2,1)S(1)}, u32[]{:S(2)}, u32[]{:S(2)}) collective-permute-start(bf16[80,768]{1,0:T(8,128)(2,1)S(1)} %get-tuple-element.50), channel_id=1, source_target_pairs={{0,192},{32,224},{64,0},{96,32},{128,64},{160,96},{192,128},{224,1... | collective-permute-start | bytes 368648 | tf_op jit(solution)/shard_map/quarters/ppermute | solution.py:38
  7.5 1.0 constant_dynamic-slice_fusion.moment_ref
  8.5 3.2 %collective-permute-done.1.refs_2_ = bf16[80,768]{1,0:T(8,128)(2,1)S(1)} collective-permute-done((bf16[80,768]{1,0:T(8,128)(2,1)S(1)}, bf16[80,768]{1,0:T(8,128)(2,1)S(1)}, u32[]{:S(2)}, u32[]{:S(2)}) %collective-permute-start.1) | collective-permute-done | bytes 122912 | tf_op jit(solution)/shard_map/quarters/ppermute | solution.py:38
  11.7 1.1 subtract_add_fusion
  12.8 3.0 %collective-permute-start.3 = (f32[80,768]{1,0:T(8,128)S(1)}, f32[80,768]{1,0:T(8,128)S(1)}, u32[]{:S(2)}, u32[]{:S(2)}) collective-permute-start(f32[80,768]{1,0:T(8,128)S(1)} %get-tuple-element.23.one), channel_id=1, source_target_pairs={{0,32},{32,0},{64,96},{96,64},{128,160},{160,128},{192,224},{224,1... | collective-permute-start | bytes 737288 | tf_op jit(solution)/shard_map/four/ppermute | solution.py:38
  15.8 4.1 %collective-permute-done.3.two = f32[80,768]{1,0:T(8,128)S(1)} collective-permute-done((f32[80,768]{1,0:T(8,128)S(1)}, f32[80,768]{1,0:T(8,128)S(1)}, u32[]{:S(2)}, u32[]{:S(2)}) %collective-permute-start.3) | collective-permute-done | bytes 245792 | tf_op jit(solution)/shard_map/four/ppermute | solution.py:38
  20.1 1.2 %collective-permute-start.4 = (bf16[80,768]{1,0:T(8,128)(2,1)S(1)}, bf16[80,768]{1,0:T(8,128)(2,1)S(1)}, u32[]{:S(2)}, u32[]{:S(2)}) collective-permute-start(bf16[80,768]{1,0:T(8,128)(2,1)S(1)} %get-tuple-element.29), channel_id=1, source_target_pairs={{0,64},{32,96},{64,128},{96,160},{128,192},{160,224},{192,0},{224,... | collective-permute-start | bytes 368648 | tf_op jit(solution)/shard_map/home/ppermute | solution.py:38
  21.3 2.4 %collective-permute-start.5 = (bf16[80,768]{1,0:T(8,128)(2,1)S(1)}, bf16[80,768]{1,0:T(8,128)(2,1)S(1)}, u32[]{:S(2)}, u32[]{:S(2)}) collective-permute-start(bf16[80,768]{1,0:T(8,128)(2,1)S(1)} %get-tuple-element.30), channel_id=1, source_target_pairs={{0,128},{32,160},{64,192},{96,224},{128,0},{160,32},{192,64},{224,... | collective-permute-start | bytes 368648 | tf_op jit(solution)/shard_map/home/ppermute | solution.py:38
  23.8 1.3 %collective-permute-done.4.refs_1_ = bf16[80,768]{1,0:T(8,128)(2,1)S(1)} collective-permute-done((bf16[80,768]{1,0:T(8,128)(2,1)S(1)}, bf16[80,768]{1,0:T(8,128)(2,1)S(1)}, u32[]{:S(2)}, u32[]{:S(2)}) %collective-permute-start.4) | collective-permute-done | bytes 122912 | tf_op jit(solution)/shard_map/home/ppermute | solution.py:38
  25.2 2.2 %collective-permute-done.5.refs_2_ = bf16[80,768]{1,0:T(8,128)(2,1)S(1)} collective-permute-done((bf16[80,768]{1,0:T(8,128)(2,1)S(1)}, bf16[80,768]{1,0:T(8,128)(2,1)S(1)}, u32[]{:S(2)}, u32[]{:S(2)}) %collective-permute-start.5) | collective-permute-done | bytes 122912 | tf_op jit(solution)/shard_map/home/ppermute | solution.py:38
  27.7 0.7 shard_map.76.refs_4_
  28.4 4.3 %collective-permute-start.8 = (bf16[320,768]{1,0:T(8,128)(2,1)S(1)}, bf16[320,768]{1,0:T(8,128)(2,1)S(1)}, u32[]{:S(2)}, u32[]{:S(2)}) collective-permute-start(bf16[320,768]{1,0:T(8,128)(2,1)S(1)} %shard_map.76.refs_4_), channel_id=1, source_target_pairs={{0,1},{1,0},{2,3},{3,2},{4,5},{5,4},{6,7},{7,6},{8,9},{9,8},{10,11... | collective-permute-start | bytes 1474568 | tf_op jit(solution)/shard_map/b/ppermute | solution.py:49
  32.8 5.6 %collective-permute-start.7 = (bf16[320,768]{1,0:T(8,128)(2,1)S(1)}, bf16[320,768]{1,0:T(8,128)(2,1)}, u32[]{:S(2)}, u32[]{:S(2)}) collective-permute-start(bf16[320,768]{1,0:T(8,128)(2,1)S(1)} %shard_map.76.refs_4_), channel_id=1, source_target_pairs={{0,2},{1,15},{2,4},{3,1},{4,6},{5,3},{6,8},{7,5},{8,10},{9,7},{10,... | collective-permute-start | bytes 1474568 | tf_op jit(solution)/shard_map/a1/ppermute | solution.py:49
  38.4 1.6 %collective-permute-start.10 = (bf16[320,768]{1,0:T(8,128)(2,1)S(1)}, bf16[320,768]{1,0:T(8,128)(2,1)S(1)}, u32[]{:S(2)}, u32[]{:S(2)}) collective-permute-start(bf16[320,768]{1,0:T(8,128)(2,1)S(1)} %shard_map.77.refs_1_), channel_id=1, source_target_pairs={{0,2},{1,15},{2,4},{3,1},{4,6},{5,3},{6,8},{7,5},{8,10},{9,7},{10,... | collective-permute-start | bytes 1474568 | tf_op jit(solution)/shard_map/b1/ppermute | solution.py:49
  40.0 4.2 %collective-permute-done.7.refs_0_ = bf16[320,768]{1,0:T(8,128)(2,1)} collective-permute-done((bf16[320,768]{1,0:T(8,128)(2,1)S(1)}, bf16[320,768]{1,0:T(8,128)(2,1)}, u32[]{:S(2)}, u32[]{:S(2)}) %collective-permute-start.7) | collective-permute-done | bytes 491552 | tf_op jit(solution)/shard_map/a1/ppermute | solution.py:49
  44.2 3.2 %collective-permute-start.9 = (bf16[320,768]{1,0:T(8,128)(2,1)}, bf16[320,768]{1,0:T(8,128)(2,1)}, u32[]{:S(2)}, u32[]{:S(2)}) collective-permute-start(bf16[320,768]{1,0:T(8,128)(2,1)} %shard_map.78.refs_1_.refs_2_), channel_id=1, source_target_pairs={{0,2},{1,15},{2,4},{3,1},{4,6},{5,3},{6,8},{7,5},{8,10},{9,7},{10,... | collective-permute-start | bytes 1474568 | tf_op jit(solution)/shard_map/a2/ppermute | solution.py:49
  47.4 1.3 %collective-permute-start.23 = (bf16[320,768]{1,0:T(8,128)(2,1)}, bf16[320,768]{1,0:T(8,128)(2,1)}, u32[]{:S(2)}, u32[]{:S(2)}) collective-permute-start(bf16[320,768]{1,0:T(8,128)(2,1)} %shard_map.78.refs_1_.refs_2_), channel_id=1, source_target_pairs={{0,16},{1,17},{2,18},{3,19},{4,20},{5,21},{6,22},{7,23},{8,24},{9,... | collective-permute-start | bytes 1474568 | tf_op jit(solution)/shard_map/side1/ppermute | solution.py:49
  48.7 3.6 %collective-permute-done.11.refs_0_ = bf16[320,768]{1,0:T(8,128)(2,1)S(1)} collective-permute-done((bf16[320,768]{1,0:T(8,128)(2,1)S(1)}, bf16[320,768]{1,0:T(8,128)(2,1)S(1)}, u32[]{:S(2)}, u32[]{:S(2)}) %collective-permute-start.11) | collective-permute-done | bytes 491552 | tf_op jit(solution)/shard_map/part_b/ppermute | solution.py:49
  52.3 0.7 collective-permute-start.14
  53.0 0.9 collective-permute-start.13
  53.9 0.9 collective-permute-done.9.refs_0_
  54.8 3.1 %collective-permute-start.12 = (bf16[320,768]{1,0:T(8,128)(2,1)}, bf16[320,768]{1,0:T(8,128)(2,1)}, u32[]{:S(2)}, u32[]{:S(2)}) collective-permute-start(bf16[320,768]{1,0:T(8,128)(2,1)} %shard_map.81.refs_1_.refs_2_), channel_id=1, source_target_pairs={{0,2},{1,15},{2,4},{3,1},{4,6},{5,3},{6,8},{7,5},{8,10},{9,7},{10,... | collective-permute-start | bytes 1474568 | tf_op jit(solution)/shard_map/a3/ppermute | solution.py:49
  57.9 2.4 %collective-permute-done.14.refs_0_ = bf16[320,768]{1,0:T(8,128)(2,1)S(1)} collective-permute-done((bf16[320,768]{1,0:T(8,128)(2,1)S(1)}, bf16[320,768]{1,0:T(8,128)(2,1)S(1)}, u32[]{:S(2)}, u32[]{:S(2)}) %collective-permute-start.14) | collective-permute-done | bytes 491552 | tf_op jit(solution)/shard_map/part_b1/ppermute | solution.py:49
  60.4 0.9 collective-permute-start.22
  61.3 3.1 %collective-permute-start.21 = (bf16[320,768]{1,0:T(8,128)(2,1)S(1)}, bf16[320,768]{1,0:T(8,128)(2,1)S(1)}, u32[]{:S(2)}, u32[]{:S(2)}) collective-permute-start(bf16[320,768]{1,0:T(8,128)(2,1)S(1)} %shard_map.82.refs_1_.refs_7_), channel_id=1, source_target_pairs={{0,2},{1,15},{2,4},{3,1},{4,6},{5,3},{6,8},{7,5},{8,10},{9,7},{10,... | collective-permute-start | bytes 1474568 | tf_op jit(solution)/shard_map/part_b2/ppermute | solution.py:49
  64.4 3.3 %shard_map.83 = (f32[256,768]{1,0:T(8,128)S(1)}, f32[256,768]{1,0:T(8,128)S(1)}, f32[8,128]{1,0:T(8,128)S(1)}) custom-call(bf16[256,10240]{1,0:T(8,128)(2,1)S(1)} %bitcast.20, bf16[256,10240]{1,0:T(8,128)(2,1)} %collective-permute-done.15.refs_1_, bf16[320,768]{1,0:T(8,128)(2,1)} %shard_map.78.refs_1_.refs_2_, ...), custom_call_target="tpu_custom_call" | custom-call | flops 30000001024 | bytes 6488064 | tf_op jit(solution)/shard_map/pallas_call | solution.py:191
  67.7 0.7 collective-permute-start.20
  68.4 2.5 %collective-permute-done.12.refs_0_ = bf16[320,768]{1,0:T(8,128)(2,1)} collective-permute-done((bf16[320,768]{1,0:T(8,128)(2,1)}, bf16[320,768]{1,0:T(8,128)(2,1)}, u32[]{:S(2)}, u32[]{:S(2)}) %collective-permute-start.12) | collective-permute-done | bytes 491552 | tf_op jit(solution)/shard_map/a3/ppermute | solution.py:49
  70.9 1.0 collective-permute-start.28
  71.9 4.3 %collective-permute-done.21.refs_0_ = bf16[320,768]{1,0:T(8,128)(2,1)S(1)} collective-permute-done((bf16[320,768]{1,0:T(8,128)(2,1)S(1)}, bf16[320,768]{1,0:T(8,128)(2,1)S(1)}, u32[]{:S(2)}, u32[]{:S(2)}) %collective-permute-start.21) | collective-permute-done | bytes 491552 | tf_op jit(solution)/shard_map/part_b2/ppermute | solution.py:49
  76.2 2.7 %collective-permute-start.26 = (bf16[320,768]{1,0:T(8,128)(2,1)S(1)}, bf16[320,768]{1,0:T(8,128)(2,1)S(1)}, u32[]{:S(2)}, u32[]{:S(2)}) collective-permute-start(bf16[320,768]{1,0:T(8,128)(2,1)S(1)} %shard_map.88.refs_5_.refs_1_), channel_id=1, source_target_pairs={{0,2},{1,15},{2,4},{3,1},{4,6},{5,3},{6,8},{7,5},{8,10},{9,7},{10,... | collective-permute-start | bytes 1474568 | tf_op jit(solution)/shard_map/part_b3/ppermute | solution.py:49
  78.9 1.1 slice_select_fusion.2
  80.1 3.9 %shard_map.89 = (f32[256,768]{1,0:T(8,128)S(1)}, f32[256,768]{1,0:T(8,128)S(1)}, f32[8,128]{1,0:T(8,128)S(1)}) custom-call(bf16[256,10240]{1,0:T(8,128)(2,1)S(1)} %bitcast.21, bf16[256,10240]{1,0:T(8,128)(2,1)} %collective-permute-done.15.refs_1_, bf16[320,768]{1,0:T(8,128)(2,1)} %shard_map.81.refs_1_.refs_2_, ...), custom_call_target="tpu_custom_call" | custom-call | flops 30000001024 | bytes 6488064 | tf_op jit(solution)/shard_map/pallas_call | solution.py:191
  84.1 0.7 collective-permute-start.24
  85.3 4.0 %collective-permute-done.19.refs_2_ = bf16[160,768]{1,0:T(8,128)(2,1)S(1)} collective-permute-done((bf16[160,768]{1,0:T(8,128)(2,1)S(1)}, bf16[160,768]{1,0:T(8,128)(2,1)S(1)}, u32[]{:S(2)}, u32[]{:S(2)}) %collective-permute-start.19) | collective-permute-done | bytes 245792 | tf_op jit(solution)/shard_map/a4/ppermute | solution.py:49
  89.2 1.2 %collective-permute-start.17 = (f32[80,768]{1,0:T(8,128)S(1)}, f32[80,768]{1,0:T(8,128)S(1)}, u32[]{:S(2)}, u32[]{:S(2)}) collective-permute-start(f32[80,768]{1,0:T(8,128)S(1)} %shard_map.86.refs_0_), channel_id=1, source_target_pairs={{0,128},{32,160},{64,192},{96,224},{128,0},{160,32},{192,64},{224,... | collective-permute-start | bytes 737288 | tf_op jit(solution)/shard_map/gradient/ppermute | solution.py:38
  90.5 1.7 %collective-permute-start.18 = (f32[80,768]{1,0:T(8,128)S(1)}, f32[80,768]{1,0:T(8,128)S(1)}, u32[]{:S(2)}, u32[]{:S(2)}) collective-permute-start(f32[80,768]{1,0:T(8,128)S(1)} %shard_map.86.refs_0_), channel_id=1, source_target_pairs={{0,192},{32,224},{64,0},{96,32},{128,64},{160,96},{192,128},{224,1... | collective-permute-start | bytes 737288 | tf_op jit(solution)/shard_map/gradient/ppermute | solution.py:38
  92.2 1.0 collective-permute-start.25
  93.2 3.4 %collective-permute-start.27 = (bf16[160,768]{1,0:T(8,128)(2,1)S(1)}, bf16[160,768]{1,0:T(8,128)(2,1)S(1)}, u32[]{:S(2)}, u32[]{:S(2)}) collective-permute-start(bf16[160,768]{1,0:T(8,128)(2,1)S(1)} %slice_select_fusion), channel_id=1, source_target_pairs={{0,2},{1,15},{2,4},{3,1},{4,6},{5,3},{6,8},{7,5},{8,10},{9,7},{10,... | collective-permute-start | bytes 737288 | tf_op jit(solution)/shard_map/part_b4/ppermute | solution.py:49
  96.7 2.8 %shard_map.92 = (f32[256,768]{1,0:T(8,128)S(1)}, f32[256,768]{1,0:T(8,128)S(1)}, f32[8,128]{1,0:T(8,128)}) custom-call(bf16[256,10240]{1,0:T(8,128)(2,1)S(1)} %bitcast.22, bf16[256,10240]{1,0:T(8,128)(2,1)} %collective-permute-done.15.refs_1_, bf16[320,768]{1,0:T(8,128)(2,1)} %shard_map.85.refs_1_.refs_2_, bf16[320,768]{1,0:T(8,128)(2,1)S(1)} %shard_map.90.refs_1_.refs_3_, ...), custom_call_target="tpu_custom_call" | custom-call | flops 30000001024 | bytes 4849664 | tf_op jit(solution)/shard_map/pallas_call | solution.py:191
  99.8 2.8 %shard_map.93 = (f32[256,768]{1,0:T(8,128)S(1)}, bf16[256,768]{1,0:T(8,128)(2,1)S(1)}, f32[8,128]{1,0:T(8,128)}) custom-call(bf16[256,10240]{1,0:T(8,128)(2,1)S(1)} %bitcast.23, bf16[256,10240]{1,0:T(8,128)(2,1)} %collective-permute-done.15.refs_1_, bf16[160,768]{1,0:T(8,128)(2,1)S(1)} %collective-permute-done.19.refs_2_, ...), custom_call_target="tpu_custom_call" | custom-call | flops 30000001024 | bytes 4849664 | tf_op jit(solution)/shard_map/pallas_call | solution.py:191
  102.6 3.8 %collective-permute-start.29 = (bf16[256,768]{1,0:T(8,128)(2,1)S(1)}, bf16[256,768]{1,0:T(8,128)(2,1)S(1)}, u32[]{:S(2)}, u32[]{:S(2)}) collective-permute-start(bf16[256,768]{1,0:T(8,128)(2,1)S(1)} %get-tuple-element.41), channel_id=1, source_target_pairs={{0,1},{1,0},{2,3},{3,2},{4,5},{5,4},{6,7},{7,6},{8,9},{9,8},{10,11... | collective-permute-start | bytes 1179656 | tf_op jit(solution)/shard_map/late/ppermute | solution.py:49
  106.5 1.4 %shard_map.87 = f32[320,768]{1,0:T(8,128)S(1)} custom-call(f32[80,768]{1,0:T(8,128)S(1)} %shard_map.86.refs_0_, f32[80,768]{1,0:T(8,128)S(1)} %collective-permute-done.16.refs_1_, f32[80,768]{1,0:T(8,128)S(1)} %collective-permute-done.17.refs_2_, f32[80,768]{1,0:T(8,128)S(1)} %collective-permute-done.18.refs_3_), custom_call_target="tpu_custom_call" | custom-call | bytes 983040 | tf_op jit(solution)/shard_map/pallas_call | solution.py:103
  107.8 1.8 %fusion.2 = (bf16[1,320,768]{2,1,0:T(8,128)(2,1)}, f32[320,768]{1,0:T(8,128)}, f32[320,768]{1,0:T(8,128)}) fusion(bf16[1,320,768]{2,1,0:T(8,128)(2,1)S(1)} %copy-done, f32[320,768]{1,0:T(8,128)S(1)} %copy-done.1, f32[320,768]{1,0:T(8,128)S(1)} %shard_map.87, f32[320,768]{1,0:T(8,128)S(1)} %copy-done.2), kind=kLoop, calls=%fused_computation.6 | loop fusion | flops 2457600 | bytes 5898240 | tf_op jit(solution)/shard_map/broadcast_in_dim | solution.py:342
  109.6 0.8 fusion.3
  (50 shorter events, 1.9 us)
Async XLA Ops:
  1.8 6.7 %collective-permute-start = (bf16[80,768]{1,0:T(8,128)(2,1)S(1)}, bf16[80,768]{1,0:T(8,128)(2,1)S(1)}, u32[]{:S(2)}, u32[]{:S(2)}) collective-permute-start(bf16[80,768]{1,0:T(8,128)(2,1)S(1)} %get-tuple-element.48), channel_id=1, source_target_pairs={{0,64},{32,96},{64,128},{96,160},{128,192},{160,224},{192,0},{224,... | collective-permute-start | bytes 368648 | tf_op jit(solution)/shard_map/quarters/ppermute | solution.py:38
  3.9 7.8 %collective-permute-start.1 = (bf16[80,768]{1,0:T(8,128)(2,1)S(1)}, bf16[80,768]{1,0:T(8,128)(2,1)S(1)}, u32[]{:S(2)}, u32[]{:S(2)}) collective-permute-start(bf16[80,768]{1,0:T(8,128)(2,1)S(1)} %get-tuple-element.49), channel_id=1, source_target_pairs={{0,128},{32,160},{64,192},{96,224},{128,0},{160,32},{192,64},{224,... | collective-permute-start | bytes 368648 | tf_op jit(solution)/shard_map/quarters/ppermute | solution.py:38
  6.3 5.4 %collective-permute-start.2 = (bf16[80,768]{1,0:T(8,128)(2,1)S(1)}, bf16[80,768]{1,0:T(8,128)(2,1)S(1)}, u32[]{:S(2)}, u32[]{:S(2)}) collective-permute-start(bf16[80,768]{1,0:T(8,128)(2,1)S(1)} %get-tuple-element.50), channel_id=1, source_target_pairs={{0,192},{32,224},{64,0},{96,32},{128,64},{160,96},{192,128},{224,1... | collective-permute-start | bytes 368648 | tf_op jit(solution)/shard_map/quarters/ppermute | solution.py:38
  12.8 7.1 %collective-permute-start.3 = (f32[80,768]{1,0:T(8,128)S(1)}, f32[80,768]{1,0:T(8,128)S(1)}, u32[]{:S(2)}, u32[]{:S(2)}) collective-permute-start(f32[80,768]{1,0:T(8,128)S(1)} %get-tuple-element.23.one), channel_id=1, source_target_pairs={{0,32},{32,0},{64,96},{96,64},{128,160},{160,128},{192,224},{224,1... | collective-permute-start | bytes 737288 | tf_op jit(solution)/shard_map/four/ppermute | solution.py:38
  20.1 5.0 %collective-permute-start.4 = (bf16[80,768]{1,0:T(8,128)(2,1)S(1)}, bf16[80,768]{1,0:T(8,128)(2,1)S(1)}, u32[]{:S(2)}, u32[]{:S(2)}) collective-permute-start(bf16[80,768]{1,0:T(8,128)(2,1)S(1)} %get-tuple-element.29), channel_id=1, source_target_pairs={{0,64},{32,96},{64,128},{96,160},{128,192},{160,224},{192,0},{224,... | collective-permute-start | bytes 368648 | tf_op jit(solution)/shard_map/home/ppermute | solution.py:38
  21.3 6.0 %collective-permute-start.5 = (bf16[80,768]{1,0:T(8,128)(2,1)S(1)}, bf16[80,768]{1,0:T(8,128)(2,1)S(1)}, u32[]{:S(2)}, u32[]{:S(2)}) collective-permute-start(bf16[80,768]{1,0:T(8,128)(2,1)S(1)} %get-tuple-element.30), channel_id=1, source_target_pairs={{0,128},{32,160},{64,192},{96,224},{128,0},{160,32},{192,64},{224,... | collective-permute-start | bytes 368648 | tf_op jit(solution)/shard_map/home/ppermute | solution.py:38
  23.7 4.0 %collective-permute-start.6 = (bf16[80,768]{1,0:T(8,128)(2,1)S(1)}, bf16[80,768]{1,0:T(8,128)(2,1)S(1)}, u32[]{:S(2)}, u32[]{:S(2)}) collective-permute-start(bf16[80,768]{1,0:T(8,128)(2,1)S(1)} %get-tuple-element.31), channel_id=1, source_target_pairs={{0,192},{32,224},{64,0},{96,32},{128,64},{160,96},{192,128},{224,1... | collective-permute-start | bytes 368648 | tf_op jit(solution)/shard_map/home/ppermute | solution.py:38
  28.4 10.0 %collective-permute-start.8 = (bf16[320,768]{1,0:T(8,128)(2,1)S(1)}, bf16[320,768]{1,0:T(8,128)(2,1)S(1)}, u32[]{:S(2)}, u32[]{:S(2)}) collective-permute-start(bf16[320,768]{1,0:T(8,128)(2,1)S(1)} %shard_map.76.refs_4_), channel_id=1, source_target_pairs={{0,1},{1,0},{2,3},{3,2},{4,5},{5,4},{6,7},{7,6},{8,9},{9,8},{10,11... | collective-permute-start | bytes 1474568 | tf_op jit(solution)/shard_map/b/ppermute | solution.py:49
  32.7 28.6 %collective-permute-start.15 = (bf16[256,10240]{1,0:T(8,128)(2,1)}, bf16[256,10240]{1,0:T(8,128)(2,1)}, u32[]{:S(2)}, u32[]{:S(2)}) collective-permute-start(bf16[256,10240]{1,0:T(8,128)(2,1)} %bitcast.17), channel_id=1, source_target_pairs={{0,1},{1,0},{2,3},{3,2},{4,5},{5,4},{6,7},{7,6},{8,9},{9,8},{10,11... | collective-permute-start | bytes 15728648 | tf_op jit(solution)/shard_map/other/ppermute | solution.py:49
  32.8 11.4 %collective-permute-start.7 = (bf16[320,768]{1,0:T(8,128)(2,1)S(1)}, bf16[320,768]{1,0:T(8,128)(2,1)}, u32[]{:S(2)}, u32[]{:S(2)}) collective-permute-start(bf16[320,768]{1,0:T(8,128)(2,1)S(1)} %shard_map.76.refs_4_), channel_id=1, source_target_pairs={{0,2},{1,15},{2,4},{3,1},{4,6},{5,3},{6,8},{7,5},{8,10},{9,7},{10,... | collective-permute-start | bytes 1474568 | tf_op jit(solution)/shard_map/a1/ppermute | solution.py:49
  38.4 13.9 %collective-permute-start.11 = (bf16[320,768]{1,0:T(8,128)(2,1)S(1)}, bf16[320,768]{1,0:T(8,128)(2,1)S(1)}, u32[]{:S(2)}, u32[]{:S(2)}) collective-permute-start(bf16[320,768]{1,0:T(8,128)(2,1)S(1)} %shard_map.76.refs_4_), channel_id=1, source_target_pairs={{0,17},{1,16},{2,19},{3,18},{4,21},{5,20},{6,23},{7,22},{8,25},{9,... | collective-permute-start | bytes 1474568 | tf_op jit(solution)/shard_map/part_b/ppermute | solution.py:49
  38.4 14.6 %collective-permute-start.10 = (bf16[320,768]{1,0:T(8,128)(2,1)S(1)}, bf16[320,768]{1,0:T(8,128)(2,1)S(1)}, u32[]{:S(2)}, u32[]{:S(2)}) collective-permute-start(bf16[320,768]{1,0:T(8,128)(2,1)S(1)} %shard_map.77.refs_1_), channel_id=1, source_target_pairs={{0,2},{1,15},{2,4},{3,1},{4,6},{5,3},{6,8},{7,5},{8,10},{9,7},{10,... | collective-permute-start | bytes 1474568 | tf_op jit(solution)/shard_map/b1/ppermute | solution.py:49
  44.2 10.6 %collective-permute-start.9 = (bf16[320,768]{1,0:T(8,128)(2,1)}, bf16[320,768]{1,0:T(8,128)(2,1)}, u32[]{:S(2)}, u32[]{:S(2)}) collective-permute-start(bf16[320,768]{1,0:T(8,128)(2,1)} %shard_map.78.refs_1_.refs_2_), channel_id=1, source_target_pairs={{0,2},{1,15},{2,4},{3,1},{4,6},{5,3},{6,8},{7,5},{8,10},{9,7},{10,... | collective-permute-start | bytes 1474568 | tf_op jit(solution)/shard_map/a2/ppermute | solution.py:49
  47.4 32.6 %collective-permute-start.23 = (bf16[320,768]{1,0:T(8,128)(2,1)}, bf16[320,768]{1,0:T(8,128)(2,1)}, u32[]{:S(2)}, u32[]{:S(2)}) collective-permute-start(bf16[320,768]{1,0:T(8,128)(2,1)} %shard_map.78.refs_1_.refs_2_), channel_id=1, source_target_pairs={{0,16},{1,17},{2,18},{3,19},{4,20},{5,21},{6,22},{7,23},{8,24},{9,... | collective-permute-start | bytes 1474568 | tf_op jit(solution)/shard_map/side1/ppermute | solution.py:49
  52.3 8.1 %collective-permute-start.14 = (bf16[320,768]{1,0:T(8,128)(2,1)S(1)}, bf16[320,768]{1,0:T(8,128)(2,1)S(1)}, u32[]{:S(2)}, u32[]{:S(2)}) collective-permute-start(bf16[320,768]{1,0:T(8,128)(2,1)S(1)} %shard_map.79.refs_1_.refs_5_), channel_id=1, source_target_pairs={{0,2},{1,15},{2,4},{3,1},{4,6},{5,3},{6,8},{7,5},{8,10},{9,7},{10,... | collective-permute-start | bytes 1474568 | tf_op jit(solution)/shard_map/part_b1/ppermute | solution.py:49
  53.0 14.7 %collective-permute-start.13 = (bf16[320,768]{1,0:T(8,128)(2,1)S(1)}, bf16[320,768]{1,0:T(8,128)(2,1)S(1)}, u32[]{:S(2)}, u32[]{:S(2)}) collective-permute-start(bf16[320,768]{1,0:T(8,128)(2,1)S(1)} %shard_map.80.refs_1_.refs_3_), channel_id=1, source_target_pairs={{0,2},{1,15},{2,4},{3,1},{4,6},{5,3},{6,8},{7,5},{8,10},{9,7},{10,... | collective-permute-start | bytes 1474568 | tf_op jit(solution)/shard_map/b2/ppermute | solution.py:49
  54.8 9.6 %slice-start = ((s8[5242880]{0:T(1024)(128)(4,1)}), s8[4194304]{0:T(1024)(128)(4,1)S(1)}, s32[]{:S(2)}) async-start(s8[5242880]{0:T(1024)(128)(4,1)} %bitcast.18), calls=%async_computation | async-start | bytes 8388608
  54.8 9.6 %slice-start.1 = ((s8[5242880]{0:T(1024)(128)(4,1)}), s8[1048576]{0:T(1024)(128)(4,1)S(1)}, s32[]{:S(2)}) async-start(s8[5242880]{0:T(1024)(128)(4,1)} %bitcast.18), calls=%async_computation.1 | async-start | bytes 2097152
  54.8 16.1 %collective-permute-start.12 = (bf16[320,768]{1,0:T(8,128)(2,1)}, bf16[320,768]{1,0:T(8,128)(2,1)}, u32[]{:S(2)}, u32[]{:S(2)}) collective-permute-start(bf16[320,768]{1,0:T(8,128)(2,1)} %shard_map.81.refs_1_.refs_2_), channel_id=1, source_target_pairs={{0,2},{1,15},{2,4},{3,1},{4,6},{5,3},{6,8},{7,5},{8,10},{9,7},{10,... | collective-permute-start | bytes 1474568 | tf_op jit(solution)/shard_map/a3/ppermute | solution.py:49
  60.4 19.7 %collective-permute-start.22 = (bf16[320,768]{1,0:T(8,128)(2,1)}, bf16[320,768]{1,0:T(8,128)(2,1)}, u32[]{:S(2)}, u32[]{:S(2)}) collective-permute-start(bf16[320,768]{1,0:T(8,128)(2,1)} %shard_map.81.refs_1_.refs_2_), channel_id=1, source_target_pairs={{0,16},{1,17},{2,18},{3,19},{4,20},{5,21},{6,22},{7,23},{8,24},{9,... | collective-permute-start | bytes 1474568 | tf_op jit(solution)/shard_map/side2/ppermute | solution.py:49
  61.3 14.9 %collective-permute-start.21 = (bf16[320,768]{1,0:T(8,128)(2,1)S(1)}, bf16[320,768]{1,0:T(8,128)(2,1)S(1)}, u32[]{:S(2)}, u32[]{:S(2)}) collective-permute-start(bf16[320,768]{1,0:T(8,128)(2,1)S(1)} %shard_map.82.refs_1_.refs_7_), channel_id=1, source_target_pairs={{0,2},{1,15},{2,4},{3,1},{4,6},{5,3},{6,8},{7,5},{8,10},{9,7},{10,... | collective-permute-start | bytes 1474568 | tf_op jit(solution)/shard_map/part_b2/ppermute | solution.py:49
  67.7 16.3 %collective-permute-start.20 = (bf16[320,768]{1,0:T(8,128)(2,1)S(1)}, bf16[320,768]{1,0:T(8,128)(2,1)S(1)}, u32[]{:S(2)}, u32[]{:S(2)}) collective-permute-start(bf16[320,768]{1,0:T(8,128)(2,1)S(1)} %shard_map.84.refs_1_.refs_3_), channel_id=1, source_target_pairs={{0,2},{1,15},{2,4},{3,1},{4,6},{5,3},{6,8},{7,5},{8,10},{9,7},{10,... | collective-permute-start | bytes 1474568 | tf_op jit(solution)/shard_map/b3/ppermute | solution.py:49
  70.9 22.3 %collective-permute-start.28 = (bf16[320,768]{1,0:T(8,128)(2,1)}, bf16[320,768]{1,0:T(8,128)(2,1)}, u32[]{:S(2)}, u32[]{:S(2)}) collective-permute-start(bf16[320,768]{1,0:T(8,128)(2,1)} %shard_map.85.refs_1_.refs_2_), channel_id=1, source_target_pairs={{0,16},{1,17},{2,18},{3,19},{4,20},{5,21},{6,22},{7,23},{8,24},{9,... | collective-permute-start | bytes 1474568 | tf_op jit(solution)/shard_map/side3/ppermute | solution.py:49
  76.2 14.3 %collective-permute-start.26 = (bf16[320,768]{1,0:T(8,128)(2,1)S(1)}, bf16[320,768]{1,0:T(8,128)(2,1)S(1)}, u32[]{:S(2)}, u32[]{:S(2)}) collective-permute-start(bf16[320,768]{1,0:T(8,128)(2,1)S(1)} %shard_map.88.refs_5_.refs_1_), channel_id=1, source_target_pairs={{0,2},{1,15},{2,4},{3,1},{4,6},{5,3},{6,8},{7,5},{8,10},{9,7},{10,... | collective-permute-start | bytes 1474568 | tf_op jit(solution)/shard_map/part_b3/ppermute | solution.py:49
  80.0 9.2 %collective-permute-start.19 = (bf16[160,768]{1,0:T(8,128)(2,1)S(1)}, bf16[160,768]{1,0:T(8,128)(2,1)S(1)}, u32[]{:S(2)}, u32[]{:S(2)}) collective-permute-start(bf16[160,768]{1,0:T(8,128)(2,1)S(1)} %slice_select_fusion.2), channel_id=1, source_target_pairs={{0,2},{1,15},{2,4},{3,1},{4,6},{5,3},{6,8},{7,5},{8,10},{9,7},{10,... | collective-permute-start | bytes 737288 | tf_op jit(solution)/shard_map/a4/ppermute | solution.py:49
  84.1 8.1 %collective-permute-start.24 = (bf16[160,768]{1,0:T(8,128)(2,1)S(1)}, bf16[160,768]{1,0:T(8,128)(2,1)S(1)}, u32[]{:S(2)}, u32[]{:S(2)}) collective-permute-start(bf16[160,768]{1,0:T(8,128)(2,1)S(1)} %slice_select_fusion.1), channel_id=1, source_target_pairs={{0,2},{1,15},{2,4},{3,1},{4,6},{5,3},{6,8},{7,5},{8,10},{9,7},{10,... | collective-permute-start | bytes 737288 | tf_op jit(solution)/shard_map/b4/ppermute | solution.py:49
  84.7 21.7 %collective-permute-start.16 = (f32[80,768]{1,0:T(8,128)S(1)}, f32[80,768]{1,0:T(8,128)S(1)}, u32[]{:S(2)}, u32[]{:S(2)}) collective-permute-start(f32[80,768]{1,0:T(8,128)S(1)} %shard_map.86.refs_0_), channel_id=1, source_target_pairs={{0,64},{32,96},{64,128},{96,160},{128,192},{160,224},{192,0},{224,... | collective-permute-start | bytes 737288 | tf_op jit(solution)/shard_map/gradient/ppermute | solution.py:38
  89.2 17.2 %collective-permute-start.17 = (f32[80,768]{1,0:T(8,128)S(1)}, f32[80,768]{1,0:T(8,128)S(1)}, u32[]{:S(2)}, u32[]{:S(2)}) collective-permute-start(f32[80,768]{1,0:T(8,128)S(1)} %shard_map.86.refs_0_), channel_id=1, source_target_pairs={{0,128},{32,160},{64,192},{96,224},{128,0},{160,32},{192,64},{224,... | collective-permute-start | bytes 737288 | tf_op jit(solution)/shard_map/gradient/ppermute | solution.py:38
  90.5 16.0 %collective-permute-start.18 = (f32[80,768]{1,0:T(8,128)S(1)}, f32[80,768]{1,0:T(8,128)S(1)}, u32[]{:S(2)}, u32[]{:S(2)}) collective-permute-start(f32[80,768]{1,0:T(8,128)S(1)} %shard_map.86.refs_0_), channel_id=1, source_target_pairs={{0,192},{32,224},{64,0},{96,32},{128,64},{160,96},{192,128},{224,1... | collective-permute-start | bytes 737288 | tf_op jit(solution)/shard_map/gradient/ppermute | solution.py:38
  92.2 7.3 %collective-permute-start.25 = (bf16[160,768]{1,0:T(8,128)(2,1)S(1)}, bf16[160,768]{1,0:T(8,128)(2,1)S(1)}, u32[]{:S(2)}, u32[]{:S(2)}) collective-permute-start(bf16[160,768]{1,0:T(8,128)(2,1)S(1)} %collective-permute-done.19.refs_2_), channel_id=1, source_target_pairs={{0,16},{1,17},{2,18},{3,19},{4,20},{5,21},{6,22},{7,23},{8,24},{9,... | collective-permute-start | bytes 737288 | tf_op jit(solution)/shard_map/far_side/ppermute | solution.py:49
  93.2 6.6 %collective-permute-start.27 = (bf16[160,768]{1,0:T(8,128)(2,1)S(1)}, bf16[160,768]{1,0:T(8,128)(2,1)S(1)}, u32[]{:S(2)}, u32[]{:S(2)}) collective-permute-start(bf16[160,768]{1,0:T(8,128)(2,1)S(1)} %slice_select_fusion), channel_id=1, source_target_pairs={{0,2},{1,15},{2,4},{3,1},{4,6},{5,3},{6,8},{7,5},{8,10},{9,7},{10,... | collective-permute-start | bytes 737288 | tf_op jit(solution)/shard_map/part_b4/ppermute | solution.py:49
  99.8 8.0 %copy-start = (bf16[1,320,768]{2,1,0:T(8,128)(2,1)S(1)}, bf16[1,320,768]{2,1,0:T(8,128)(2,1)}, u32[]{:S(2)}) copy-start(bf16[1,320,768]{2,1,0:T(8,128)(2,1)} %param.6) | copy-start | bytes 1474564
  99.8 8.0 %copy-start.1 = (f32[320,768]{1,0:T(8,128)S(1)}, f32[320,768]{1,0:T(8,128)}, u32[]{:S(2)}) copy-start(f32[320,768]{1,0:T(8,128)} %param.4) | copy-start | bytes 2949124
  99.8 8.0 %copy-start.2 = (f32[320,768]{1,0:T(8,128)S(1)}, f32[320,768]{1,0:T(8,128)}, u32[]{:S(2)}) copy-start(f32[320,768]{1,0:T(8,128)} %param.5) | copy-start | bytes 2949124
  102.6 7.0 %collective-permute-start.29 = (bf16[256,768]{1,0:T(8,128)(2,1)S(1)}, bf16[256,768]{1,0:T(8,128)(2,1)S(1)}, u32[]{:S(2)}, u32[]{:S(2)}) collective-permute-start(bf16[256,768]{1,0:T(8,128)(2,1)S(1)} %get-tuple-element.41), channel_id=1, source_target_pairs={{0,1},{1,0},{2,3},{3,2},{4,5},{5,4},{6,7},{7,6},{8,9},{9,8},{10,11... | collective-permute-start | bytes 1179656 | tf_op jit(solution)/shard_map/late/ppermute | solution.py:49
